TPU v7x, 32 devices: a whole 2x2x4 slice. The times are simulated.
32 devices in a mesh: space: 8 (over y, x, core), chan: 4 (over z).
Axes of the slice: x: 2, y: 2, z: 4, core: 2. Of those that a mesh axis runs over, the one named last changes fastest.
Arguments:
- volume: bfloat16 [32, 16, 8, 128], P(None, 'space', 'chan'), may hold values from -6 to 6
- weight_first: bfloat16 [3, 3, 3, 64, 32], replicated, may hold values from -0.21875 to 0.21875
- weight_deep: bfloat16 [3, 3, 3, 512, 64], P(None, None, None, 'chan'), may hold values from -0.15625 to 0.15625
- cotangent: bfloat16 [512, 8, 256], P('chan', 'space'), may hold values from -6 to 6
Outputs:
- deep_out: bfloat16 [512, 8, 256], P('chan', 'space')
- grad_deep: float32 [3, 3, 3, 512, 64], P(None, None, None, 'chan')
All inputs are finite; a program needn't handle non-finite values.
Results may differ from a plain program's by a relative error of at most 0.0051.
Values may be sent and summed in bfloat16 or wider, within the bound.
No kernel may reach another device: no remote copies, remote signals or barrier semaphores. Data moves between devices by JAX's collectives and lax.ppermute only.
A program may use at most 64 MiB of HBM per device.

v0:
```python
import jax
import jax.numpy as jnp
from jax import lax
from jax.sharding import PartitionSpec as P


def padded_2(array, sides, width):
    for axis, dim in sides:
        peers, length = (lax.axis_size(axis), array.shape[dim])
        up = [(i, (i + 1) % peers) for i in range(peers - 1)]
        down = [(j, i) for i, j in up]
        last = lax.slice_in_dim(array, length - width, length, axis=dim)
        leading = lax.slice_in_dim(array, 0, width, axis=dim)
        before = lax.ppermute(last, axis, up)
        after = lax.ppermute(leading, axis, down)
        array = jnp.concatenate([before, array, after], axis=dim)
    return array


def convolve(padded, weight, planes, rows, depth):
    total = jnp.zeros((weight.shape[3], planes, rows, depth), jnp.float32)
    for offset_x in range(3):
        for offset_y in range(3):
            for offset_z in range(3):
                window = padded[
                    :,
                    offset_x : offset_x + planes,
                    offset_y : offset_y + rows,
                    offset_z : offset_z + depth,
                ]
                total = total + jnp.einsum(
                    "oc,cxyz->oxyz",
                    weight[offset_x, offset_y, offset_z],
                    window,
                    preferred_element_type=jnp.float32,
                )
    return total


def weight_terms(grad_pre, padded, planes, rows, depth):
    outer = []
    for offset_x in range(3):
        middle = []
        for offset_y in range(3):
            inner = []
            for offset_z in range(3):
                window = padded[
                    :,
                    offset_x : offset_x + planes,
                    offset_y : offset_y + rows,
                    offset_z : offset_z + depth,
                ]
                inner.append(
                    jnp.einsum(
                        "oxyz,cxyz->oc", grad_pre, window, preferred_element_type=jnp.float32
                    )
                )
            middle.append(jnp.stack(inner))
        outer.append(jnp.stack(middle))
    return jnp.stack(outer)


def pool_mean(act):
    chans, planes, rows, depth = act.shape
    blocks = act.reshape(chans, planes // 2, 2, rows // 2, 2, depth // 2, 2)
    return jnp.mean(blocks, axis=(2, 4, 6))


def on_device(volume, weight_first, weight_deep, cotangent):
    planes = volume.shape[1]
    rows = volume.shape[2]
    depth = volume.shape[3]
    rimmed = padded_2(volume, (("space", 1), ("chan", 2)), 1)
    padded = jnp.pad(rimmed, ((0, 0), (0, 0), (0, 0), (1, 1)))
    pre_first = convolve(padded, weight_first, planes, rows, depth)
    pooled = pool_mean(jax.nn.silu(pre_first)).astype(jnp.bfloat16)
    whole = lax.all_gather(pooled, "chan", axis=2, tiled=True)
    framed = padded_2(whole, (("space", 1),), 1)
    deep_in = jnp.pad(framed, ((0, 0), (0, 0), (1, 1), (1, 1)))
    deep_planes = pooled.shape[1]
    deep_rows = framed.shape[2]
    deep_depth = framed.shape[3]
    pre_deep = convolve(deep_in, weight_deep, deep_planes, deep_rows, deep_depth)
    out_chans = pre_deep.shape[0]
    deep_out = (
        jax.nn.silu(pre_deep)
        .astype(jnp.bfloat16)
        .reshape(out_chans, deep_planes, deep_rows * deep_depth)
    )
    sigma = jax.nn.sigmoid(pre_deep)
    cot_grid = cotangent.reshape(out_chans, deep_planes, deep_rows, deep_depth).astype(jnp.float32)
    grad_pre = (cot_grid * sigma * (1.0 + pre_deep * (1.0 - sigma))).astype(jnp.bfloat16)
    local_grad = weight_terms(grad_pre, deep_in, deep_planes, deep_rows, deep_depth)
    grad_deep = lax.psum(local_grad, "space")
    return (deep_out, grad_deep)


def solution(mesh):
    return jax.shard_map(
        on_device,
        mesh=mesh,
        in_specs=(
            P(None, "space", "chan", None),
            P(),
            P(None, None, None, "chan", None),
            P("chan", "space", None),
        ),
        out_specs=(P("chan", "space", None), P(None, None, None, "chan", None)),
        check_vma=False,
    )
```

profile of v0, /device:TPU:0, one launch (start us, length us, event | category | flops | bytes accessed | tf_op | source)
XLA Modules:
  0.0 130.1 jit_solution(15757951367255437157)
XLA Ops:
  7.2 0.8 copy.76
  8.0 2.5 %collective-permute-start = (bf16[32,1,2,128]{3,0,2,1:T(8,128)(2,1)S(1)}, bf16[32,1,2,128]{3,0,2,1:T(8,128)(2,1)S(1)}, u32[]{:S(2)}, u32[]{:S(2)}) collective-permute-start(bf16[32,1,2,128]{3,0,2,1:T(8,128)(2,1)S(1)} %get-tuple-element.13), channel_id=1, source_target_pairs={{0,4},{4,8},{8,12},{12,16},{16,20},{20,24},{24,28},{1,5},{5,9},{9,... | collective-permute-start | bytes 49160 | tf_op jit(solution)/shard_map/ppermute | solution.py:14
  10.5 1.3 collective-permute-start.1
  11.8 0.9 fusion.149
  12.7 3.0 %collective-permute-done.1 = bf16[32,1,2,128]{3,0,2,1:T(8,128)(2,1)S(1)} collective-permute-done((bf16[32,1,2,128]{3,0,2,1:T(8,128)(2,1)S(1)}, bf16[32,1,2,128]{3,0,2,1:T(8,128)(2,1)S(1)}, u32[]{:S(2)}, u32[]{:S(2)}) %collective-permute-start.1) | collective-permute-done | bytes 16416 | tf_op jit(solution)/shard_map/ppermute | solution.py:15
  15.7 3.5 %collective-permute-start.2 = (bf16[32,4,1,128]{3,0,2,1:T(8,128)(2,1)S(1)}, bf16[32,4,1,128]{3,0,2,1:T(8,128)(2,1)S(1)}, u32[]{:S(2)}, u32[]{:S(2)}) collective-permute-start(bf16[32,4,1,128]{3,0,2,1:T(8,128)(2,1)S(1)} %get-tuple-element.10), channel_id=1, source_target_pairs={{0,1},{1,2},{2,3},{4,5},{5,6},{6,7},{8,9},{9,10},{10,11},{12,13},{... | collective-permute-start | bytes 98312 | tf_op jit(solution)/shard_map/ppermute | solution.py:14
  19.2 1.3 collective-permute-start.3
  20.8 4.2 %collective-permute-done.3 = bf16[32,4,1,128]{3,0,2,1:T(8,128)(2,1)S(1)} collective-permute-done((bf16[32,4,1,128]{3,0,2,1:T(8,128)(2,1)S(1)}, bf16[32,4,1,128]{3,0,2,1:T(8,128)(2,1)S(1)}, u32[]{:S(2)}, u32[]{:S(2)}) %collective-permute-start.3) | collective-permute-done | bytes 32800 | tf_op jit(solution)/shard_map/ppermute | solution.py:15
  25.4 0.2 fusion.76
  25.6 0.2 fusion.70
  25.8 0.2 fusion.72
  26.2 0.2 fusion.68
  26.5 0.2 convolution_bitcast_fusion.14
  26.9 0.2 convolution_bitcast_fusion.16
  27.4 0.2 convolution_bitcast_fusion.18
  27.8 0.2 convolution_bitcast_fusion.20
  28.5 0.2 convolution_add_fusion.20
  28.7 0.2 convolution_add_fusion.19
  28.9 0.2 convolution_add_fusion.18
  29.7 0.2 fusion.30
  30.0 0.2 fusion.28
  30.2 0.2 fusion.26
  30.4 0.3 multiply_reduce_fusion
  31.0 13.6 %all-gather = bf16[64,256]{0,1:T(8,128)(2,1)S(1)} all-gather(bf16[64,64]{0,1:T(8,128)(2,1)S(1)} %multiply_convert_fusion.2), channel_id=2, replica_groups=mesh['space'=8,'chan'=4] {'chan'}, dimensions={1}, use_global_device_ids=true | all-gather | bytes 40960 | tf_op jit(solution)/shard_map/all_gather | solution.py:77
  44.5 1.3 collective-permute-start.4
  45.8 1.3 collective-permute-start.5
  47.2 4.3 %collective-permute-done.5 = bf16[64,1,4,64]{0,3,2,1:T(8,128)(2,1)S(1)} collective-permute-done((bf16[64,1,4,64]{0,3,2,1:T(8,128)(2,1)S(1)}, bf16[64,1,4,64]{0,3,2,1:T(8,128)(2,1)S(1)}, u32[]{:S(2)}, u32[]{:S(2)}) %collective-permute-start.5) | collective-permute-done | bytes 32800 | tf_op jit(solution)/shard_map/ppermute | solution.py:15
  55.4 0.2 multiply_convert_fusion
  61.4 1.0 pad_maximum_fusion
  62.4 0.7 copy.111
  63.1 57.9 %all-reduce.4.cloned.1.call-done = f32[3,3,3,128,64]{3,4,2,1,0:T(8,128)} async-done(((f32[3,3,3,128,64]{3,4,2,1,0:T(8,128)}), f32[3,3,3,128,64]{3,4,2,1,0:T(8,128)}) %all-reduce.4.cloned.1.call-update) | async-done | bytes 884752 | tf_op jit(solution)/shard_map/psum | solution.py:94
  121.0 2.2 %copy.172 = f32[3,3,3,128,64]{3,4,2,1,0:T(8,128)} copy(f32[3,3,3,128,64]{3,4,2,1,0:T(8,128)} %all-reduce.4.cloned.1.call-done) | data formatting | bytes 1769472
  (97 shorter events, 12.0 us)
Async XLA Ops:
  7.2 113.9 %all-reduce.4.cloned.1.call-start = ((), (), s32[]{:S(2)}) async-start(), calls=%async_computation | async-start | bytes 1769472 | tf_op jit(solution)/shard_map/psum | solution.py:94
  8.0 3.8 %copy-start.1 = (bf16[32,2,2,128]{3,2,1,0:T(2,128)(2,1)S(1)}, bf16[32,2,2,128]{3,2,1,0:T(2,128)(2,1)}, u32[]{:S(2)}) copy-start(bf16[32,2,2,128]{3,2,1,0:T(2,128)(2,1)} %param.4) | copy-start | bytes 98308
  8.0 12.5 %copy-start.2 = (bf16[3,3,3,64,32]{3,4,2,1,0:T(8,128)(2,1)S(1)}, bf16[3,3,3,64,32]{3,4,2,1,0:T(8,128)(2,1)}, u32[]{:S(2)}) copy-start(bf16[3,3,3,64,32]{3,4,2,1,0:T(8,128)(2,1)} %param.5) | copy-start | bytes 331780
  8.0 4.7 %collective-permute-start = (bf16[32,1,2,128]{3,0,2,1:T(8,128)(2,1)S(1)}, bf16[32,1,2,128]{3,0,2,1:T(8,128)(2,1)S(1)}, u32[]{:S(2)}, u32[]{:S(2)}) collective-permute-start(bf16[32,1,2,128]{3,0,2,1:T(8,128)(2,1)S(1)} %get-tuple-element.13), channel_id=1, source_target_pairs={{0,4},{4,8},{8,12},{12,16},{16,20},{20,24},{24,28},{1,5},{5,9},{9,... | collective-permute-start | bytes 49160 | tf_op jit(solution)/shard_map/ppermute | solution.py:14
  10.5 5.2 %collective-permute-start.1 = (bf16[32,1,2,128]{3,0,2,1:T(8,128)(2,1)S(1)}, bf16[32,1,2,128]{3,0,2,1:T(8,128)(2,1)S(1)}, u32[]{:S(2)}, u32[]{:S(2)}) collective-permute-start(bf16[32,1,2,128]{3,0,2,1:T(8,128)(2,1)S(1)} %get-tuple-element.12), channel_id=1, source_target_pairs={{4,0},{8,4},{12,8},{16,12},{20,16},{24,20},{28,24},{5,1},{9,5},{13... | collective-permute-start | bytes 49160 | tf_op jit(solution)/shard_map/ppermute | solution.py:15
  15.7 5.1 %collective-permute-start.2 = (bf16[32,4,1,128]{3,0,2,1:T(8,128)(2,1)S(1)}, bf16[32,4,1,128]{3,0,2,1:T(8,128)(2,1)S(1)}, u32[]{:S(2)}, u32[]{:S(2)}) collective-permute-start(bf16[32,4,1,128]{3,0,2,1:T(8,128)(2,1)S(1)} %get-tuple-element.10), channel_id=1, source_target_pairs={{0,1},{1,2},{2,3},{4,5},{5,6},{6,7},{8,9},{9,10},{10,11},{12,13},{... | collective-permute-start | bytes 98312 | tf_op jit(solution)/shard_map/ppermute | solution.py:14
  19.2 5.8 %collective-permute-start.3 = (bf16[32,4,1,128]{3,0,2,1:T(8,128)(2,1)S(1)}, bf16[32,4,1,128]{3,0,2,1:T(8,128)(2,1)S(1)}, u32[]{:S(2)}, u32[]{:S(2)}) collective-permute-start(bf16[32,4,1,128]{3,0,2,1:T(8,128)(2,1)S(1)} %get-tuple-element.11), channel_id=1, source_target_pairs={{1,0},{2,1},{3,2},{5,4},{6,5},{7,6},{9,8},{10,9},{11,10},{13,12},{... | collective-permute-start | bytes 98312 | tf_op jit(solution)/shard_map/ppermute | solution.py:15
  30.8 16.3 %copy-start.3 = (bf16[128,1,256]{2,0,1:T(8,128)(2,1)S(1)}, bf16[128,1,256]{2,0,1:T(8,128)(2,1)}, u32[]{:S(2)}) copy-start(bf16[128,1,256]{2,0,1:T(8,128)(2,1)} %param.7) | copy-start | bytes 196612
  30.9 20.7 %copy-start = (bf16[3,3,3,128,64]{3,4,2,1,0:T(8,128)(2,1)S(1)}, bf16[3,3,3,128,64]{3,4,2,1,0:T(8,128)(2,1)}, u32[]{:S(2)}) copy-start(bf16[3,3,3,128,64]{3,4,2,1,0:T(8,128)(2,1)} %param.6) | copy-start | bytes 1327108
  44.5 2.7 %collective-permute-start.4 = (bf16[64,1,4,64]{0,3,2,1:T(8,128)(2,1)S(1)}, bf16[64,1,4,64]{0,3,2,1:T(8,128)(2,1)S(1)}, u32[]{:S(2)}, u32[]{:S(2)}) collective-permute-start(bf16[64,1,4,64]{0,3,2,1:T(8,128)(2,1)S(1)} %bitcast.673), channel_id=1, source_target_pairs={{0,4},{4,8},{8,12},{12,16},{16,20},{20,24},{24,28},{1,5},{5,9},{9,... | collective-permute-start | bytes 98312 | tf_op jit(solution)/shard_map/ppermute | solution.py:14
  45.8 5.8 %collective-permute-start.5 = (bf16[64,1,4,64]{0,3,2,1:T(8,128)(2,1)S(1)}, bf16[64,1,4,64]{0,3,2,1:T(8,128)(2,1)S(1)}, u32[]{:S(2)}, u32[]{:S(2)}) collective-permute-start(bf16[64,1,4,64]{0,3,2,1:T(8,128)(2,1)S(1)} %bitcast.674), channel_id=1, source_target_pairs={{4,0},{8,4},{12,8},{16,12},{20,16},{24,20},{28,24},{5,1},{9,5},{13... | collective-permute-start | bytes 98312 | tf_op jit(solution)/shard_map/ppermute | solution.py:15
Sparse Core Ops, SparseCore 0:
  62.5 58.4 all-reduce.3
where the time goes:
time: 130 us
  waiting for transfers between devices  69.5 us (53%)
  matrix products  15.8 us (12%)
  between operations  14.7 us (11%)
  blocking collectives  13.6 us (10%)
  starting transfers between devices  11.2 us (9%)
  local copies, waits for them, and re-layouts  3.93 us (3%)
  other arithmetic  1.49 us (1%)
    psum x1, waiting for transfers between devices, on_device(): grad_deep = lax.psum(local_grad, 'space')  57.9 us
    all_gather x1, blocking collectives, on_device(): whole = lax.all_gather(pooled, 'chan', axis=2, tiled=True)  13.6 us
    ppermute x3, waiting for transfers between devices, padded_2(): after = lax.ppermute(leading, axis, down)  11.5 us
    dot_general x54, matrix products, convolve(): jnp.einsum('oc,cxyz->oxyz', weight[offset_x, offset_y, offset_z], window,...  10.5 us
    ppermute x3, starting transfers between devices, padded_2(): before = lax.ppermute(last, axis, up)  7.25 us
    dot_general x27, matrix products, weight_terms(): jnp.einsum('oxyz,cxyz->oc', grad_pre, window, preferred_element_type=jnp....  5.3 us
    ppermute x3, starting transfers between devices, padded_2(): after = lax.ppermute(leading, axis, down)  3.88 us
    unnamed x13, local copies, waits for them, and re-layouts  3.72 us
  transfers between devices with their start and end apart: 7, of which 5 were waited for; matrix products, arithmetic and copies ran while one was open for 1% of the time, Pallas kernels for 0%

commit v1 on v0

v1 whole, which is shorter than its diff:
```python
import functools

import jax
import jax.numpy as jnp
from jax import lax
from jax.experimental import pallas as pl
from jax.experimental.pallas import tpu as pltpu
from jax.sharding import PartitionSpec as P


def padded_2(array, sides, width):
    for axis, dim in sides:
        peers, length = (lax.axis_size(axis), array.shape[dim])
        up = [(i, (i + 1) % peers) for i in range(peers - 1)]
        down = [(j, i) for i, j in up]
        last = lax.slice_in_dim(array, length - width, length, axis=dim)
        leading = lax.slice_in_dim(array, 0, width, axis=dim)
        before = lax.ppermute(last, axis, up)
        after = lax.ppermute(leading, axis, down)
        array = jnp.concatenate([before, array, after], axis=dim)
    return array


def windows(padded, planes, rows, depth):
    for offset_x in range(3):
        for offset_y in range(3):
            for offset_z in range(3):
                yield (offset_x, offset_y, offset_z), padded[
                    :,
                    offset_x : offset_x + planes,
                    offset_y : offset_y + rows,
                    offset_z : offset_z + depth,
                ]


def convolve(padded, weight, planes, rows, depth):
    total = jnp.zeros((weight.shape[3], planes, rows, depth), jnp.float32)
    for tap, window in windows(padded, planes, rows, depth):
        total = total + jnp.einsum(
            "oc,cxyz->oxyz", weight[tap], window, preferred_element_type=jnp.float32
        )
    return total


def weight_terms(grad_pre, padded, planes, rows, depth):
    terms = [
        jnp.einsum("oxyz,cxyz->oc", grad_pre, window, preferred_element_type=jnp.float32)
        for _, window in windows(padded, planes, rows, depth)
    ]
    return jnp.stack(terms).reshape((3, 3, 3) + terms[0].shape)


def pool_mean(act):
    chans, planes, rows, depth = act.shape
    blocks = act.reshape(chans, planes // 2, 2, rows // 2, 2, depth // 2, 2)
    return jnp.mean(blocks, axis=(2, 4, 6))


def by_halos(volume, weight_first, weight_deep, cotangent):
    planes, rows, depth = volume.shape[1:]
    rimmed = padded_2(volume, (("space", 1), ("chan", 2)), 1)
    padded = jnp.pad(rimmed, ((0, 0), (0, 0), (0, 0), (1, 1)))
    pre_first = convolve(padded, weight_first, planes, rows, depth)
    pooled = pool_mean(jax.nn.silu(pre_first)).astype(jnp.bfloat16)
    whole = lax.all_gather(pooled, "chan", axis=2, tiled=True)
    framed = padded_2(whole, (("space", 1),), 1)
    deep_in = jnp.pad(framed, ((0, 0), (0, 0), (1, 1), (1, 1)))
    deep_planes = pooled.shape[1]
    deep_rows, deep_depth = framed.shape[2:]
    pre_deep = convolve(deep_in, weight_deep, deep_planes, deep_rows, deep_depth)
    deep_out = jax.nn.silu(pre_deep).astype(jnp.bfloat16).reshape(cotangent.shape)
    sigma = jax.nn.sigmoid(pre_deep)
    cot_grid = cotangent.reshape(pre_deep.shape).astype(jnp.float32)
    grad_pre = (cot_grid * sigma * (1.0 + pre_deep * (1.0 - sigma))).astype(jnp.bfloat16)
    local_grad = weight_terms(grad_pre, deep_in, deep_planes, deep_rows, deep_depth)
    return deep_out, lax.psum(local_grad, "space")


DN = (((1,), (0,)), ((), ()))
NT = (((1,), (1,)), ((), ()))


def first_kernel(chans, place_ref, w_ref, *refs):
    pieces, (out_ref, grid, moved, patches) = refs[:chans], refs[chans:]
    planes, rows, cin, depth = grid.shape
    cmid = w_ref.shape[0]
    mine = place_ref[0]
    edge = jnp.zeros((cin, depth), jnp.bfloat16)
    for plane in range(planes):
        grid[plane, 0] = edge
        grid[plane, rows - 1] = edge
    for k in range(chans):
        per = pieces[k].shape[1]
        start = 1 + (mine ^ k) * per
        for plane in range(planes):
            for row in range(per):
                grid[plane, start + row] = pieces[k][plane, row]
    lane = lax.broadcasted_iota(jnp.int32, (rows * cin, depth), 1)
    for plane in range(planes):
        flat = grid[plane].reshape(rows * cin, depth).astype(jnp.float32)
        left = jnp.where(lane == 0, 0.0, pltpu.roll(flat, 1, 1))
        right = jnp.where(lane == depth - 1, 0.0, pltpu.roll(flat, depth - 1, 1))
        moved[0, plane] = left.astype(jnp.bfloat16).reshape(rows, cin, depth)
        moved[1, plane] = right.astype(jnp.bfloat16).reshape(rows, cin, depth)
    pair_rows = (rows - 2) // 2
    sums = []
    for pair in range(pair_rows):
        for a in range(3):
            for b in range(3):
                for c in range(3):
                    at = ((a * 3 + b) * 3 + c) * cin
                    for px in range(2):
                        for py in range(2):
                            x, y = px + a, 2 * pair + py + b
                            col = ((pair * 2 + px) * 2 + py) * depth
                            block = grid[x, y] if c == 1 else moved[c // 2, x, y]
                            patches[at : at + cin, col : col + depth] = block
        cols = patches[:, pair * 4 * depth : (pair + 1) * 4 * depth]
        pre = lax.dot_general(w_ref[...], cols, DN, preferred_element_type=jnp.float32)
        act = pre / (1.0 + jnp.exp(-pre))
        total = act[:, :depth]
        for part in range(1, 4):
            total = total + act[:, part * depth : (part + 1) * depth]
        sums.append(total * 0.125)
    fold_in = lax.broadcasted_iota(jnp.int32, (2 * depth, depth), 0)
    fold_out = lax.broadcasted_iota(jnp.int32, (2 * depth, depth), 1)
    fold = (fold_in // 2 == fold_out).astype(jnp.float32)
    for pair in range(0, pair_rows, 2):
        both = jnp.concatenate([sums[pair], sums[pair + 1]], axis=1)
        halved = lax.dot_general(
            both, fold, DN, precision=lax.Precision.HIGHEST, preferred_element_type=jnp.float32
        )
        out_ref[:, pair // 2 * depth : (pair // 2 + 1) * depth] = halved.astype(jnp.bfloat16)


def deep_kernel(groups, rowlen, place_ref, w_ref, *refs):
    same, refs = refs[:groups], refs[groups:]
    other, refs = refs[:groups], refs[groups:]
    cots, refs = refs[:groups], refs[groups:]
    out_ref, grad_ref, held, cot, pre, tap_same, tap_other = refs
    cmid, cells = same[0].shape
    mine = place_ref[0] // 2
    odd = place_ref[0] % 2
    held[groups] = jnp.zeros((cmid, cells), jnp.bfloat16)
    held[2 * groups] = jnp.zeros((cmid, cells), jnp.bfloat16)
    for k in range(groups):
        held[mine ^ k] = same[k][...]
        held[groups + (mine ^ k) + 1 - odd] = other[k][...]
        cot[mine ^ k] = cots[k][...]
    lane = lax.broadcasted_iota(jnp.int32, (cmid, cells), 1)
    z = lane % rowlen
    for slot in range(2 * groups + 1):
        plane = held[slot].astype(jnp.float32)
        target, at = (tap_same, slot) if slot < groups else (tap_other, slot - groups)
        for b in range(3):
            for c in range(3):
                shift = (b - 1) * rowlen + (c - 1)
                value = plane
                if shift:
                    value = pltpu.roll(plane, (-shift) % cells, 1)
                    ok = None
                    if b == 0:
                        ok = lane >= rowlen
                    if b == 2:
                        ok = lane < cells - rowlen
                    if c != 1:
                        inside = z > 0 if c == 0 else z < rowlen - 1
                        ok = inside if ok is None else ok & inside
                    value = jnp.where(ok, value, 0.0)
                row = (b * 3 + c) * cmid
                target[row : row + cmid, at * cells : (at + 1) * cells] = value.astype(jnp.bfloat16)
    width = groups * cells
    views = (
        tap_other.at[:, :width],
        tap_same.at[:, :],
        tap_other.at[:, cells : cells + width],
    )
    depth = tap_same.shape[0]
    total = None
    for a in range(3):
        term = lax.dot_general(
            w_ref[:, a * depth : (a + 1) * depth], views[a][...], DN, preferred_element_type=jnp.float32
        )
        total = term if total is None else total + term
    grads = []
    for k in range(groups):
        value = total[:, k * cells : (k + 1) * cells]
        sigma = 1.0 / (1.0 + jnp.exp(-value))
        pre[k] = (value * sigma).astype(jnp.bfloat16)
        grads.append(
            (cot[k].astype(jnp.float32) * sigma * (1.0 + value * (1.0 - sigma))).astype(jnp.bfloat16)
        )
    out_ref[...] = pre[mine]
    grad_pre = jnp.concatenate(grads, axis=1)
    for a in range(3):
        grad_ref[a * depth : (a + 1) * depth] = lax.dot_general(
            views[a][...], grad_pre, NT, preferred_element_type=jnp.float32
        )


def swap(array, axis, bits):
    peers = lax.axis_size(axis)
    return lax.ppermute(array, axis, [(i, i ^ bits) for i in range(peers)])


def by_gather(volume, weight_first, weight_deep, cotangent):
    cin, planes, rows, depth = volume.shape
    spaces, chans = lax.axis_size("space"), lax.axis_size("chan")
    groups = spaces // 2
    cmid = weight_first.shape[3]
    cout = weight_deep.shape[3]
    cells = cotangent.shape[2]
    at_space, at_chan = lax.axis_index("space"), lax.axis_index("chan")
    odd = at_space % 2 == 1

    block = jnp.transpose(volume, (1, 2, 0, 3))
    first, last = block[0], block[planes - 1]
    near = swap(jnp.where(odd, first, last), "space", 1)
    pairs = [(i, i + 1) for i in range(1, spaces - 1, 2)]
    far = lax.ppermute(jnp.where(odd, last, first), "space", pairs + [(j, i) for i, j in pairs])
    before, after = jnp.where(odd, near, far), jnp.where(odd, far, near)
    slab = jnp.concatenate([before[None], block, after[None]], axis=0)
    slabs = [slab] + [swap(slab, "chan", k) for k in range(1, chans)]

    cots = cotangent[:, 0]
    all_cots = [cots] + [swap(cots, "space", 2 * k) for k in range(1, groups)]

    taps_first = jnp.transpose(weight_first, (3, 0, 1, 2, 4)).reshape(cmid, 27 * cin)
    taps_deep = jnp.transpose(weight_deep, (3, 0, 1, 2, 4)).reshape(cout, 27 * cmid)

    all_rows = chans * rows
    vmem = pl.BlockSpec(memory_space=pltpu.VMEM)
    smem = pl.BlockSpec(memory_space=pltpu.SMEM)
    pooled = pl.pallas_call(
        functools.partial(first_kernel, chans),
        out_shape=jax.ShapeDtypeStruct((cmid, all_rows * depth // 4), jnp.bfloat16),
        in_specs=[smem, vmem] + [vmem] * chans,
        out_specs=vmem,
        scratch_shapes=[
            pltpu.VMEM((planes + 2, all_rows + 2, cin, depth), jnp.bfloat16),
            pltpu.VMEM((2, planes + 2, all_rows + 2, cin, depth), jnp.bfloat16),
            pltpu.VMEM((27 * cin, planes * all_rows * depth), jnp.bfloat16),
        ],
        compiler_params=pltpu.CompilerParams(vmem_limit_bytes=32 * 2**20),
        name="first",
    )(at_chan.reshape(1), taps_first, *slabs)

    same = [pooled] + [swap(pooled, "space", 2 * k) for k in range(1, groups)]
    other = [swap(p, "space", 1) for p in same]

    deep_out, terms = pl.pallas_call(
        functools.partial(deep_kernel, groups, depth // 2),
        out_shape=(
            jax.ShapeDtypeStruct((cout, cells), jnp.bfloat16),
            jax.ShapeDtypeStruct((27 * cmid, cout), jnp.float32),
        ),
        in_specs=[smem, vmem] + [vmem] * (3 * groups),
        out_specs=(vmem, vmem),
        scratch_shapes=[
            pltpu.VMEM((2 * groups + 1, cmid, cells), jnp.bfloat16),
            pltpu.VMEM((groups, cout, cells), jnp.bfloat16),
            pltpu.VMEM((groups, cout, cells), jnp.bfloat16),
            pltpu.VMEM((9 * cmid, groups * cells), jnp.bfloat16),
            pltpu.VMEM((9 * cmid, (groups + 1) * cells), jnp.bfloat16),
        ],
        compiler_params=pltpu.CompilerParams(vmem_limit_bytes=32 * 2**20),
        name="deep",
    )(at_space.reshape(1), taps_deep, *same, *other, *all_cots)

    grad = terms + swap(terms, "space", 1)
    grad = jnp.transpose(grad.reshape(3, 3, 3, cmid, cout), (0, 1, 2, 4, 3))
    return deep_out[:, None], grad


def on_device(volume, weight_first, weight_deep, cotangent):
    spaces, chans = lax.axis_size("space"), lax.axis_size("chan")
    powers = spaces & (spaces - 1) == 0 and chans & (chans - 1) == 0
    fits = spaces * cotangent.shape[0] * cotangent.shape[2] <= 2**20
    if powers and fits and spaces > 1 and volume.shape[1:3] == (2, 2):
        return by_gather(volume, weight_first, weight_deep, cotangent)
    return by_halos(volume, weight_first, weight_deep, cotangent)


def solution(mesh):
    return jax.shard_map(
        on_device,
        mesh=mesh,
        in_specs=(
            P(None, "space", "chan", None),
            P(),
            P(None, None, None, "chan", None),
            P("chan", "space", None),
        ),
        out_specs=(P("chan", "space", None), P(None, None, None, "chan", None)),
        check_vma=False,
    )
```

time: 130 us -> 33.6 us (0.26)
  waiting for transfers between devices: 69.5 us -> 4.47 us
  matrix products: 15.8 us -> 0 us
  between operations: 14.7 us -> 0.77 us
  blocking collectives: 13.6 us -> 0 us
  starting transfers between devices: 11.2 us -> 22.7 us
  Pallas kernels: 0 us -> 3.27 us
  local copies, waits for them, and re-layouts: 3.93 us -> 1.17 us
    psum x1 -> x0, waiting for transfers between devices: 57.9 us -> none  [on_device(): grad_deep = lax.psum(local_grad, 'space')]
    dot_general x81 -> x0, matrix products: 15.8 us -> none  [the longest x54 10.5 us: convolve(): jnp.einsum('oc,cxyz->oxyz', weight[offset_x, offset_y, offset_z], window,...]
    all_gather x1 -> x0, blocking collectives: 13.6 us -> none  [on_device(): whole = lax.all_gather(pooled, 'chan', axis=2, tiled=True)]
    ppermute x6 -> x16, starting transfers between devices: 11.1 us -> 22.7 us  [the longest x15 22.1 us: swap(): return lax.ppermute(array, axis, [(i, i ^ bits) for i in range(peers)])]
    ppermute x6 -> x16, waiting for transfers between devices: 11.6 us -> 4.47 us  [the longest x15 4.47 us: swap(): return lax.ppermute(array, axis, [(i, i ^ bits) for i in range(peers)])]
    pallas_call x0 -> x2, Pallas kernels: none -> 3.27 us  [the longest x1 1.99 us: by_gather(): pl.pallas_call(functools.partial(deep_kernel, groups, depth // 2), out_sh...]
    unnamed x13 -> x7, local copies, waits for them, and re-layouts: 3.72 us -> 0.82 us
  transfers between devices with their start and end apart: 7 -> 16, of which waited for: 5 -> 5; matrix products, arithmetic and copies ran while one was open for 1% -> 1% of each run, Pallas kernels for 0% -> 4%
where the time goes in v1:
time: 33.6 us; the launch traced here: 33.4 us
  starting transfers between devices  22.7 us (68%)
  waiting for transfers between devices  4.47 us (13%)
  Pallas kernels  3.27 us (10%)
  local copies, waits for them, and re-layouts  1.17 us (3%)
  other arithmetic  1.03 us (3%)
  between operations  0.77 us (2%)
    ppermute x15, starting transfers between devices, swap(): return lax.ppermute(array, axis, [(i, i ^ bits) for i in range(peers)])  22.1 us
    ppermute x15, waiting for transfers between devices, swap(): return lax.ppermute(array, axis, [(i, i ^ bits) for i in range(peers)])  4.47 us
    pallas_call x1, Pallas kernels, by_gather(): pl.pallas_call(functools.partial(deep_kernel, groups, depth // 2), out_sh...  1.99 us
    pallas_call x1, Pallas kernels, by_gather(): pl.pallas_call(functools.partial(first_kernel, chans), out_shape=jax.Shap...  1.29 us
    add x1, other arithmetic, by_gather(): grad = terms + swap(terms, 'space', 1)  1 us
    unnamed x7, local copies, waits for them, and re-layouts  0.82 us
  transfers between devices with their start and end apart: 16, of which 5 were waited for; matrix products, arithmetic and copies ran while one was open for 1% of the time, Pallas kernels for 4%

profile of v1, /device:TPU:0, one launch (start us, length us, event | category | flops | bytes accessed | tf_op | source)
XLA Modules:
  0.0 33.4 jit_solution(6943427042984889589)
XLA Ops:
  0.7 0.8 %copy.13 = bf16[32,2,2,128]{3,0,2,1:T(8,128)(2,1)S(1)} copy(bf16[32,2,2,128]{3,2,1,0:T(2,128)(2,1)} %param.4) | data formatting | bytes 65536 | tf_op args[0]
  1.5 0.5 %collective-permute-start = (bf16[2,32,128]{2,1,0:T(8,128)(2,1)S(1)}, bf16[2,32,128]{2,1,0:T(8,128)(2,1)S(1)}, u32[]{:S(2)}, u32[]{:S(2)}) collective-permute-start(bf16[2,32,128]{2,1,0:T(8,128)(2,1)S(1)} %get-tuple-element.8), channel_id=1, source_target_pairs={{0,4},{4,0},{8,12},{12,8},{16,20},{20,16},{24,28},{28,24},{1,5},{5... | collective-permute-start | bytes 49160 | tf_op jit(solution)/shard_map/ppermute | solution.py:203
  2.0 0.7 %collective-permute-start.1 = (bf16[2,32,128]{2,1,0:T(8,128)(2,1)S(1)}, bf16[2,32,128]{2,1,0:T(8,128)(2,1)S(1)}, u32[]{:S(2)}, u32[]{:S(2)}) collective-permute-start(bf16[2,32,128]{2,1,0:T(8,128)(2,1)S(1)} %get-tuple-element.9), channel_id=1, source_target_pairs={{4,8},{12,16},{20,24},{8,4},{16,12},{24,20},{5,9},{13,17},{21,25},... | collective-permute-start | bytes 49160 | tf_op jit(solution)/shard_map/ppermute | solution.py:220
  2.6 0.2 collective-permute-done
  2.8 0.0 collective-permute-done.1
  2.8 0.0 copy-start
  2.9 0.0 copy-start.1
  2.9 5.0 %collective-permute-start.4 = (bf16[4,2,32,128]{3,2,1,0:T(8,128)(2,1)S(1)}, bf16[4,2,32,128]{3,2,1,0:T(8,128)(2,1)S(1)}, u32[]{:S(2)}, u32[]{:S(2)}) collective-permute-start(bf16[4,2,32,128]{3,2,1,0:T(8,128)(2,1)S(1)} %pad_maximum_fusion.refs_0_), channel_id=1, source_target_pairs={{0,3},{1,2},{2,1},{3,0},{4,7},{5,6},{6,5},{7,4},{8,11},{9,10},{10,... | collective-permute-start | bytes 196616 | tf_op jit(solution)/shard_map/ppermute | solution.py:203
  7.9 0.6 %collective-permute-start.2 = (bf16[4,2,32,128]{3,2,1,0:T(8,128)(2,1)S(1)}, bf16[4,2,32,128]{3,2,1,0:T(8,128)(2,1)S(1)}, u32[]{:S(2)}, u32[]{:S(2)}) collective-permute-start(bf16[4,2,32,128]{3,2,1,0:T(8,128)(2,1)S(1)} %pad_maximum_fusion.refs_0_), channel_id=1, source_target_pairs={{0,1},{1,0},{2,3},{3,2},{4,5},{5,4},{6,7},{7,6},{8,9},{9,8},{10,11... | collective-permute-start | bytes 196616 | tf_op jit(solution)/shard_map/ppermute | solution.py:203
  8.5 6.5 %collective-permute-start.14 = (bf16[128,256]{1,0:T(8,128)(2,1)S(1)}, bf16[128,256]{1,0:T(8,128)(2,1)S(1)}, u32[]{:S(2)}, u32[]{:S(2)}) collective-permute-start(bf16[128,256]{1,0:T(8,128)(2,1)S(1)} %bitcast.24), channel_id=1, source_target_pairs={{0,24},{4,28},{8,16},{12,20},{16,8},{20,12},{24,0},{28,4},{1,25},{... | collective-permute-start | bytes 196616 | tf_op jit(solution)/shard_map/ppermute | solution.py:203
  15.0 0.5 %collective-permute-start.13 = (bf16[128,256]{1,0:T(8,128)(2,1)S(1)}, bf16[128,256]{1,0:T(8,128)(2,1)S(1)}, u32[]{:S(2)}, u32[]{:S(2)}) collective-permute-start(bf16[128,256]{1,0:T(8,128)(2,1)S(1)} %bitcast.25), channel_id=1, source_target_pairs={{0,16},{4,20},{8,24},{12,28},{16,0},{20,4},{24,8},{28,12},{1,17},{... | collective-permute-start | bytes 196616 | tf_op jit(solution)/shard_map/ppermute | solution.py:203
  15.5 0.1 copy.10.w_ref
  15.7 0.0 collective-permute-done.3.refs_2_
  15.7 0.0 collective-permute-done.2.refs_1_
  15.7 1.3 %first.1.refs_0_ = bf16[64,256]{1,0:T(8,128)(2,1)S(1)} custom-call(s32[1]{0:T(128)} %bitcast.3.place_ref, bf16[64,864]{1,0:T(8,128)(2,1)S(1)} %copy.10.w_ref, bf16[4,2,32,128]{3,2,1,0:T(8,128)(2,1)S(1)} %pad_maximum_fusion.refs_0_, bf16[4,2,32,128]{3,2,1,0:T(8,128)(2,1)S(1)} %collective-permute-done.2.refs_1_, ...), custom_call_target="tpu_custom_call" | custom-call | tf_op jit(solution)/shard_map/first/pallas_call | solution.py:234
  17.0 3.8 %collective-permute-start.7 = (bf16[64,256]{1,0:T(8,128)(2,1)S(1)}, bf16[64,256]{1,0:T(8,128)(2,1)S(1)}, u32[]{:S(2)}, u32[]{:S(2)}) collective-permute-start(bf16[64,256]{1,0:T(8,128)(2,1)S(1)} %first.1.refs_0_), channel_id=1, source_target_pairs={{0,24},{4,28},{8,16},{12,20},{16,8},{20,12},{24,0},{28,4},{1,25},{... | collective-permute-start | bytes 98312 | tf_op jit(solution)/shard_map/ppermute | solution.py:203
  20.7 1.9 %collective-permute-start.12 = (bf16[128,256]{1,0:T(8,128)(2,1)S(1)}, bf16[128,256]{1,0:T(8,128)(2,1)S(1)}, u32[]{:S(2)}, u32[]{:S(2)}) collective-permute-start(bf16[128,256]{1,0:T(8,128)(2,1)S(1)} %bitcast.26), channel_id=1, source_target_pairs={{0,8},{4,12},{8,0},{12,4},{16,24},{20,28},{24,16},{28,20},{1,9},{5... | collective-permute-start | bytes 196616 | tf_op jit(solution)/shard_map/ppermute | solution.py:203
  22.7 0.0 collective-permute-start.6
  22.7 0.0 collective-permute-done.14.refs_11_
  22.7 1.8 %collective-permute-start.5 = (bf16[64,256]{1,0:T(8,128)(2,1)S(1)}, bf16[64,256]{1,0:T(8,128)(2,1)S(1)}, u32[]{:S(2)}, u32[]{:S(2)}) collective-permute-start(bf16[64,256]{1,0:T(8,128)(2,1)S(1)} %first.1.refs_0_), channel_id=1, source_target_pairs={{0,8},{4,12},{8,0},{12,4},{16,24},{20,28},{24,16},{28,20},{1,9},{5... | collective-permute-start | bytes 98312 | tf_op jit(solution)/shard_map/ppermute | solution.py:203
  24.5 0.0 collective-permute-start.8
  24.5 0.5 %collective-permute-start.11 = (bf16[64,256]{1,0:T(8,128)(2,1)S(1)}, bf16[64,256]{1,0:T(8,128)(2,1)S(1)}, u32[]{:S(2)}, u32[]{:S(2)}) collective-permute-start(bf16[64,256]{1,0:T(8,128)(2,1)S(1)} %collective-permute-done.7.refs_3_), channel_id=1, source_target_pairs={{0,4},{4,0},{8,12},{12,8},{16,20},{20,16},{24,28},{28,24},{1,5},{5... | collective-permute-start | bytes 98312 | tf_op jit(solution)/shard_map/ppermute | solution.py:203
  25.0 1.6 %collective-permute-done.6.refs_2_ = bf16[64,256]{1,0:T(8,128)(2,1)S(1)} collective-permute-done((bf16[64,256]{1,0:T(8,128)(2,1)S(1)}, bf16[64,256]{1,0:T(8,128)(2,1)S(1)}, u32[]{:S(2)}, u32[]{:S(2)}) %collective-permute-start.6) | collective-permute-done | bytes 32800 | tf_op jit(solution)/shard_map/ppermute | solution.py:203
  26.6 0.0 collective-permute-done.5.refs_1_
  26.6 0.5 %collective-permute-start.9 = (bf16[64,256]{1,0:T(8,128)(2,1)S(1)}, bf16[64,256]{1,0:T(8,128)(2,1)S(1)}, u32[]{:S(2)}, u32[]{:S(2)}) collective-permute-start(bf16[64,256]{1,0:T(8,128)(2,1)S(1)} %collective-permute-done.5.refs_1_), channel_id=1, source_target_pairs={{0,4},{4,0},{8,12},{12,8},{16,20},{20,16},{24,28},{28,24},{1,5},{5... | collective-permute-start | bytes 98312 | tf_op jit(solution)/shard_map/ppermute | solution.py:203
  27.1 0.2 copy.11.w_ref
  27.3 0.4 %collective-permute-done.10.refs_6_ = bf16[64,256]{1,0:T(8,128)(2,1)S(1)} collective-permute-done((bf16[64,256]{1,0:T(8,128)(2,1)S(1)}, bf16[64,256]{1,0:T(8,128)(2,1)S(1)}, u32[]{:S(2)}, u32[]{:S(2)}) %collective-permute-start.10) | collective-permute-done | bytes 32800 | tf_op jit(solution)/shard_map/ppermute | solution.py:203
  27.8 0.2 collective-permute-done.9.refs_5_
  27.9 2.0 %deep.1 = (bf16[128,256]{1,0:T(8,128)(2,1)}, f32[1728,128]{1,0:T(8,128)S(1)}) custom-call(s32[1]{0:T(128)} %bitcast.place_ref, bf16[128,1728]{1,0:T(8,128)(2,1)S(1)} %copy.11.w_ref, bf16[64,256]{1,0:T(8,128)(2,1)S(1)} %first.1.refs_0_, bf16[64,256]{1,0:T(8,128)(2,1)S(1)} %collective-permute-done.5.refs_1_, ...), custom_call_target="tpu_custom_call" | custom-call | tf_op jit(solution)/shard_map/deep/pallas_call | solution.py:251
  29.9 0.4 %collective-permute-start.15 = (f32[1728,128]{1,0:T(8,128)S(1)}, f32[1728,128]{1,0:T(8,128)S(1)}, u32[]{:S(2)}, u32[]{:S(2)}) collective-permute-start(f32[1728,128]{1,0:T(8,128)S(1)} %get-tuple-element.5), channel_id=1, source_target_pairs={{0,4},{4,0},{8,12},{12,8},{16,20},{20,16},{24,28},{28,24},{1,5},{5... | collective-permute-start | bytes 2654216 | tf_op jit(solution)/shard_map/ppermute | solution.py:203
  30.4 2.1 %collective-permute-done.15 = f32[1728,128]{1,0:T(8,128)S(1)} collective-permute-done((f32[1728,128]{1,0:T(8,128)S(1)}, f32[1728,128]{1,0:T(8,128)S(1)}, u32[]{:S(2)}, u32[]{:S(2)}) %collective-permute-start.15) | collective-permute-done | bytes 884768 | tf_op jit(solution)/shard_map/ppermute | solution.py:203
  32.4 1.0 %add.8 = f32[1728,128]{1,0:T(8,128)} add(f32[1728,128]{1,0:T(8,128)S(1)} %get-tuple-element.5, f32[1728,128]{1,0:T(8,128)S(1)} %collective-permute-done.15) | non-fusion elementwise | flops 221184 | bytes 2654208 | tf_op jit(solution)/shard_map/add | solution.py:270
  (15 shorter events, 0.1 us)
Async XLA Ops:
  0.6 14.9 %copy-start.2 = (bf16[3,3,3,64,32]{3,4,2,1,0:T(8,128)(2,1)S(1)}, bf16[3,3,3,64,32]{3,4,2,1,0:T(8,128)(2,1)}, u32[]{:S(2)}) copy-start(bf16[3,3,3,64,32]{3,4,2,1,0:T(8,128)(2,1)} %param.5) | copy-start | bytes 331780
  1.5 1.4 %collective-permute-start = (bf16[2,32,128]{2,1,0:T(8,128)(2,1)S(1)}, bf16[2,32,128]{2,1,0:T(8,128)(2,1)S(1)}, u32[]{:S(2)}, u32[]{:S(2)}) collective-permute-start(bf16[2,32,128]{2,1,0:T(8,128)(2,1)S(1)} %get-tuple-element.8), channel_id=1, source_target_pairs={{0,4},{4,0},{8,12},{12,8},{16,20},{20,16},{24,28},{28,24},{1,5},{5... | collective-permute-start | bytes 49160 | tf_op jit(solution)/shard_map/ppermute | solution.py:203
  2.0 0.8 %collective-permute-start.1 = (bf16[2,32,128]{2,1,0:T(8,128)(2,1)S(1)}, bf16[2,32,128]{2,1,0:T(8,128)(2,1)S(1)}, u32[]{:S(2)}, u32[]{:S(2)}) collective-permute-start(bf16[2,32,128]{2,1,0:T(8,128)(2,1)S(1)} %get-tuple-element.9), channel_id=1, source_target_pairs={{4,8},{12,16},{20,24},{8,4},{16,12},{24,20},{5,9},{13,17},{21,25},... | collective-permute-start | bytes 49160 | tf_op jit(solution)/shard_map/ppermute | solution.py:220
  2.8 5.7 %copy-start = (bf16[128,1,256]{2,0,1:T(8,128)(2,1)S(1)}, bf16[128,1,256]{2,0,1:T(8,128)(2,1)}, u32[]{:S(2)}) copy-start(bf16[128,1,256]{2,0,1:T(8,128)(2,1)} %param.7) | copy-start | bytes 196612
  2.9 24.2 %copy-start.1 = (bf16[3,3,3,128,64]{3,4,2,1,0:T(8,128)(2,1)S(1)}, bf16[3,3,3,128,64]{3,4,2,1,0:T(8,128)(2,1)}, u32[]{:S(2)}) copy-start(bf16[3,3,3,128,64]{3,4,2,1,0:T(8,128)(2,1)} %param.6) | copy-start | bytes 1327108
  2.9 12.8 %collective-permute-start.4 = (bf16[4,2,32,128]{3,2,1,0:T(8,128)(2,1)S(1)}, bf16[4,2,32,128]{3,2,1,0:T(8,128)(2,1)S(1)}, u32[]{:S(2)}, u32[]{:S(2)}) collective-permute-start(bf16[4,2,32,128]{3,2,1,0:T(8,128)(2,1)S(1)} %pad_maximum_fusion.refs_0_), channel_id=1, source_target_pairs={{0,3},{1,2},{2,1},{3,0},{4,7},{5,6},{6,5},{7,4},{8,11},{9,10},{10,... | collective-permute-start | bytes 196616 | tf_op jit(solution)/shard_map/ppermute | solution.py:203
  7.9 7.8 %collective-permute-start.3 = (bf16[4,2,32,128]{3,2,1,0:T(8,128)(2,1)S(1)}, bf16[4,2,32,128]{3,2,1,0:T(8,128)(2,1)S(1)}, u32[]{:S(2)}, u32[]{:S(2)}) collective-permute-start(bf16[4,2,32,128]{3,2,1,0:T(8,128)(2,1)S(1)} %pad_maximum_fusion.refs_0_), channel_id=1, source_target_pairs={{0,2},{1,3},{2,0},{3,1},{4,6},{5,7},{6,4},{7,5},{8,10},{9,11},{10,... | collective-permute-start | bytes 196616 | tf_op jit(solution)/shard_map/ppermute | solution.py:203
  7.9 7.8 %collective-permute-start.2 = (bf16[4,2,32,128]{3,2,1,0:T(8,128)(2,1)S(1)}, bf16[4,2,32,128]{3,2,1,0:T(8,128)(2,1)S(1)}, u32[]{:S(2)}, u32[]{:S(2)}) collective-permute-start(bf16[4,2,32,128]{3,2,1,0:T(8,128)(2,1)S(1)} %pad_maximum_fusion.refs_0_), channel_id=1, source_target_pairs={{0,1},{1,0},{2,3},{3,2},{4,5},{5,4},{6,7},{7,6},{8,9},{9,8},{10,11... | collective-permute-start | bytes 196616 | tf_op jit(solution)/shard_map/ppermute | solution.py:203
  8.5 14.1 %collective-permute-start.14 = (bf16[128,256]{1,0:T(8,128)(2,1)S(1)}, bf16[128,256]{1,0:T(8,128)(2,1)S(1)}, u32[]{:S(2)}, u32[]{:S(2)}) collective-permute-start(bf16[128,256]{1,0:T(8,128)(2,1)S(1)} %bitcast.24), channel_id=1, source_target_pairs={{0,24},{4,28},{8,16},{12,20},{16,8},{20,12},{24,0},{28,4},{1,25},{... | collective-permute-start | bytes 196616 | tf_op jit(solution)/shard_map/ppermute | solution.py:203
  15.0 9.5 %collective-permute-start.13 = (bf16[128,256]{1,0:T(8,128)(2,1)S(1)}, bf16[128,256]{1,0:T(8,128)(2,1)S(1)}, u32[]{:S(2)}, u32[]{:S(2)}) collective-permute-start(bf16[128,256]{1,0:T(8,128)(2,1)S(1)} %bitcast.25), channel_id=1, source_target_pairs={{0,16},{4,20},{8,24},{12,28},{16,0},{20,4},{24,8},{28,12},{1,17},{... | collective-permute-start | bytes 196616 | tf_op jit(solution)/shard_map/ppermute | solution.py:203
  17.0 7.5 %collective-permute-start.7 = (bf16[64,256]{1,0:T(8,128)(2,1)S(1)}, bf16[64,256]{1,0:T(8,128)(2,1)S(1)}, u32[]{:S(2)}, u32[]{:S(2)}) collective-permute-start(bf16[64,256]{1,0:T(8,128)(2,1)S(1)} %first.1.refs_0_), channel_id=1, source_target_pairs={{0,24},{4,28},{8,16},{12,20},{16,8},{20,12},{24,0},{28,4},{1,25},{... | collective-permute-start | bytes 98312 | tf_op jit(solution)/shard_map/ppermute | solution.py:203
  20.7 6.6 %collective-permute-start.12 = (bf16[128,256]{1,0:T(8,128)(2,1)S(1)}, bf16[128,256]{1,0:T(8,128)(2,1)S(1)}, u32[]{:S(2)}, u32[]{:S(2)}) collective-permute-start(bf16[128,256]{1,0:T(8,128)(2,1)S(1)} %bitcast.26), channel_id=1, source_target_pairs={{0,8},{4,12},{8,0},{12,4},{16,24},{20,28},{24,16},{28,20},{1,9},{5... | collective-permute-start | bytes 196616 | tf_op jit(solution)/shard_map/ppermute | solution.py:203
  22.7 3.9 %collective-permute-start.6 = (bf16[64,256]{1,0:T(8,128)(2,1)S(1)}, bf16[64,256]{1,0:T(8,128)(2,1)S(1)}, u32[]{:S(2)}, u32[]{:S(2)}) collective-permute-start(bf16[64,256]{1,0:T(8,128)(2,1)S(1)} %first.1.refs_0_), channel_id=1, source_target_pairs={{0,16},{4,20},{8,24},{12,28},{16,0},{20,4},{24,8},{28,12},{1,17},{... | collective-permute-start | bytes 98312 | tf_op jit(solution)/shard_map/ppermute | solution.py:203
  22.7 3.9 %collective-permute-start.5 = (bf16[64,256]{1,0:T(8,128)(2,1)S(1)}, bf16[64,256]{1,0:T(8,128)(2,1)S(1)}, u32[]{:S(2)}, u32[]{:S(2)}) collective-permute-start(bf16[64,256]{1,0:T(8,128)(2,1)S(1)} %first.1.refs_0_), channel_id=1, source_target_pairs={{0,8},{4,12},{8,0},{12,4},{16,24},{20,28},{24,16},{28,20},{1,9},{5... | collective-permute-start | bytes 98312 | tf_op jit(solution)/shard_map/ppermute | solution.py:203
  24.5 2.8 %collective-permute-start.8 = (bf16[64,256]{1,0:T(8,128)(2,1)S(1)}, bf16[64,256]{1,0:T(8,128)(2,1)S(1)}, u32[]{:S(2)}, u32[]{:S(2)}) collective-permute-start(bf16[64,256]{1,0:T(8,128)(2,1)S(1)} %first.1.refs_0_), channel_id=1, source_target_pairs={{0,4},{4,0},{8,12},{12,8},{16,20},{20,16},{24,28},{28,24},{1,5},{5... | collective-permute-start | bytes 98312 | tf_op jit(solution)/shard_map/ppermute | solution.py:203
  24.5 2.8 %collective-permute-start.11 = (bf16[64,256]{1,0:T(8,128)(2,1)S(1)}, bf16[64,256]{1,0:T(8,128)(2,1)S(1)}, u32[]{:S(2)}, u32[]{:S(2)}) collective-permute-start(bf16[64,256]{1,0:T(8,128)(2,1)S(1)} %collective-permute-done.7.refs_3_), channel_id=1, source_target_pairs={{0,4},{4,0},{8,12},{12,8},{16,20},{20,16},{24,28},{28,24},{1,5},{5... | collective-permute-start | bytes 98312 | tf_op jit(solution)/shard_map/ppermute | solution.py:203
  26.6 1.2 %collective-permute-start.10 = (bf16[64,256]{1,0:T(8,128)(2,1)S(1)}, bf16[64,256]{1,0:T(8,128)(2,1)S(1)}, u32[]{:S(2)}, u32[]{:S(2)}) collective-permute-start(bf16[64,256]{1,0:T(8,128)(2,1)S(1)} %collective-permute-done.6.refs_2_), channel_id=1, source_target_pairs={{0,4},{4,0},{8,12},{12,8},{16,20},{20,16},{24,28},{28,24},{1,5},{5... | collective-permute-start | bytes 98312 | tf_op jit(solution)/shard_map/ppermute | solution.py:203
  26.6 1.4 %collective-permute-start.9 = (bf16[64,256]{1,0:T(8,128)(2,1)S(1)}, bf16[64,256]{1,0:T(8,128)(2,1)S(1)}, u32[]{:S(2)}, u32[]{:S(2)}) collective-permute-start(bf16[64,256]{1,0:T(8,128)(2,1)S(1)} %collective-permute-done.5.refs_1_), channel_id=1, source_target_pairs={{0,4},{4,0},{8,12},{12,8},{16,20},{20,16},{24,28},{28,24},{1,5},{5... | collective-permute-start | bytes 98312 | tf_op jit(solution)/shard_map/ppermute | solution.py:203
  29.9 2.5 %collective-permute-start.15 = (f32[1728,128]{1,0:T(8,128)S(1)}, f32[1728,128]{1,0:T(8,128)S(1)}, u32[]{:S(2)}, u32[]{:S(2)}) collective-permute-start(f32[1728,128]{1,0:T(8,128)S(1)} %get-tuple-element.5), channel_id=1, source_target_pairs={{0,4},{4,0},{8,12},{12,8},{16,20},{20,16},{24,28},{28,24},{1,5},{5... | collective-permute-start | bytes 2654216 | tf_op jit(solution)/shard_map/ppermute | solution.py:203

commit v2 on v1

v2 whole, which is shorter than its diff:
```python
import functools

import jax
import jax.numpy as jnp
from jax import lax
from jax.experimental import pallas as pl
from jax.experimental.pallas import tpu as pltpu
from jax.sharding import PartitionSpec as P


def padded_2(array, sides, width):
    for axis, dim in sides:
        peers, length = (lax.axis_size(axis), array.shape[dim])
        up = [(i, (i + 1) % peers) for i in range(peers - 1)]
        down = [(j, i) for i, j in up]
        last = lax.slice_in_dim(array, length - width, length, axis=dim)
        leading = lax.slice_in_dim(array, 0, width, axis=dim)
        before = lax.ppermute(last, axis, up)
        after = lax.ppermute(leading, axis, down)
        array = jnp.concatenate([before, array, after], axis=dim)
    return array


def windows(padded, planes, rows, depth):
    for offset_x in range(3):
        for offset_y in range(3):
            for offset_z in range(3):
                yield (offset_x, offset_y, offset_z), padded[
                    :,
                    offset_x : offset_x + planes,
                    offset_y : offset_y + rows,
                    offset_z : offset_z + depth,
                ]


def convolve(padded, weight, planes, rows, depth):
    total = jnp.zeros((weight.shape[3], planes, rows, depth), jnp.float32)
    for tap, window in windows(padded, planes, rows, depth):
        total = total + jnp.einsum(
            "oc,cxyz->oxyz", weight[tap], window, preferred_element_type=jnp.float32
        )
    return total


def weight_terms(grad_pre, padded, planes, rows, depth):
    terms = [
        jnp.einsum("oxyz,cxyz->oc", grad_pre, window, preferred_element_type=jnp.float32)
        for _, window in windows(padded, planes, rows, depth)
    ]
    return jnp.stack(terms).reshape((3, 3, 3) + terms[0].shape)


def pool_mean(act):
    chans, planes, rows, depth = act.shape
    blocks = act.reshape(chans, planes // 2, 2, rows // 2, 2, depth // 2, 2)
    return jnp.mean(blocks, axis=(2, 4, 6))


def by_halos(volume, weight_first, weight_deep, cotangent):
    planes, rows, depth = volume.shape[1:]
    rimmed = padded_2(volume, (("space", 1), ("chan", 2)), 1)
    padded = jnp.pad(rimmed, ((0, 0), (0, 0), (0, 0), (1, 1)))
    pre_first = convolve(padded, weight_first, planes, rows, depth)
    pooled = pool_mean(jax.nn.silu(pre_first)).astype(jnp.bfloat16)
    whole = lax.all_gather(pooled, "chan", axis=2, tiled=True)
    framed = padded_2(whole, (("space", 1),), 1)
    deep_in = jnp.pad(framed, ((0, 0), (0, 0), (1, 1), (1, 1)))
    deep_planes = pooled.shape[1]
    deep_rows, deep_depth = framed.shape[2:]
    pre_deep = convolve(deep_in, weight_deep, deep_planes, deep_rows, deep_depth)
    deep_out = jax.nn.silu(pre_deep).astype(jnp.bfloat16).reshape(cotangent.shape)
    sigma = jax.nn.sigmoid(pre_deep)
    cot_grid = cotangent.reshape(pre_deep.shape).astype(jnp.float32)
    grad_pre = (cot_grid * sigma * (1.0 + pre_deep * (1.0 - sigma))).astype(jnp.bfloat16)
    local_grad = weight_terms(grad_pre, deep_in, deep_planes, deep_rows, deep_depth)
    return deep_out, lax.psum(local_grad, "space")


DN = (((1,), (0,)), ((), ()))
NT = (((1,), (1,)), ((), ()))
TN = (((0,), (0,)), ((), ()))


def fill_patches(grid, moved, patches):
    planes, rows, cin, depth = grid.shape
    lane = lax.broadcasted_iota(jnp.int32, (rows * cin, depth), 1)
    for plane in range(planes):
        flat = grid[plane].reshape(rows * cin, depth).astype(jnp.float32)
        left = jnp.where(lane == 0, 0.0, pltpu.roll(flat, 1, 1))
        right = jnp.where(lane == depth - 1, 0.0, pltpu.roll(flat, depth - 1, 1))
        moved[0, plane] = left.astype(jnp.bfloat16).reshape(rows, cin, depth)
        moved[1, plane] = right.astype(jnp.bfloat16).reshape(rows, cin, depth)
    for plane in range(planes):
        for b in range(3):
            for c in range(3):
                at = ((plane * 3 + b) * 3 + c) * cin
                for row in range(rows - 2):
                    block = grid[plane, row + b] if c == 1 else moved[c // 2, plane, row + b]
                    patches[at : at + cin, row * depth : (row + 1) * depth] = block


def silu(value):
    return value / (1.0 + jnp.exp(-value))


def first_part(chans, place_ref, w_ref, near_ref, *refs):
    blocks, (part_ref, sums_ref, grid, moved, patches) = refs[:chans], refs[-5:]
    planes, rows, cin, depth = grid.shape
    mine, odd = place_ref[0], place_ref[1]
    edge = jnp.zeros((cin, depth), jnp.bfloat16)
    for plane in range(planes):
        grid[plane, 0] = edge
        grid[plane, rows - 1] = edge
    for k in range(chans):
        per = near_ref.shape[1]
        start = 1 + (mine ^ k) * per
        for row in range(per):
            grid[0, start + row] = blocks[k][odd, row]
            grid[1, start + row] = blocks[k][1 - odd, row]
            grid[2, start + row] = near_ref[k, row]
    fill_patches(grid, moved, patches)
    to_far, centre, from_far = w_ref[2 * odd], w_ref[1], w_ref[2 - 2 * odd]
    inner = jnp.concatenate([to_far, centre, from_far], axis=0)
    outer = jnp.concatenate([centre, from_far], axis=0)
    for pair in range((rows - 2) // 2):
        cols = slice(pair * 2 * depth, (pair + 1) * 2 * depth)
        act = silu(lax.dot_general(inner, patches[:, cols], TN, preferred_element_type=jnp.float32))
        sums_ref[:, pair * depth : (pair + 1) * depth] = act[:, :depth] + act[:, depth:]
        part_ref[:, cols] = lax.dot_general(
            outer, patches[: outer.shape[0], cols], TN, preferred_element_type=jnp.float32
        )


def first_rest(place_ref, w_ref, far_ref, part_ref, sums_ref, *refs):
    out_ref, grid, moved, patches = refs[-4:]
    _, rows, cin, depth = grid.shape
    mine, odd, has_far = place_ref[0], place_ref[1], place_ref[2] == 1
    edge = jnp.zeros((cin, depth), jnp.bfloat16)
    grid[0, 0] = edge
    grid[0, rows - 1] = edge
    per = far_ref.shape[1]
    for k in range(far_ref.shape[0]):
        for row in range(per):
            grid[0, 1 + (mine ^ k) * per + row] = jnp.where(has_far, far_ref[k, row], edge)
    fill_patches(grid, moved, patches)
    to_far = w_ref[2 * odd]
    sums = []
    for pair in range((rows - 2) // 2):
        cols = slice(pair * 2 * depth, (pair + 1) * 2 * depth)
        term = lax.dot_general(to_far, patches[:, cols], TN, preferred_element_type=jnp.float32)
        act = silu(part_ref[:, cols] + term)
        total = sums_ref[:, pair * depth : (pair + 1) * depth] + act[:, :depth] + act[:, depth:]
        sums.append(total * 0.125)
    fold_in = lax.broadcasted_iota(jnp.int32, (2 * depth, depth), 0)
    fold_out = lax.broadcasted_iota(jnp.int32, (2 * depth, depth), 1)
    fold = (fold_in // 2 == fold_out).astype(jnp.float32)
    for pair in range(0, len(sums), 2):
        both = jnp.concatenate([sums[pair], sums[pair + 1]], axis=1)
        halved = lax.dot_general(
            both, fold, DN, precision=lax.Precision.HIGHEST, preferred_element_type=jnp.float32
        )
        out_ref[:, pair // 2 * depth : (pair // 2 + 1) * depth] = halved.astype(jnp.bfloat16)


def deep_kernel(rowlen, order, place_ref, w_ref, cot_ref, cot_swapped_ref, *refs):
    count = len(refs) - 7
    planes, refs = refs[:count], refs[count:]
    out_ref, grad_ref, held, cot, act, taps, shifted = refs
    cmid, cells = held.shape[1:]
    cout = cot.shape[1]
    mine = place_ref[0]
    for k in range(count):
        held[mine ^ 1 ^ k] = planes[k][...]
    for k, bits in enumerate(order):
        cot[mine ^ bits] = cot_ref[k]
        cot[mine ^ bits ^ 1] = cot_swapped_ref[k]
    lane = lax.broadcasted_iota(jnp.int32, (cmid, cells), 1)
    z = lane % rowlen
    edge = jnp.zeros((9 * cmid, cells), jnp.bfloat16)
    taps[:, :cells] = edge
    taps[:, (count + 1) * cells :] = edge
    for slot in range(count):
        plane = held[slot].astype(jnp.float32)
        for b in range(3):
            for c in range(3):
                shift = (b - 1) * rowlen + (c - 1)
                value = plane
                if shift:
                    value = pltpu.roll(plane, (-shift) % cells, 1)
                    ok = None
                    if b == 0:
                        ok = lane >= rowlen
                    if b == 2:
                        ok = lane < cells - rowlen
                    if c != 1:
                        inside = z > 0 if c == 0 else z < rowlen - 1
                        ok = inside if ok is None else ok & inside
                    value = jnp.where(ok, value, 0.0)
                row = (b * 3 + c) * cmid
                taps[row : row + cmid, (slot + 1) * cells : (slot + 2) * cells] = value.astype(jnp.bfloat16)
    depth = 9 * cmid
    empty = jnp.zeros((cout, cells), jnp.bfloat16)
    for p in range(count):
        rhs = jnp.concatenate(
            [taps[:, (p + a) * cells : (p + a + 1) * cells] for a in range(3)], axis=0
        )
        value = lax.dot_general(w_ref[...], rhs, DN, preferred_element_type=jnp.float32)
        sigma = 1.0 / (1.0 + jnp.exp(-value))
        act[p] = (value * sigma).astype(jnp.bfloat16)
        grad_pre = cot[p].astype(jnp.float32) * sigma * (1.0 + value * (1.0 - sigma))
        for a in range(3):
            q = p + a - 1
            if 0 <= q < count:
                shifted[a * cout : (a + 1) * cout, q * cells : (q + 1) * cells] = grad_pre.astype(
                    jnp.bfloat16
                )
    shifted[:cout, (count - 1) * cells :] = empty
    shifted[2 * cout :, :cells] = empty
    out_ref[...] = act[mine]
    half = depth // 2
    for row in range(0, depth, half):
        terms = lax.dot_general(
            taps[row : row + half, cells : (count + 1) * cells],
            shifted[...],
            NT,
            preferred_element_type=jnp.float32,
        )
        for a in range(3):
            at = a * depth + row
            grad_ref[at : at + half] = terms[:, a * cout : (a + 1) * cout]


def swap(array, axis, bits):
    peers = lax.axis_size(axis)
    return lax.ppermute(array, axis, [(i, i ^ bits) for i in range(peers)])


def crossed(array, bits):
    spaces, chans = lax.axis_size("space"), lax.axis_size("chan")
    pairs = [(s * chans + c, (s ^ 1) * chans + (c ^ bits)) for s in range(spaces) for c in range(chans)]
    return lax.ppermute(array, ("space", "chan"), pairs)


def spread(array, order):
    direct = [swap(array, "space", bits) if bits else array for bits in order]
    pieces = {}
    for bits, piece in zip(order, direct):
        pieces[bits], pieces[bits ^ 1] = piece, swap(piece, "space", 1)
    return [pieces[k] for k in range(2 * len(order))]


def by_gather(volume, weight_first, weight_deep, cotangent):
    cin, planes, rows, depth = volume.shape
    spaces, chans = lax.axis_size("space"), lax.axis_size("chan")
    cmid, cout, cells = weight_first.shape[3], weight_deep.shape[3], cotangent.shape[2]
    all_rows = chans * rows
    at_space, at_chan = lax.axis_index("space"), lax.axis_index("chan")
    role = at_space ^ 1
    odd = role % 2
    order = [k | k.bit_count() % 2 for k in range(0, spaces, 2)]
    vmem, smem = pl.BlockSpec(memory_space=pltpu.VMEM), pl.BlockSpec(memory_space=pltpu.SMEM)
    unread = pl.BlockSpec(memory_space=pl.ANY)

    block = jnp.transpose(volume, (1, 2, 0, 3))
    blocks = [crossed(block, k) for k in range(chans)]
    first = jnp.stack([piece[0] for piece in blocks])
    last = jnp.stack([piece[planes - 1] for piece in blocks])
    near = swap(jnp.where(odd == 1, first, last), "space", 1)
    pairs = [(i ^ 1, ((i + 1) % spaces) ^ 1) for i in range(1, spaces, 2)]
    far = lax.ppermute(
        jnp.where(odd == 1, last, first), "space", pairs + [(j, i) for i, j in pairs]
    )
    has_far = ((role > 0) & (role < spaces - 1)).astype(jnp.int32)
    place = jnp.stack([at_chan, odd, has_far])

    cots = [cotangent[:, 0]]
    cots = cots + [swap(cots[0], "space", bits) for bits in order[1:]]

    taps_first = jnp.transpose(weight_first, (0, 1, 2, 4, 3)).reshape(3, 9 * cin, cmid)

    def patch_scratch(count):
        return [
            pltpu.VMEM((count, all_rows + 2, cin, depth), jnp.bfloat16),
            pltpu.VMEM((2, count, all_rows + 2, cin, depth), jnp.bfloat16),
            pltpu.VMEM((count * 9 * cin, all_rows * depth), jnp.bfloat16),
        ]

    params = pltpu.CompilerParams(vmem_limit_bytes=32 * 2**20)
    part, sums = pl.pallas_call(
        functools.partial(first_part, chans),
        out_shape=(
            jax.ShapeDtypeStruct((cmid, all_rows * depth), jnp.float32),
            jax.ShapeDtypeStruct((cmid, all_rows * depth // 2), jnp.float32),
        ),
        in_specs=[smem, vmem, vmem] + [vmem] * chans,
        out_specs=(vmem, vmem),
        scratch_shapes=patch_scratch(planes + 1),
        compiler_params=params,
        name="first_part",
        cost_estimate=pl.CostEstimate(flops=0, bytes_accessed=5000000, transcendentals=0),
    )(place, taps_first, near, *blocks)

    pooled = pl.pallas_call(
        first_rest,
        out_shape=jax.ShapeDtypeStruct((cmid, cells), jnp.bfloat16),
        in_specs=[smem, vmem, vmem, vmem, vmem],
        out_specs=vmem,
        scratch_shapes=patch_scratch(1),
        compiler_params=params,
        name="first_rest",
        cost_estimate=pl.CostEstimate(flops=0, bytes_accessed=4000000, transcendentals=0),
    )(place, taps_first, far, part, sums)

    pooled, weight_deep, *cots = lax.optimization_barrier((pooled, weight_deep, *cots))
    taps_deep = jnp.transpose(weight_deep, (3, 0, 1, 2, 4)).reshape(cout, 27 * cmid)
    cots = jnp.stack(cots)
    cots_swapped = swap(cots, "space", 1)
    all_pooled = spread(pooled, order)

    deep_out, terms = pl.pallas_call(
        functools.partial(deep_kernel, depth // 2, order),
        out_shape=(
            jax.ShapeDtypeStruct((cout, cells), jnp.bfloat16),
            jax.ShapeDtypeStruct((27 * cmid, cout), jnp.float32),
        ),
        in_specs=[smem] + [vmem] * (3 + spaces),
        out_specs=(vmem, vmem),
        scratch_shapes=[
            pltpu.VMEM((spaces, cmid, cells), jnp.bfloat16),
            pltpu.VMEM((spaces, cout, cells), jnp.bfloat16),
            pltpu.VMEM((spaces, cout, cells), jnp.bfloat16),
            pltpu.VMEM((9 * cmid, (spaces + 2) * cells), jnp.bfloat16),
            pltpu.VMEM((3 * cout, spaces * cells), jnp.bfloat16),
        ],
        compiler_params=params,
        name="deep",
        cost_estimate=pl.CostEstimate(flops=0, bytes_accessed=12000000, transcendentals=0),
    )(at_space.reshape(1), taps_deep, cots, cots_swapped, *all_pooled)

    grad = jnp.transpose(terms.reshape(3, 3, 3, cmid, cout), (0, 1, 2, 4, 3))
    return deep_out[:, None], grad


def on_device(volume, weight_first, weight_deep, cotangent):
    spaces, chans = lax.axis_size("space"), lax.axis_size("chan")
    powers = spaces & (spaces - 1) == 0 and chans & (chans - 1) == 0
    fits = spaces * cotangent.shape[0] * cotangent.shape[2] <= 2**20
    if powers and fits and spaces > 1 and volume.shape[1:3] == (2, 2):
        return by_gather(volume, weight_first, weight_deep, cotangent)
    return by_halos(volume, weight_first, weight_deep, cotangent)


def solution(mesh):
    return jax.shard_map(
        on_device,
        mesh=mesh,
        in_specs=(
            P(None, "space", "chan", None),
            P(),
            P(None, None, None, "chan", None),
            P("chan", "space", None),
        ),
        out_specs=(P("chan", "space", None), P(None, None, None, "chan", None)),
        check_vma=False,
    )
```

time: 33.6 us -> 29.1 us (0.87)
  starting transfers between devices: 22.7 us -> 15.7 us
  Pallas kernels: 3.27 us -> 5.93 us
  waiting for transfers between devices: 4.47 us -> 5.38 us
  other arithmetic: 1.03 us -> 0.14 us
    ppermute x15 -> x12, starting transfers between devices: 22.1 us -> 9.77 us  [swap(): return lax.ppermute(array, axis, [(i, i ^ bits) for i in range(peers)])]
    ppermute x1 -> x5, starting transfers between devices: 0.65 us -> 5.91 us  [the longest x4 5.41 us: crossed(): return lax.ppermute(array, ('space', 'chan'), pairs)]
    pallas_call x2 -> x3, Pallas kernels: 3.27 us -> 5.93 us  [the longest x1 3.43 us: by_gather(): pl.pallas_call(functools.partial(deep_kernel, depth // 2, order), out_sha...]
    ppermute x1 -> x5, waiting for transfers between devices: 0.01 us -> 2.05 us  [the longest x1 1.22 us: by_gather(): lax.ppermute(jnp.where(odd == 1, last, first), 'space', pairs + [(j, i) f...]
    ppermute x15 -> x12, waiting for transfers between devices: 4.47 us -> 3.33 us  [swap(): return lax.ppermute(array, axis, [(i, i ^ bits) for i in range(peers)])]
    add x1 -> x0, other arithmetic: 1 us -> none  [by_gather(): grad = terms + swap(terms, 'space', 1)]
  transfers between devices with their start and end apart: 16 -> 17, of which waited for: 5 -> 8; matrix products, arithmetic and copies ran while one was open for 1% -> 1% of each run, Pallas kernels for 4% -> 9%
where the time goes in v2:
time: 29.1 us; the launch traced here: 28.9 us
  starting transfers between devices  15.7 us (54%)
  Pallas kernels  5.93 us (20%)
  waiting for transfers between devices  5.38 us (18%)
  local copies, waits for them, and re-layouts  1.04 us (4%)
  between operations  0.75 us (3%)
    ppermute x12, starting transfers between devices, swap(): return lax.ppermute(array, axis, [(i, i ^ bits) for i in range(peers)])  9.77 us
    ppermute x4, starting transfers between devices, crossed(): return lax.ppermute(array, ('space', 'chan'), pairs)  5.41 us
    pallas_call x1, Pallas kernels, by_gather(): pl.pallas_call(functools.partial(deep_kernel, depth // 2, order), out_sha...  3.43 us
    ppermute x12, waiting for transfers between devices, swap(): return lax.ppermute(array, axis, [(i, i ^ bits) for i in range(peers)])  3.33 us
    pallas_call x1, Pallas kernels, by_gather(): pl.pallas_call(functools.partial(first_part, chans), out_shape=(jax.Shape...  1.36 us
    ppermute x1, waiting for transfers between devices, by_gather(): lax.ppermute(jnp.where(odd == 1, last, first), 'space', pairs + [(j, i) f...  1.22 us
    pallas_call x1, Pallas kernels, by_gather(): pl.pallas_call(first_rest, out_shape=jax.ShapeDtypeStruct((cmid, cells),...  1.15 us
    ppermute x4, waiting for transfers between devices, crossed(): return lax.ppermute(array, ('space', 'chan'), pairs)  0.83 us
  transfers between devices with their start and end apart: 17, of which 8 were waited for; matrix products, arithmetic and copies ran while one was open for 1% of the time, Pallas kernels for 9%

profile of v2, /device:TPU:0, one launch (start us, length us, event | category | flops | bytes accessed | tf_op | source)
XLA Modules:
  0.0 28.9 jit_solution(916721382371533777)
XLA Ops:
  0.6 0.8 %copy.11 = bf16[32,2,2,128]{3,0,2,1:T(8,128)(2,1)S(1)} copy(bf16[32,2,2,128]{3,2,1,0:T(2,128)(2,1)} %param.4) | data formatting | bytes 65536 | tf_op args[0]
  1.4 4.5 %collective-permute-start.3 = (bf16[2,2,32,128]{3,2,1,0:T(8,128)(2,1)S(1)}, bf16[2,2,32,128]{3,2,1,0:T(8,128)(2,1)S(1)}, u32[]{:S(2)}, u32[]{:S(2)}) collective-permute-start(bf16[2,2,32,128]{3,2,1,0:T(8,128)(2,1)S(1)} %bitcast.32), channel_id=1, source_target_pairs={{0,7},{1,6},{2,5},{3,4},{4,3},{5,2},{6,1},{7,0},{8,15},{9,14},{10,... | collective-permute-start | bytes 98312 | tf_op jit(solution)/shard_map/ppermute | solution.py:241
  5.9 0.0 collective-permute-start.2
  5.9 0.9 %collective-permute-start.1 = (bf16[2,2,32,128]{3,2,1,0:T(8,128)(2,1)S(1)}, bf16[2,2,32,128]{3,2,1,0:T(8,128)(2,1)S(1)}, u32[]{:S(2)}, u32[]{:S(2)}) collective-permute-start(bf16[2,2,32,128]{3,2,1,0:T(8,128)(2,1)S(1)} %bitcast.34), channel_id=1, source_target_pairs={{0,5},{1,4},{2,7},{3,6},{4,1},{5,0},{6,3},{7,2},{8,13},{9,12},{10,... | collective-permute-start | bytes 98312 | tf_op jit(solution)/shard_map/ppermute | solution.py:241
  6.8 2.7 %collective-permute-start.8 = (bf16[128,256]{1,0:T(8,128)(2,1)S(1)}, bf16[128,256]{1,0:T(8,128)(2,1)S(1)}, u32[]{:S(2)}, u32[]{:S(2)}) collective-permute-start(bf16[128,256]{1,0:T(8,128)(2,1)S(1)} %bitcast.25), channel_id=1, source_target_pairs={{0,24},{4,28},{8,16},{12,20},{16,8},{20,12},{24,0},{28,4},{1,25},{... | collective-permute-start | bytes 196616 | tf_op jit(solution)/shard_map/ppermute | solution.py:235
  9.6 0.0 collective-permute-done.3.refs_3_
  9.6 0.1 collective-permute-start.7
  9.6 0.8 %collective-permute-done.2.refs_2_ = bf16[2,2,32,128]{3,2,1,0:T(8,128)(2,1)S(1)} collective-permute-done((bf16[2,2,32,128]{3,2,1,0:T(8,128)(2,1)S(1)}, bf16[2,2,32,128]{3,2,1,0:T(8,128)(2,1)S(1)}, u32[]{:S(2)}, u32[]{:S(2)}) %collective-permute-start.2) | collective-permute-done | bytes 32800 | tf_op jit(solution)/shard_map/ppermute | solution.py:241
  10.5 1.5 %collective-permute-start.6 = (bf16[128,256]{1,0:T(8,128)(2,1)S(1)}, bf16[128,256]{1,0:T(8,128)(2,1)S(1)}, u32[]{:S(2)}, u32[]{:S(2)}) collective-permute-start(bf16[128,256]{1,0:T(8,128)(2,1)S(1)} %bitcast.27), channel_id=1, source_target_pairs={{0,12},{4,8},{8,4},{12,0},{16,28},{20,24},{24,20},{28,16},{1,13},{... | collective-permute-start | bytes 196616 | tf_op jit(solution)/shard_map/ppermute | solution.py:235
  12.0 0.2 collective-permute-start.5
  12.2 0.5 %collective-permute-start.4 = (bf16[4,2,32,128]{3,2,1,0:T(8,128)(2,1)S(1)}, bf16[4,2,32,128]{3,2,1,0:T(8,128)(2,1)S(1)}, u32[]{:S(2)}, u32[]{:S(2)}) collective-permute-start(bf16[4,2,32,128]{3,2,1,0:T(8,128)(2,1)S(1)} %get-tuple-element.23), channel_id=1, source_target_pairs={{0,12},{8,20},{16,28},{24,4},{12,0},{20,8},{28,16},{4,24},{1,13},{... | collective-permute-start | bytes 196616 | tf_op jit(solution)/shard_map/ppermute | solution.py:270
  12.7 0.1 pad_add_fusion.place_ref
  12.8 0.5 %collective-permute-done.5.near_ref = bf16[4,2,32,128]{3,2,1,0:T(8,128)(2,1)S(1)} collective-permute-done((bf16[4,2,32,128]{3,2,1,0:T(8,128)(2,1)S(1)}, bf16[4,2,32,128]{3,2,1,0:T(8,128)(2,1)S(1)}, u32[]{:S(2)}, u32[]{:S(2)}) %collective-permute-start.5) | collective-permute-done | bytes 65568 | tf_op jit(solution)/shard_map/ppermute | solution.py:235
  13.3 1.4 %first_part.1 = (f32[64,1024]{1,0:T(8,128)S(1)}, f32[64,512]{1,0:T(8,128)S(1)}) custom-call(s32[3]{0:T(128)S(1)} %pad_add_fusion.place_ref, bf16[3,288,64]{2,1,0:T(8,128)(2,1)S(1)} %bitcast.22, bf16[4,2,32,128]{3,2,1,0:T(8,128)(2,1)S(1)} %collective-permute-done.5.near_ref, bf16[2,2,32,128]{3,2,1,0:T(8,128)(2,1)S(1)} %collective-permute-done.refs_0_, ...), custom_call_target="tpu_custom_call" | custom-call | bytes 5000000 | tf_op jit(solution)/shard_map/first_part/pallas_call | solution.py:289
  14.7 1.2 %collective-permute-done.4.far_ref = bf16[4,2,32,128]{3,2,1,0:T(8,128)(2,1)S(1)} collective-permute-done((bf16[4,2,32,128]{3,2,1,0:T(8,128)(2,1)S(1)}, bf16[4,2,32,128]{3,2,1,0:T(8,128)(2,1)S(1)}, u32[]{:S(2)}, u32[]{:S(2)}) %collective-permute-start.4) | collective-permute-done | bytes 65568 | tf_op jit(solution)/shard_map/ppermute | solution.py:270
  15.9 1.1 %first_rest.1.refs_0_ = bf16[64,256]{1,0:T(8,128)(2,1)S(1)} custom-call(s32[3]{0:T(128)S(1)} %pad_add_fusion.place_ref, bf16[3,288,64]{2,1,0:T(8,128)(2,1)S(1)} %bitcast.23, bf16[4,2,32,128]{3,2,1,0:T(8,128)(2,1)S(1)} %collective-permute-done.4.far_ref, f32[64,1024]{1,0:T(8,128)S(1)} %get-tuple-element.12.part_ref, f32[64,512]{1,0:T(8,128)S(1)} %get-tuple-element.13.sums_ref), custom_call_target="tpu_custom_call" | custom-call | bytes 4000000 | tf_op jit(solution)/shard_map/first_rest/pallas_call | solution.py:303
  17.1 0.0 copy-start.1
  17.1 0.0 collective-permute-done.8
  17.1 0.0 collective-permute-done.7
  17.2 1.5 %collective-permute-start.9 = (bf16[4,128,256]{2,1,0:T(8,128)(2,1)S(1)}, bf16[4,128,256]{2,1,0:T(8,128)(2,1)S(1)}, u32[]{:S(2)}, u32[]{:S(2)}) collective-permute-start(bf16[4,128,256]{2,1,0:T(8,128)(2,1)S(1)} %pad_maximum_fusion.cot_ref), channel_id=1, source_target_pairs={{0,4},{4,0},{8,12},{12,8},{16,20},{20,16},{24,28},{28,24},{1,5},{5... | collective-permute-start | bytes 786440 | tf_op jit(solution)/shard_map/ppermute | solution.py:235
  18.7 1.4 %collective-permute-start.15 = (bf16[64,256]{1,0:T(8,128)(2,1)S(1)}, bf16[64,256]{1,0:T(8,128)(2,1)S(1)}, u32[]{:S(2)}, u32[]{:S(2)}) collective-permute-start(bf16[64,256]{1,0:T(8,128)(2,1)S(1)} %first_rest.1.refs_0_), channel_id=1, source_target_pairs={{0,24},{4,28},{8,16},{12,20},{16,8},{20,12},{24,0},{28,4},{1,25},{... | collective-permute-start | bytes 98312 | tf_op jit(solution)/shard_map/ppermute | solution.py:235
  20.1 0.7 %collective-permute-start.13 = (bf16[64,256]{1,0:T(8,128)(2,1)S(1)}, bf16[64,256]{1,0:T(8,128)(2,1)S(1)}, u32[]{:S(2)}, u32[]{:S(2)}) collective-permute-start(bf16[64,256]{1,0:T(8,128)(2,1)S(1)} %first_rest.1.refs_0_), channel_id=1, source_target_pairs={{0,20},{4,16},{8,28},{12,24},{16,4},{20,0},{24,12},{28,8},{1,21},{... | collective-permute-start | bytes 98312 | tf_op jit(solution)/shard_map/ppermute | solution.py:235
  20.9 1.0 %collective-permute-start.11 = (bf16[64,256]{1,0:T(8,128)(2,1)S(1)}, bf16[64,256]{1,0:T(8,128)(2,1)S(1)}, u32[]{:S(2)}, u32[]{:S(2)}) collective-permute-start(bf16[64,256]{1,0:T(8,128)(2,1)S(1)} %first_rest.1.refs_0_), channel_id=1, source_target_pairs={{0,12},{4,8},{8,4},{12,0},{16,28},{20,24},{24,20},{28,16},{1,13},{... | collective-permute-start | bytes 98312 | tf_op jit(solution)/shard_map/ppermute | solution.py:235
  21.9 1.7 %collective-permute-done.15.refs_6_ = bf16[64,256]{1,0:T(8,128)(2,1)S(1)} collective-permute-done((bf16[64,256]{1,0:T(8,128)(2,1)S(1)}, bf16[64,256]{1,0:T(8,128)(2,1)S(1)}, u32[]{:S(2)}, u32[]{:S(2)}) %collective-permute-start.15) | collective-permute-done | bytes 32800 | tf_op jit(solution)/shard_map/ppermute | solution.py:235
  23.6 0.4 %collective-permute-done.13.refs_5_ = bf16[64,256]{1,0:T(8,128)(2,1)S(1)} collective-permute-done((bf16[64,256]{1,0:T(8,128)(2,1)S(1)}, bf16[64,256]{1,0:T(8,128)(2,1)S(1)}, u32[]{:S(2)}, u32[]{:S(2)}) %collective-permute-start.13) | collective-permute-done | bytes 32800 | tf_op jit(solution)/shard_map/ppermute | solution.py:235
  24.0 0.3 collective-permute-start.14
  24.3 0.3 collective-permute-start.12
  24.6 0.2 copy.9.w_ref
  24.8 0.1 collective-permute-done.16.refs_7_
  24.8 0.4 %collective-permute-done.14.refs_4_ = bf16[64,256]{1,0:T(8,128)(2,1)S(1)} collective-permute-done((bf16[64,256]{1,0:T(8,128)(2,1)S(1)}, bf16[64,256]{1,0:T(8,128)(2,1)S(1)}, u32[]{:S(2)}, u32[]{:S(2)}) %collective-permute-start.14) | collective-permute-done | bytes 32800 | tf_op jit(solution)/shard_map/ppermute | solution.py:235
  25.2 0.3 collective-permute-done.12.refs_2_
  25.5 3.4 %deep.1 = (bf16[128,256]{1,0:T(8,128)(2,1)}, f32[1728,128]{1,0:T(8,128)}) custom-call(s32[1]{0:T(128)} %bitcast.place_ref, bf16[128,1728]{1,0:T(8,128)(2,1)S(1)} %copy.9.w_ref, bf16[4,128,256]{2,1,0:T(8,128)(2,1)S(1)} %pad_maximum_fusion.cot_ref, bf16[4,128,256]{2,1,0:T(8,128)(2,1)S(1)} %collective-permute-done.9.cot_swapped_ref, ...), custom_call_target="tpu_custom_call" | custom-call | bytes 12000000 | tf_op jit(solution)/shard_map/deep/pallas_call | solution.py:320
  (20 shorter events, 0.1 us)
Async XLA Ops:
  0.6 6.2 %copy-start.2 = (bf16[128,1,256]{2,0,1:T(8,128)(2,1)S(1)}, bf16[128,1,256]{2,0,1:T(8,128)(2,1)}, u32[]{:S(2)}) copy-start(bf16[128,1,256]{2,0,1:T(8,128)(2,1)} %param.7) | copy-start | bytes 196612
  1.4 8.1 %collective-permute-start.3 = (bf16[2,2,32,128]{3,2,1,0:T(8,128)(2,1)S(1)}, bf16[2,2,32,128]{3,2,1,0:T(8,128)(2,1)S(1)}, u32[]{:S(2)}, u32[]{:S(2)}) collective-permute-start(bf16[2,2,32,128]{3,2,1,0:T(8,128)(2,1)S(1)} %bitcast.32), channel_id=1, source_target_pairs={{0,7},{1,6},{2,5},{3,4},{4,3},{5,2},{6,1},{7,0},{8,15},{9,14},{10,... | collective-permute-start | bytes 98312 | tf_op jit(solution)/shard_map/ppermute | solution.py:241
  5.9 4.5 %collective-permute-start.2 = (bf16[2,2,32,128]{3,2,1,0:T(8,128)(2,1)S(1)}, bf16[2,2,32,128]{3,2,1,0:T(8,128)(2,1)S(1)}, u32[]{:S(2)}, u32[]{:S(2)}) collective-permute-start(bf16[2,2,32,128]{3,2,1,0:T(8,128)(2,1)S(1)} %bitcast.33), channel_id=1, source_target_pairs={{0,6},{1,7},{2,4},{3,5},{4,2},{5,3},{6,0},{7,1},{8,14},{9,15},{10,... | collective-permute-start | bytes 98312 | tf_op jit(solution)/shard_map/ppermute | solution.py:241
  5.9 6.0 %collective-permute-start.1 = (bf16[2,2,32,128]{3,2,1,0:T(8,128)(2,1)S(1)}, bf16[2,2,32,128]{3,2,1,0:T(8,128)(2,1)S(1)}, u32[]{:S(2)}, u32[]{:S(2)}) collective-permute-start(bf16[2,2,32,128]{3,2,1,0:T(8,128)(2,1)S(1)} %bitcast.34), channel_id=1, source_target_pairs={{0,5},{1,4},{2,7},{3,6},{4,1},{5,0},{6,3},{7,2},{8,13},{9,12},{10,... | collective-permute-start | bytes 98312 | tf_op jit(solution)/shard_map/ppermute | solution.py:241
  6.8 5.1 %collective-permute-start = (bf16[2,2,32,128]{3,2,1,0:T(8,128)(2,1)S(1)}, bf16[2,2,32,128]{3,2,1,0:T(8,128)(2,1)S(1)}, u32[]{:S(2)}, u32[]{:S(2)}) collective-permute-start(bf16[2,2,32,128]{3,2,1,0:T(8,128)(2,1)S(1)} %bitcast.35), channel_id=1, source_target_pairs={{0,4},{1,5},{2,6},{3,7},{4,0},{5,1},{6,2},{7,3},{8,12},{9,13},{10,... | collective-permute-start | bytes 98312 | tf_op jit(solution)/shard_map/ppermute | solution.py:241
  6.8 10.2 %collective-permute-start.8 = (bf16[128,256]{1,0:T(8,128)(2,1)S(1)}, bf16[128,256]{1,0:T(8,128)(2,1)S(1)}, u32[]{:S(2)}, u32[]{:S(2)}) collective-permute-start(bf16[128,256]{1,0:T(8,128)(2,1)S(1)} %bitcast.25), channel_id=1, source_target_pairs={{0,24},{4,28},{8,16},{12,20},{16,8},{20,12},{24,0},{28,4},{1,25},{... | collective-permute-start | bytes 196616 | tf_op jit(solution)/shard_map/ppermute | solution.py:235
  9.6 7.5 %collective-permute-start.7 = (bf16[128,256]{1,0:T(8,128)(2,1)S(1)}, bf16[128,256]{1,0:T(8,128)(2,1)S(1)}, u32[]{:S(2)}, u32[]{:S(2)}) collective-permute-start(bf16[128,256]{1,0:T(8,128)(2,1)S(1)} %bitcast.26), channel_id=1, source_target_pairs={{0,20},{4,16},{8,28},{12,24},{16,4},{20,0},{24,12},{28,8},{1,21},{... | collective-permute-start | bytes 196616 | tf_op jit(solution)/shard_map/ppermute | solution.py:235
  10.5 6.6 %collective-permute-start.6 = (bf16[128,256]{1,0:T(8,128)(2,1)S(1)}, bf16[128,256]{1,0:T(8,128)(2,1)S(1)}, u32[]{:S(2)}, u32[]{:S(2)}) collective-permute-start(bf16[128,256]{1,0:T(8,128)(2,1)S(1)} %bitcast.27), channel_id=1, source_target_pairs={{0,12},{4,8},{8,4},{12,0},{16,28},{20,24},{24,20},{28,16},{1,13},{... | collective-permute-start | bytes 196616 | tf_op jit(solution)/shard_map/ppermute | solution.py:235
  11.9 1.4 %copy-start = (bf16[3,3,3,64,32]{3,4,2,1,0:T(8,128)(2,1)S(1)}, bf16[3,3,3,64,32]{3,4,2,1,0:T(8,128)(2,1)}, u32[]{:S(2)}) copy-start(bf16[3,3,3,64,32]{3,4,2,1,0:T(8,128)(2,1)} %param.5) | copy-start | bytes 331780
  12.0 1.3 %collective-permute-start.5 = (bf16[4,2,32,128]{3,2,1,0:T(8,128)(2,1)S(1)}, bf16[4,2,32,128]{3,2,1,0:T(8,128)(2,1)S(1)}, u32[]{:S(2)}, u32[]{:S(2)}) collective-permute-start(bf16[4,2,32,128]{3,2,1,0:T(8,128)(2,1)S(1)} %get-tuple-element.22), channel_id=1, source_target_pairs={{0,4},{4,0},{8,12},{12,8},{16,20},{20,16},{24,28},{28,24},{1,5},{5... | collective-permute-start | bytes 196616 | tf_op jit(solution)/shard_map/ppermute | solution.py:235
  12.2 3.7 %collective-permute-start.4 = (bf16[4,2,32,128]{3,2,1,0:T(8,128)(2,1)S(1)}, bf16[4,2,32,128]{3,2,1,0:T(8,128)(2,1)S(1)}, u32[]{:S(2)}, u32[]{:S(2)}) collective-permute-start(bf16[4,2,32,128]{3,2,1,0:T(8,128)(2,1)S(1)} %get-tuple-element.23), channel_id=1, source_target_pairs={{0,12},{8,20},{16,28},{24,4},{12,0},{20,8},{28,16},{4,24},{1,13},{... | collective-permute-start | bytes 196616 | tf_op jit(solution)/shard_map/ppermute | solution.py:270
  17.1 7.5 %copy-start.1 = (bf16[3,3,3,128,64]{3,4,2,1,0:T(8,128)(2,1)S(1)}, bf16[3,3,3,128,64]{3,4,2,1,0:T(8,128)(2,1)}, u32[]{:S(2)}) copy-start(bf16[3,3,3,128,64]{3,4,2,1,0:T(8,128)(2,1)} %param.6) | copy-start | bytes 1327108
  17.2 8.3 %collective-permute-start.9 = (bf16[4,128,256]{2,1,0:T(8,128)(2,1)S(1)}, bf16[4,128,256]{2,1,0:T(8,128)(2,1)S(1)}, u32[]{:S(2)}, u32[]{:S(2)}) collective-permute-start(bf16[4,128,256]{2,1,0:T(8,128)(2,1)S(1)} %pad_maximum_fusion.cot_ref), channel_id=1, source_target_pairs={{0,4},{4,0},{8,12},{12,8},{16,20},{20,16},{24,28},{28,24},{1,5},{5... | collective-permute-start | bytes 786440 | tf_op jit(solution)/shard_map/ppermute | solution.py:235
  18.7 4.9 %collective-permute-start.15 = (bf16[64,256]{1,0:T(8,128)(2,1)S(1)}, bf16[64,256]{1,0:T(8,128)(2,1)S(1)}, u32[]{:S(2)}, u32[]{:S(2)}) collective-permute-start(bf16[64,256]{1,0:T(8,128)(2,1)S(1)} %first_rest.1.refs_0_), channel_id=1, source_target_pairs={{0,24},{4,28},{8,16},{12,20},{16,8},{20,12},{24,0},{28,4},{1,25},{... | collective-permute-start | bytes 98312 | tf_op jit(solution)/shard_map/ppermute | solution.py:235
  20.1 3.9 %collective-permute-start.13 = (bf16[64,256]{1,0:T(8,128)(2,1)S(1)}, bf16[64,256]{1,0:T(8,128)(2,1)S(1)}, u32[]{:S(2)}, u32[]{:S(2)}) collective-permute-start(bf16[64,256]{1,0:T(8,128)(2,1)S(1)} %first_rest.1.refs_0_), channel_id=1, source_target_pairs={{0,20},{4,16},{8,28},{12,24},{16,4},{20,0},{24,12},{28,8},{1,21},{... | collective-permute-start | bytes 98312 | tf_op jit(solution)/shard_map/ppermute | solution.py:235
  20.9 3.4 %collective-permute-start.11 = (bf16[64,256]{1,0:T(8,128)(2,1)S(1)}, bf16[64,256]{1,0:T(8,128)(2,1)S(1)}, u32[]{:S(2)}, u32[]{:S(2)}) collective-permute-start(bf16[64,256]{1,0:T(8,128)(2,1)S(1)} %first_rest.1.refs_0_), channel_id=1, source_target_pairs={{0,12},{4,8},{8,4},{12,0},{16,28},{20,24},{24,20},{28,16},{1,13},{... | collective-permute-start | bytes 98312 | tf_op jit(solution)/shard_map/ppermute | solution.py:235
  21.9 2.9 %collective-permute-start.10 = (bf16[64,256]{1,0:T(8,128)(2,1)S(1)}, bf16[64,256]{1,0:T(8,128)(2,1)S(1)}, u32[]{:S(2)}, u32[]{:S(2)}) collective-permute-start(bf16[64,256]{1,0:T(8,128)(2,1)S(1)} %first_rest.1.refs_0_), channel_id=1, source_target_pairs={{0,4},{4,0},{8,12},{12,8},{16,20},{20,16},{24,28},{28,24},{1,5},{5... | collective-permute-start | bytes 98312 | tf_op jit(solution)/shard_map/ppermute | solution.py:235
  23.6 1.2 %collective-permute-start.16 = (bf16[64,256]{1,0:T(8,128)(2,1)S(1)}, bf16[64,256]{1,0:T(8,128)(2,1)S(1)}, u32[]{:S(2)}, u32[]{:S(2)}) collective-permute-start(bf16[64,256]{1,0:T(8,128)(2,1)S(1)} %collective-permute-done.15.refs_6_), channel_id=1, source_target_pairs={{0,4},{4,0},{8,12},{12,8},{16,20},{20,16},{24,28},{28,24},{1,5},{5... | collective-permute-start | bytes 98312 | tf_op jit(solution)/shard_map/ppermute | solution.py:235
  24.0 1.2 %collective-permute-start.14 = (bf16[64,256]{1,0:T(8,128)(2,1)S(1)}, bf16[64,256]{1,0:T(8,128)(2,1)S(1)}, u32[]{:S(2)}, u32[]{:S(2)}) collective-permute-start(bf16[64,256]{1,0:T(8,128)(2,1)S(1)} %collective-permute-done.13.refs_5_), channel_id=1, source_target_pairs={{0,4},{4,0},{8,12},{12,8},{16,20},{20,16},{24,28},{28,24},{1,5},{5... | collective-permute-start | bytes 98312 | tf_op jit(solution)/shard_map/ppermute | solution.py:235
  24.3 1.2 %collective-permute-start.12 = (bf16[64,256]{1,0:T(8,128)(2,1)S(1)}, bf16[64,256]{1,0:T(8,128)(2,1)S(1)}, u32[]{:S(2)}, u32[]{:S(2)}) collective-permute-start(bf16[64,256]{1,0:T(8,128)(2,1)S(1)} %collective-permute-done.11.refs_3_), channel_id=1, source_target_pairs={{0,4},{4,0},{8,12},{12,8},{16,20},{20,16},{24,28},{28,24},{1,5},{5... | collective-permute-start | bytes 98312 | tf_op jit(solution)/shard_map/ppermute | solution.py:235

commit v3 on v2

--- a/solution.py
+++ b/solution.py
@@ -81,6 +81,11 @@
 TN = (((0,), (0,)), ((), ()))
 
 
+def place():
+    role = lax.axis_index("space") ^ 1
+    return lax.axis_index("chan"), role & 1, (role > 0) & (role < lax.axis_size("space") - 1)
+
+
 def fill_patches(grid, moved, patches):
     planes, rows, cin, depth = grid.shape
     lane = lax.broadcasted_iota(jnp.int32, (rows * cin, depth), 1)
@@ -103,10 +108,10 @@
     return value / (1.0 + jnp.exp(-value))
 
 
-def first_part(chans, place_ref, w_ref, near_ref, *refs):
+def first_part(chans, w_ref, near_ref, *refs):
     blocks, (part_ref, sums_ref, grid, moved, patches) = refs[:chans], refs[-5:]
     planes, rows, cin, depth = grid.shape
-    mine, odd = place_ref[0], place_ref[1]
+    mine, odd, _ = place()
     edge = jnp.zeros((cin, depth), jnp.bfloat16)
     for plane in range(planes):
         grid[plane, 0] = edge
@@ -131,10 +136,10 @@
         )
 
 
-def first_rest(place_ref, w_ref, far_ref, part_ref, sums_ref, *refs):
+def first_rest(w_ref, far_ref, part_ref, sums_ref, *refs):
     out_ref, grid, moved, patches = refs[-4:]
     _, rows, cin, depth = grid.shape
-    mine, odd, has_far = place_ref[0], place_ref[1], place_ref[2] == 1
+    mine, odd, has_far = place()
     edge = jnp.zeros((cin, depth), jnp.bfloat16)
     grid[0, 0] = edge
     grid[0, rows - 1] = edge
@@ -162,13 +167,13 @@
         out_ref[:, pair // 2 * depth : (pair // 2 + 1) * depth] = halved.astype(jnp.bfloat16)
 
 
-def deep_kernel(rowlen, order, place_ref, w_ref, cot_ref, cot_swapped_ref, *refs):
+def deep_kernel(rowlen, order, w_ref, cot_ref, cot_swapped_ref, *refs):
     count = len(refs) - 7
     planes, refs = refs[:count], refs[count:]
     out_ref, grad_ref, held, cot, act, taps, shifted = refs
     cmid, cells = held.shape[1:]
     cout = cot.shape[1]
-    mine = place_ref[0]
+    mine = lax.axis_index("space")
     for k in range(count):
         held[mine ^ 1 ^ k] = planes[k][...]
     for k, bits in enumerate(order):
@@ -230,6 +235,10 @@
             grad_ref[at : at + half] = terms[:, a * cout : (a + 1) * cout]
 
 
+def after(event, *arrays):
+    return lax.optimization_barrier((event, *arrays))[1:]
+
+
 def swap(array, axis, bits):
     peers = lax.axis_size(axis)
     return lax.ppermute(array, axis, [(i, i ^ bits) for i in range(peers)])
@@ -241,8 +250,7 @@
     return lax.ppermute(array, ("space", "chan"), pairs)
 
 
-def spread(array, order):
-    direct = [swap(array, "space", bits) if bits else array for bits in order]
+def spread(direct, order):
     pieces = {}
     for bits, piece in zip(order, direct):
         pieces[bits], pieces[bits ^ 1] = piece, swap(piece, "space", 1)
@@ -254,12 +262,9 @@
     spaces, chans = lax.axis_size("space"), lax.axis_size("chan")
     cmid, cout, cells = weight_first.shape[3], weight_deep.shape[3], cotangent.shape[2]
     all_rows = chans * rows
-    at_space, at_chan = lax.axis_index("space"), lax.axis_index("chan")
-    role = at_space ^ 1
-    odd = role % 2
+    odd = (lax.axis_index("space") ^ 1) & 1
     order = [k | k.bit_count() % 2 for k in range(0, spaces, 2)]
-    vmem, smem = pl.BlockSpec(memory_space=pltpu.VMEM), pl.BlockSpec(memory_space=pltpu.SMEM)
-    unread = pl.BlockSpec(memory_space=pl.ANY)
+    vmem = pl.BlockSpec(memory_space=pltpu.VMEM)
 
     block = jnp.transpose(volume, (1, 2, 0, 3))
     blocks = [crossed(block, k) for k in range(chans)]
@@ -270,8 +275,6 @@
     far = lax.ppermute(
         jnp.where(odd == 1, last, first), "space", pairs + [(j, i) for i, j in pairs]
     )
-    has_far = ((role > 0) & (role < spaces - 1)).astype(jnp.int32)
-    place = jnp.stack([at_chan, odd, has_far])
 
     cots = [cotangent[:, 0]]
     cots = cots + [swap(cots[0], "space", bits) for bits in order[1:]]
@@ -292,30 +295,32 @@
             jax.ShapeDtypeStruct((cmid, all_rows * depth), jnp.float32),
             jax.ShapeDtypeStruct((cmid, all_rows * depth // 2), jnp.float32),
         ),
-        in_specs=[smem, vmem, vmem] + [vmem] * chans,
+        in_specs=[vmem] * (2 + chans) + [pl.BlockSpec(memory_space=pl.ANY)] * (len(order) - 1),
         out_specs=(vmem, vmem),
         scratch_shapes=patch_scratch(planes + 1),
         compiler_params=params,
         name="first_part",
         cost_estimate=pl.CostEstimate(flops=0, bytes_accessed=5000000, transcendentals=0),
-    )(place, taps_first, near, *blocks)
+    )(taps_first, near, *blocks, *cots[1:])
 
     pooled = pl.pallas_call(
         first_rest,
         out_shape=jax.ShapeDtypeStruct((cmid, cells), jnp.bfloat16),
-        in_specs=[smem, vmem, vmem, vmem, vmem],
+        in_specs=[vmem] * 4,
         out_specs=vmem,
         scratch_shapes=patch_scratch(1),
         compiler_params=params,
         name="first_rest",
         cost_estimate=pl.CostEstimate(flops=0, bytes_accessed=4000000, transcendentals=0),
-    )(place, taps_first, far, part, sums)
-
-    pooled, weight_deep, *cots = lax.optimization_barrier((pooled, weight_deep, *cots))
+    )(taps_first, far, part, sums)
+
+    direct = [pooled] + [swap(pooled, "space", bits) for bits in order[1:]]
+    (weight_deep,) = after(pooled, weight_deep)
     taps_deep = jnp.transpose(weight_deep, (3, 0, 1, 2, 4)).reshape(cout, 27 * cmid)
+    cots = after(pooled, *cots)
     cots = jnp.stack(cots)
     cots_swapped = swap(cots, "space", 1)
-    all_pooled = spread(pooled, order)
+    all_pooled = spread(direct, order)
 
     deep_out, terms = pl.pallas_call(
         functools.partial(deep_kernel, depth // 2, order),
@@ -323,7 +328,7 @@
             jax.ShapeDtypeStruct((cout, cells), jnp.bfloat16),
             jax.ShapeDtypeStruct((27 * cmid, cout), jnp.float32),
         ),
-        in_specs=[smem] + [vmem] * (3 + spaces),
+        in_specs=[vmem] * (3 + spaces),
         out_specs=(vmem, vmem),
         scratch_shapes=[
             pltpu.VMEM((spaces, cmid, cells), jnp.bfloat16),
@@ -335,7 +340,7 @@
         compiler_params=params,
         name="deep",
         cost_estimate=pl.CostEstimate(flops=0, bytes_accessed=12000000, transcendentals=0),
-    )(at_space.reshape(1), taps_deep, cots, cots_swapped, *all_pooled)
+    )(taps_deep, cots, cots_swapped, *all_pooled)
 
     grad = jnp.transpose(terms.reshape(3, 3, 3, cmid, cout), (0, 1, 2, 4, 3))
     return deep_out[:, None], grad

time: 29.1 us -> 28.5 us (0.979)
  Pallas kernels: 5.93 us -> 4.86 us
  waiting for transfers between devices: 5.38 us -> 5.98 us
    ppermute x12, waiting for transfers between devices: 3.33 us -> 4.45 us  [swap(): return lax.ppermute(array, axis, [(i, i ^ bits) for i in range(peers)])]
    pallas_call x1, Pallas kernels: 1.36 us -> 0.82 us  [by_gather(): pl.pallas_call(functools.partial(first_part, chans), out_shape=(jax.Shape...]
    pallas_call x1, Pallas kernels: 1.15 us -> 0.61 us  [by_gather(): pl.pallas_call(first_rest, out_shape=jax.ShapeDtypeStruct((cmid, cells),...]
    ppermute x1, waiting for transfers between devices: 1.22 us -> 0.7 us  [by_gather(): lax.ppermute(jnp.where(odd == 1, last, first), 'space', pairs + [(j, i) f...]
  transfers between devices with their start and end apart: 17 -> 17, of which waited for: 8 -> 9; matrix products, arithmetic and copies ran while one was open for 1% -> 1% of each run, Pallas kernels for 9% -> 3%
where the time goes in v3:
time: 28.5 us; the launch traced here: 28.4 us
  starting transfers between devices  15.7 us (55%)
  waiting for transfers between devices  5.98 us (21%)
  Pallas kernels  4.86 us (17%)
  local copies, waits for them, and re-layouts  1.04 us (4%)
  between operations  0.73 us (3%)
    ppermute x12, starting transfers between devices, swap(): return lax.ppermute(array, axis, [(i, i ^ bits) for i in range(peers)])  9.78 us
    ppermute x4, starting transfers between devices, crossed(): return lax.ppermute(array, ('space', 'chan'), pairs)  5.41 us
    ppermute x12, waiting for transfers between devices, swap(): return lax.ppermute(array, axis, [(i, i ^ bits) for i in range(peers)])  4.45 us
    pallas_call x1, Pallas kernels, by_gather(): pl.pallas_call(functools.partial(deep_kernel, depth // 2, order), out_sha...  3.43 us
    ppermute x4, waiting for transfers between devices, crossed(): return lax.ppermute(array, ('space', 'chan'), pairs)  0.83 us
    pallas_call x1, Pallas kernels, by_gather(): pl.pallas_call(functools.partial(first_part, chans), out_shape=(jax.Shape...  0.82 us
    unnamed x7, local copies, waits for them, and re-layouts  0.81 us
    ppermute x1, waiting for transfers between devices, by_gather(): lax.ppermute(jnp.where(odd == 1, last, first), 'space', pairs + [(j, i) f...  0.7 us
  transfers between devices with their start and end apart: 17, of which 9 were waited for; matrix products, arithmetic and copies ran while one was open for 1% of the time, Pallas kernels for 3%

profile of v3, /device:TPU:0, one launch (start us, length us, event | category | flops | bytes accessed | tf_op | source)
XLA Modules:
  0.0 28.4 jit_solution(4640757229534982106)
XLA Ops:
  0.6 0.8 %copy.11 = bf16[32,2,2,128]{3,0,2,1:T(8,128)(2,1)S(1)} copy(bf16[32,2,2,128]{3,2,1,0:T(2,128)(2,1)} %param.4) | data formatting | bytes 65536 | tf_op args[0]
  1.4 4.5 %collective-permute-start.3 = (bf16[2,2,32,128]{3,2,1,0:T(8,128)(2,1)S(1)}, bf16[2,2,32,128]{3,2,1,0:T(8,128)(2,1)S(1)}, u32[]{:S(2)}, u32[]{:S(2)}) collective-permute-start(bf16[2,2,32,128]{3,2,1,0:T(8,128)(2,1)S(1)} %bitcast.28), channel_id=1, source_target_pairs={{0,7},{1,6},{2,5},{3,4},{4,3},{5,2},{6,1},{7,0},{8,15},{9,14},{10,... | collective-permute-start | bytes 98312 | tf_op jit(solution)/shard_map/ppermute | solution.py:250
  5.9 0.0 collective-permute-start.2
  5.9 0.9 %collective-permute-start.1 = (bf16[2,2,32,128]{3,2,1,0:T(8,128)(2,1)S(1)}, bf16[2,2,32,128]{3,2,1,0:T(8,128)(2,1)S(1)}, u32[]{:S(2)}, u32[]{:S(2)}) collective-permute-start(bf16[2,2,32,128]{3,2,1,0:T(8,128)(2,1)S(1)} %bitcast.30), channel_id=1, source_target_pairs={{0,5},{1,4},{2,7},{3,6},{4,1},{5,0},{6,3},{7,2},{8,13},{9,12},{10,... | collective-permute-start | bytes 98312 | tf_op jit(solution)/shard_map/ppermute | solution.py:250
  6.8 2.7 %collective-permute-start.8 = (bf16[128,256]{1,0:T(8,128)(2,1)S(1)}, bf16[128,256]{1,0:T(8,128)(2,1)S(1)}, u32[]{:S(2)}, u32[]{:S(2)}) collective-permute-start(bf16[128,256]{1,0:T(8,128)(2,1)S(1)} %bitcast.24), channel_id=1, source_target_pairs={{0,24},{4,28},{8,16},{12,20},{16,8},{20,12},{24,0},{28,4},{1,25},{... | collective-permute-start | bytes 196616 | tf_op jit(solution)/shard_map/ppermute | solution.py:244
  9.6 0.0 collective-permute-done.3.refs_3_
  9.6 0.1 collective-permute-start.7
  9.6 0.8 %collective-permute-done.2.refs_2_ = bf16[2,2,32,128]{3,2,1,0:T(8,128)(2,1)S(1)} collective-permute-done((bf16[2,2,32,128]{3,2,1,0:T(8,128)(2,1)S(1)}, bf16[2,2,32,128]{3,2,1,0:T(8,128)(2,1)S(1)}, u32[]{:S(2)}, u32[]{:S(2)}) %collective-permute-start.2) | collective-permute-done | bytes 32800 | tf_op jit(solution)/shard_map/ppermute | solution.py:250
  10.5 1.5 %collective-permute-start.6 = (bf16[128,256]{1,0:T(8,128)(2,1)S(1)}, bf16[128,256]{1,0:T(8,128)(2,1)S(1)}, u32[]{:S(2)}, u32[]{:S(2)}) collective-permute-start(bf16[128,256]{1,0:T(8,128)(2,1)S(1)} %bitcast.26), channel_id=1, source_target_pairs={{0,12},{4,8},{8,4},{12,0},{16,28},{20,24},{24,20},{28,16},{1,13},{... | collective-permute-start | bytes 196616 | tf_op jit(solution)/shard_map/ppermute | solution.py:244
  12.0 0.2 collective-permute-start.5
  12.2 0.5 %collective-permute-start.4 = (bf16[4,2,32,128]{3,2,1,0:T(8,128)(2,1)S(1)}, bf16[4,2,32,128]{3,2,1,0:T(8,128)(2,1)S(1)}, u32[]{:S(2)}, u32[]{:S(2)}) collective-permute-start(bf16[4,2,32,128]{3,2,1,0:T(8,128)(2,1)S(1)} %get-tuple-element.21), channel_id=1, source_target_pairs={{0,12},{8,20},{16,28},{24,4},{12,0},{20,8},{28,16},{4,24},{1,13},{... | collective-permute-start | bytes 196616 | tf_op jit(solution)/shard_map/ppermute | solution.py:275
  12.7 1.1 %collective-permute-done.7.refs_5_ = bf16[128,256]{1,0:T(8,128)(2,1)S(1)} collective-permute-done((bf16[128,256]{1,0:T(8,128)(2,1)S(1)}, bf16[128,256]{1,0:T(8,128)(2,1)S(1)}, u32[]{:S(2)}, u32[]{:S(2)}) %collective-permute-start.7) | collective-permute-done | bytes 65568 | tf_op jit(solution)/shard_map/ppermute | solution.py:244
  13.8 0.6 %collective-permute-done.6.refs_4_ = bf16[128,256]{1,0:T(8,128)(2,1)S(1)} collective-permute-done((bf16[128,256]{1,0:T(8,128)(2,1)S(1)}, bf16[128,256]{1,0:T(8,128)(2,1)S(1)}, u32[]{:S(2)}, u32[]{:S(2)}) %collective-permute-start.6) | collective-permute-done | bytes 65568 | tf_op jit(solution)/shard_map/ppermute | solution.py:244
  14.4 0.0 collective-permute-done.5.near_ref
  14.4 0.8 %first_part.1 = (f32[64,1024]{1,0:T(8,128)S(1)}, f32[64,512]{1,0:T(8,128)S(1)}) custom-call(bf16[3,288,64]{2,1,0:T(8,128)(2,1)S(1)} %bitcast.18, bf16[4,2,32,128]{3,2,1,0:T(8,128)(2,1)S(1)} %collective-permute-done.5.near_ref, bf16[2,2,32,128]{3,2,1,0:T(8,128)(2,1)S(1)} %collective-permute-done.refs_0_, ...), custom_call_target="tpu_custom_call" | custom-call | bytes 5000000 | tf_op jit(solution)/shard_map/first_part/pallas_call | solution.py:292
  15.2 0.7 %collective-permute-done.4.far_ref = bf16[4,2,32,128]{3,2,1,0:T(8,128)(2,1)S(1)} collective-permute-done((bf16[4,2,32,128]{3,2,1,0:T(8,128)(2,1)S(1)}, bf16[4,2,32,128]{3,2,1,0:T(8,128)(2,1)S(1)}, u32[]{:S(2)}, u32[]{:S(2)}) %collective-permute-start.4) | collective-permute-done | bytes 65568 | tf_op jit(solution)/shard_map/ppermute | solution.py:275
  15.9 0.6 %first_rest.1.refs_0_ = bf16[64,256]{1,0:T(8,128)(2,1)S(1)} custom-call(bf16[3,288,64]{2,1,0:T(8,128)(2,1)S(1)} %bitcast.19, bf16[4,2,32,128]{3,2,1,0:T(8,128)(2,1)S(1)} %collective-permute-done.4.far_ref, f32[64,1024]{1,0:T(8,128)S(1)} %get-tuple-element.11.part_ref, f32[64,512]{1,0:T(8,128)S(1)} %get-tuple-element.12.sums_ref), custom_call_target="tpu_custom_call" | custom-call | bytes 4000000 | tf_op jit(solution)/shard_map/first_rest/pallas_call | solution.py:306
  16.5 0.0 copy-start.1
  16.6 1.5 %collective-permute-start.9 = (bf16[4,128,256]{2,1,0:T(8,128)(2,1)S(1)}, bf16[4,128,256]{2,1,0:T(8,128)(2,1)S(1)}, u32[]{:S(2)}, u32[]{:S(2)}) collective-permute-start(bf16[4,128,256]{2,1,0:T(8,128)(2,1)S(1)} %pad_maximum_fusion.cot_ref), channel_id=1, source_target_pairs={{0,4},{4,0},{8,12},{12,8},{16,20},{20,16},{24,28},{28,24},{1,5},{5... | collective-permute-start | bytes 786440 | tf_op jit(solution)/shard_map/ppermute | solution.py:244
  18.1 1.4 %collective-permute-start.15 = (bf16[64,256]{1,0:T(8,128)(2,1)S(1)}, bf16[64,256]{1,0:T(8,128)(2,1)S(1)}, u32[]{:S(2)}, u32[]{:S(2)}) collective-permute-start(bf16[64,256]{1,0:T(8,128)(2,1)S(1)} %first_rest.1.refs_0_), channel_id=1, source_target_pairs={{0,24},{4,28},{8,16},{12,20},{16,8},{20,12},{24,0},{28,4},{1,25},{... | collective-permute-start | bytes 98312 | tf_op jit(solution)/shard_map/ppermute | solution.py:244
  19.6 0.7 %collective-permute-start.13 = (bf16[64,256]{1,0:T(8,128)(2,1)S(1)}, bf16[64,256]{1,0:T(8,128)(2,1)S(1)}, u32[]{:S(2)}, u32[]{:S(2)}) collective-permute-start(bf16[64,256]{1,0:T(8,128)(2,1)S(1)} %first_rest.1.refs_0_), channel_id=1, source_target_pairs={{0,20},{4,16},{8,28},{12,24},{16,4},{20,0},{24,12},{28,8},{1,21},{... | collective-permute-start | bytes 98312 | tf_op jit(solution)/shard_map/ppermute | solution.py:244
  20.3 1.1 %collective-permute-start.11 = (bf16[64,256]{1,0:T(8,128)(2,1)S(1)}, bf16[64,256]{1,0:T(8,128)(2,1)S(1)}, u32[]{:S(2)}, u32[]{:S(2)}) collective-permute-start(bf16[64,256]{1,0:T(8,128)(2,1)S(1)} %first_rest.1.refs_0_), channel_id=1, source_target_pairs={{0,12},{4,8},{8,4},{12,0},{16,28},{20,24},{24,20},{28,16},{1,13},{... | collective-permute-start | bytes 98312 | tf_op jit(solution)/shard_map/ppermute | solution.py:244
  21.4 0.0 collective-permute-start.10
  21.4 1.7 %collective-permute-done.15.refs_6_ = bf16[64,256]{1,0:T(8,128)(2,1)S(1)} collective-permute-done((bf16[64,256]{1,0:T(8,128)(2,1)S(1)}, bf16[64,256]{1,0:T(8,128)(2,1)S(1)}, u32[]{:S(2)}, u32[]{:S(2)}) %collective-permute-start.15) | collective-permute-done | bytes 32800 | tf_op jit(solution)/shard_map/ppermute | solution.py:244
  23.1 0.4 %collective-permute-done.13.refs_5_ = bf16[64,256]{1,0:T(8,128)(2,1)S(1)} collective-permute-done((bf16[64,256]{1,0:T(8,128)(2,1)S(1)}, bf16[64,256]{1,0:T(8,128)(2,1)S(1)}, u32[]{:S(2)}, u32[]{:S(2)}) %collective-permute-start.13) | collective-permute-done | bytes 32800 | tf_op jit(solution)/shard_map/ppermute | solution.py:244
  23.4 0.3 collective-permute-start.14
  23.7 0.3 collective-permute-start.12
  24.0 0.2 copy.9.w_ref
  24.2 0.1 collective-permute-done.16.refs_7_
  24.3 0.4 %collective-permute-done.14.refs_4_ = bf16[64,256]{1,0:T(8,128)(2,1)S(1)} collective-permute-done((bf16[64,256]{1,0:T(8,128)(2,1)S(1)}, bf16[64,256]{1,0:T(8,128)(2,1)S(1)}, u32[]{:S(2)}, u32[]{:S(2)}) %collective-permute-start.14) | collective-permute-done | bytes 32800 | tf_op jit(solution)/shard_map/ppermute | solution.py:244
  24.6 0.3 %collective-permute-done.12.refs_2_ = bf16[64,256]{1,0:T(8,128)(2,1)S(1)} collective-permute-done((bf16[64,256]{1,0:T(8,128)(2,1)S(1)}, bf16[64,256]{1,0:T(8,128)(2,1)S(1)}, u32[]{:S(2)}, u32[]{:S(2)}) %collective-permute-start.12) | collective-permute-done | bytes 32800 | tf_op jit(solution)/shard_map/ppermute | solution.py:244
  24.9 3.4 %deep.1 = (bf16[128,256]{1,0:T(8,128)(2,1)}, f32[1728,128]{1,0:T(8,128)}) custom-call(bf16[128,1728]{1,0:T(8,128)(2,1)S(1)} %copy.9.w_ref, bf16[4,128,256]{2,1,0:T(8,128)(2,1)S(1)} %pad_maximum_fusion.cot_ref, bf16[4,128,256]{2,1,0:T(8,128)(2,1)S(1)} %collective-permute-done.9.cot_swapped_ref, bf16[64,256]{1,0:T(8,128)(2,1)S(1)} %first_rest.1.refs_0_, ...), custom_call_target="tpu_custom_call" | custom-call | bytes 12000000 | tf_op jit(solution)/shard_map/deep/pallas_call | solution.py:325
  (19 shorter events, 0.1 us)
Async XLA Ops:
  0.6 6.2 %copy-start.2 = (bf16[128,1,256]{2,0,1:T(8,128)(2,1)S(1)}, bf16[128,1,256]{2,0,1:T(8,128)(2,1)}, u32[]{:S(2)}) copy-start(bf16[128,1,256]{2,0,1:T(8,128)(2,1)} %param.7) | copy-start | bytes 196612
  1.4 8.1 %collective-permute-start.3 = (bf16[2,2,32,128]{3,2,1,0:T(8,128)(2,1)S(1)}, bf16[2,2,32,128]{3,2,1,0:T(8,128)(2,1)S(1)}, u32[]{:S(2)}, u32[]{:S(2)}) collective-permute-start(bf16[2,2,32,128]{3,2,1,0:T(8,128)(2,1)S(1)} %bitcast.28), channel_id=1, source_target_pairs={{0,7},{1,6},{2,5},{3,4},{4,3},{5,2},{6,1},{7,0},{8,15},{9,14},{10,... | collective-permute-start | bytes 98312 | tf_op jit(solution)/shard_map/ppermute | solution.py:250
  5.9 4.5 %collective-permute-start.2 = (bf16[2,2,32,128]{3,2,1,0:T(8,128)(2,1)S(1)}, bf16[2,2,32,128]{3,2,1,0:T(8,128)(2,1)S(1)}, u32[]{:S(2)}, u32[]{:S(2)}) collective-permute-start(bf16[2,2,32,128]{3,2,1,0:T(8,128)(2,1)S(1)} %bitcast.29), channel_id=1, source_target_pairs={{0,6},{1,7},{2,4},{3,5},{4,2},{5,3},{6,0},{7,1},{8,14},{9,15},{10,... | collective-permute-start | bytes 98312 | tf_op jit(solution)/shard_map/ppermute | solution.py:250
  5.9 6.0 %collective-permute-start.1 = (bf16[2,2,32,128]{3,2,1,0:T(8,128)(2,1)S(1)}, bf16[2,2,32,128]{3,2,1,0:T(8,128)(2,1)S(1)}, u32[]{:S(2)}, u32[]{:S(2)}) collective-permute-start(bf16[2,2,32,128]{3,2,1,0:T(8,128)(2,1)S(1)} %bitcast.30), channel_id=1, source_target_pairs={{0,5},{1,4},{2,7},{3,6},{4,1},{5,0},{6,3},{7,2},{8,13},{9,12},{10,... | collective-permute-start | bytes 98312 | tf_op jit(solution)/shard_map/ppermute | solution.py:250
  6.8 5.1 %collective-permute-start = (bf16[2,2,32,128]{3,2,1,0:T(8,128)(2,1)S(1)}, bf16[2,2,32,128]{3,2,1,0:T(8,128)(2,1)S(1)}, u32[]{:S(2)}, u32[]{:S(2)}) collective-permute-start(bf16[2,2,32,128]{3,2,1,0:T(8,128)(2,1)S(1)} %bitcast.31), channel_id=1, source_target_pairs={{0,4},{1,5},{2,6},{3,7},{4,0},{5,1},{6,2},{7,3},{8,12},{9,13},{10,... | collective-permute-start | bytes 98312 | tf_op jit(solution)/shard_map/ppermute | solution.py:250
  6.8 5.9 %collective-permute-start.8 = (bf16[128,256]{1,0:T(8,128)(2,1)S(1)}, bf16[128,256]{1,0:T(8,128)(2,1)S(1)}, u32[]{:S(2)}, u32[]{:S(2)}) collective-permute-start(bf16[128,256]{1,0:T(8,128)(2,1)S(1)} %bitcast.24), channel_id=1, source_target_pairs={{0,24},{4,28},{8,16},{12,20},{16,8},{20,12},{24,0},{28,4},{1,25},{... | collective-permute-start | bytes 196616 | tf_op jit(solution)/shard_map/ppermute | solution.py:244
  9.6 4.3 %collective-permute-start.7 = (bf16[128,256]{1,0:T(8,128)(2,1)S(1)}, bf16[128,256]{1,0:T(8,128)(2,1)S(1)}, u32[]{:S(2)}, u32[]{:S(2)}) collective-permute-start(bf16[128,256]{1,0:T(8,128)(2,1)S(1)} %bitcast.25), channel_id=1, source_target_pairs={{0,20},{4,16},{8,28},{12,24},{16,4},{20,0},{24,12},{28,8},{1,21},{... | collective-permute-start | bytes 196616 | tf_op jit(solution)/shard_map/ppermute | solution.py:244
  10.5 3.9 %collective-permute-start.6 = (bf16[128,256]{1,0:T(8,128)(2,1)S(1)}, bf16[128,256]{1,0:T(8,128)(2,1)S(1)}, u32[]{:S(2)}, u32[]{:S(2)}) collective-permute-start(bf16[128,256]{1,0:T(8,128)(2,1)S(1)} %bitcast.26), channel_id=1, source_target_pairs={{0,12},{4,8},{8,4},{12,0},{16,28},{20,24},{24,20},{28,16},{1,13},{... | collective-permute-start | bytes 196616 | tf_op jit(solution)/shard_map/ppermute | solution.py:244
  11.9 2.5 %copy-start = (bf16[3,3,3,64,32]{3,4,2,1,0:T(8,128)(2,1)S(1)}, bf16[3,3,3,64,32]{3,4,2,1,0:T(8,128)(2,1)}, u32[]{:S(2)}) copy-start(bf16[3,3,3,64,32]{3,4,2,1,0:T(8,128)(2,1)} %param.5) | copy-start | bytes 331780
  12.0 2.4 %collective-permute-start.5 = (bf16[4,2,32,128]{3,2,1,0:T(8,128)(2,1)S(1)}, bf16[4,2,32,128]{3,2,1,0:T(8,128)(2,1)S(1)}, u32[]{:S(2)}, u32[]{:S(2)}) collective-permute-start(bf16[4,2,32,128]{3,2,1,0:T(8,128)(2,1)S(1)} %get-tuple-element.20), channel_id=1, source_target_pairs={{0,4},{4,0},{8,12},{12,8},{16,20},{20,16},{24,28},{28,24},{1,5},{5... | collective-permute-start | bytes 196616 | tf_op jit(solution)/shard_map/ppermute | solution.py:244
  12.2 3.7 %collective-permute-start.4 = (bf16[4,2,32,128]{3,2,1,0:T(8,128)(2,1)S(1)}, bf16[4,2,32,128]{3,2,1,0:T(8,128)(2,1)S(1)}, u32[]{:S(2)}, u32[]{:S(2)}) collective-permute-start(bf16[4,2,32,128]{3,2,1,0:T(8,128)(2,1)S(1)} %get-tuple-element.21), channel_id=1, source_target_pairs={{0,12},{8,20},{16,28},{24,4},{12,0},{20,8},{28,16},{4,24},{1,13},{... | collective-permute-start | bytes 196616 | tf_op jit(solution)/shard_map/ppermute | solution.py:275
  16.5 7.4 %copy-start.1 = (bf16[3,3,3,128,64]{3,4,2,1,0:T(8,128)(2,1)S(1)}, bf16[3,3,3,128,64]{3,4,2,1,0:T(8,128)(2,1)}, u32[]{:S(2)}) copy-start(bf16[3,3,3,128,64]{3,4,2,1,0:T(8,128)(2,1)} %param.6) | copy-start | bytes 1327108
  16.6 8.3 %collective-permute-start.9 = (bf16[4,128,256]{2,1,0:T(8,128)(2,1)S(1)}, bf16[4,128,256]{2,1,0:T(8,128)(2,1)S(1)}, u32[]{:S(2)}, u32[]{:S(2)}) collective-permute-start(bf16[4,128,256]{2,1,0:T(8,128)(2,1)S(1)} %pad_maximum_fusion.cot_ref), channel_id=1, source_target_pairs={{0,4},{4,0},{8,12},{12,8},{16,20},{20,16},{24,28},{28,24},{1,5},{5... | collective-permute-start | bytes 786440 | tf_op jit(solution)/shard_map/ppermute | solution.py:244
  18.1 4.9 %collective-permute-start.15 = (bf16[64,256]{1,0:T(8,128)(2,1)S(1)}, bf16[64,256]{1,0:T(8,128)(2,1)S(1)}, u32[]{:S(2)}, u32[]{:S(2)}) collective-permute-start(bf16[64,256]{1,0:T(8,128)(2,1)S(1)} %first_rest.1.refs_0_), channel_id=1, source_target_pairs={{0,24},{4,28},{8,16},{12,20},{16,8},{20,12},{24,0},{28,4},{1,25},{... | collective-permute-start | bytes 98312 | tf_op jit(solution)/shard_map/ppermute | solution.py:244
  19.6 3.9 %collective-permute-start.13 = (bf16[64,256]{1,0:T(8,128)(2,1)S(1)}, bf16[64,256]{1,0:T(8,128)(2,1)S(1)}, u32[]{:S(2)}, u32[]{:S(2)}) collective-permute-start(bf16[64,256]{1,0:T(8,128)(2,1)S(1)} %first_rest.1.refs_0_), channel_id=1, source_target_pairs={{0,20},{4,16},{8,28},{12,24},{16,4},{20,0},{24,12},{28,8},{1,21},{... | collective-permute-start | bytes 98312 | tf_op jit(solution)/shard_map/ppermute | solution.py:244
  20.3 3.4 %collective-permute-start.11 = (bf16[64,256]{1,0:T(8,128)(2,1)S(1)}, bf16[64,256]{1,0:T(8,128)(2,1)S(1)}, u32[]{:S(2)}, u32[]{:S(2)}) collective-permute-start(bf16[64,256]{1,0:T(8,128)(2,1)S(1)} %first_rest.1.refs_0_), channel_id=1, source_target_pairs={{0,12},{4,8},{8,4},{12,0},{16,28},{20,24},{24,20},{28,16},{1,13},{... | collective-permute-start | bytes 98312 | tf_op jit(solution)/shard_map/ppermute | solution.py:244
  21.4 2.9 %collective-permute-start.10 = (bf16[64,256]{1,0:T(8,128)(2,1)S(1)}, bf16[64,256]{1,0:T(8,128)(2,1)S(1)}, u32[]{:S(2)}, u32[]{:S(2)}) collective-permute-start(bf16[64,256]{1,0:T(8,128)(2,1)S(1)} %first_rest.1.refs_0_), channel_id=1, source_target_pairs={{0,4},{4,0},{8,12},{12,8},{16,20},{20,16},{24,28},{28,24},{1,5},{5... | collective-permute-start | bytes 98312 | tf_op jit(solution)/shard_map/ppermute | solution.py:244
  23.1 1.2 %collective-permute-start.16 = (bf16[64,256]{1,0:T(8,128)(2,1)S(1)}, bf16[64,256]{1,0:T(8,128)(2,1)S(1)}, u32[]{:S(2)}, u32[]{:S(2)}) collective-permute-start(bf16[64,256]{1,0:T(8,128)(2,1)S(1)} %collective-permute-done.15.refs_6_), channel_id=1, source_target_pairs={{0,4},{4,0},{8,12},{12,8},{16,20},{20,16},{24,28},{28,24},{1,5},{5... | collective-permute-start | bytes 98312 | tf_op jit(solution)/shard_map/ppermute | solution.py:244
  23.4 1.2 %collective-permute-start.14 = (bf16[64,256]{1,0:T(8,128)(2,1)S(1)}, bf16[64,256]{1,0:T(8,128)(2,1)S(1)}, u32[]{:S(2)}, u32[]{:S(2)}) collective-permute-start(bf16[64,256]{1,0:T(8,128)(2,1)S(1)} %collective-permute-done.13.refs_5_), channel_id=1, source_target_pairs={{0,4},{4,0},{8,12},{12,8},{16,20},{20,16},{24,28},{28,24},{1,5},{5... | collective-permute-start | bytes 98312 | tf_op jit(solution)/shard_map/ppermute | solution.py:244
  23.7 1.2 %collective-permute-start.12 = (bf16[64,256]{1,0:T(8,128)(2,1)S(1)}, bf16[64,256]{1,0:T(8,128)(2,1)S(1)}, u32[]{:S(2)}, u32[]{:S(2)}) collective-permute-start(bf16[64,256]{1,0:T(8,128)(2,1)S(1)} %collective-permute-done.11.refs_3_), channel_id=1, source_target_pairs={{0,4},{4,0},{8,12},{12,8},{16,20},{20,16},{24,28},{28,24},{1,5},{5... | collective-permute-start | bytes 98312 | tf_op jit(solution)/shard_map/ppermute | solution.py:244

commit v4 on v3

--- a/solution.py
+++ b/solution.py
@@ -4,6 +4,7 @@
 import jax.numpy as jnp
 from jax import lax
 from jax.experimental import pallas as pl
+from jax.experimental.layout import Layout, with_layout_constraint
 from jax.experimental.pallas import tpu as pltpu
 from jax.sharding import PartitionSpec as P
 
@@ -104,6 +105,12 @@
                     patches[at : at + cin, row * depth : (row + 1) * depth] = block
 
 
+def place_rows(grid, plane, owner, rows):
+    rows = jnp.swapaxes(rows, 0, 1)
+    for row in range(rows.shape[0]):
+        grid[plane, 1 + owner * rows.shape[0] + row] = rows[row]
+
+
 def silu(value):
     return value / (1.0 + jnp.exp(-value))
 
@@ -117,12 +124,9 @@
         grid[plane, 0] = edge
         grid[plane, rows - 1] = edge
     for k in range(chans):
-        per = near_ref.shape[1]
-        start = 1 + (mine ^ k) * per
-        for row in range(per):
-            grid[0, start + row] = blocks[k][odd, row]
-            grid[1, start + row] = blocks[k][1 - odd, row]
-            grid[2, start + row] = near_ref[k, row]
+        place_rows(grid, 0, mine ^ k, blocks[k][:, odd])
+        place_rows(grid, 1, mine ^ k, blocks[k][:, 1 - odd])
+        place_rows(grid, 2, mine ^ k, near_ref[chans - 1 - k])
     fill_patches(grid, moved, patches)
     to_far, centre, from_far = w_ref[2 * odd], w_ref[1], w_ref[2 - 2 * odd]
     inner = jnp.concatenate([to_far, centre, from_far], axis=0)
@@ -143,10 +147,9 @@
     edge = jnp.zeros((cin, depth), jnp.bfloat16)
     grid[0, 0] = edge
     grid[0, rows - 1] = edge
-    per = far_ref.shape[1]
     for k in range(far_ref.shape[0]):
-        for row in range(per):
-            grid[0, 1 + (mine ^ k) * per + row] = jnp.where(has_far, far_ref[k, row], edge)
+        rows_k = far_ref[far_ref.shape[0] - 1 - k]
+        place_rows(grid, 0, mine ^ k, jnp.where(has_far, rows_k, jnp.zeros_like(rows_k)))
     fill_patches(grid, moved, patches)
     to_far = w_ref[2 * odd]
     sums = []
@@ -263,13 +266,13 @@
     cmid, cout, cells = weight_first.shape[3], weight_deep.shape[3], cotangent.shape[2]
     all_rows = chans * rows
     odd = (lax.axis_index("space") ^ 1) & 1
-    order = [k | k.bit_count() % 2 for k in range(0, spaces, 2)]
+    order = [0] + [k | 1 for k in range(2, spaces, 2)]
     vmem = pl.BlockSpec(memory_space=pltpu.VMEM)
 
-    block = jnp.transpose(volume, (1, 2, 0, 3))
-    blocks = [crossed(block, k) for k in range(chans)]
-    first = jnp.stack([piece[0] for piece in blocks])
-    last = jnp.stack([piece[planes - 1] for piece in blocks])
+    as_given = Layout(major_to_minor=(0, 1, 2, 3))
+    blocks = [with_layout_constraint(crossed(volume, k), as_given) for k in range(chans)[::-1]][::-1]
+    first = jnp.stack([piece[:, 0] for piece in blocks[::-1]])
+    last = jnp.stack([piece[:, planes - 1] for piece in blocks[::-1]])
     near = swap(jnp.where(odd == 1, first, last), "space", 1)
     pairs = [(i ^ 1, ((i + 1) % spaces) ^ 1) for i in range(1, spaces, 2)]
     far = lax.ppermute(

time: 28.5 us -> 28.3 us (level)
  local copies, waits for them, and re-layouts: 1.04 us -> 0.33 us
  waiting for transfers between devices: 5.98 us -> 5.34 us
  starting transfers between devices: 15.7 us -> 16.3 us
    ppermute x12, waiting for transfers between devices: 4.45 us -> 3.1 us  [swap(): return lax.ppermute(array, axis, [(i, i ^ bits) for i in range(peers)])]
    unnamed x7 -> x6, local copies, waits for them, and re-layouts: 0.81 us -> 0.02 us
    ppermute x1, waiting for transfers between devices: 0.7 us -> 1.35 us  [by_gather(): lax.ppermute(jnp.where(odd == 1, last, first), 'space', pairs + [(j, i) f...]
    ppermute x12, starting transfers between devices: 9.78 us -> 10.2 us  [swap(): return lax.ppermute(array, axis, [(i, i ^ bits) for i in range(peers)])]
  transfers between devices with their start and end apart: 17 -> 17, of which waited for: 9 -> 8; matrix products, arithmetic and copies ran while one was open for 1% -> 2% of each run, Pallas kernels for 3% -> 3%
where the time goes in v4:
time: 28.3 us; the launch traced here: 28.1 us
  starting transfers between devices  16.3 us (58%)
  waiting for transfers between devices  5.34 us (19%)
  Pallas kernels  5.08 us (18%)
  between operations  0.77 us (3%)
  local copies, waits for them, and re-layouts  0.33 us (1%)
  other arithmetic  0.33 us (1%)
    ppermute x12, starting transfers between devices, swap(): return lax.ppermute(array, axis, [(i, i ^ bits) for i in range(peers)])  10.2 us
    ppermute x4, starting transfers between devices, crossed(): return lax.ppermute(array, ('space', 'chan'), pairs)  5.4 us
    pallas_call x1, Pallas kernels, by_gather(): pl.pallas_call(functools.partial(deep_kernel, depth // 2, order), out_sha...  3.43 us
    ppermute x12, waiting for transfers between devices, swap(): return lax.ppermute(array, axis, [(i, i ^ bits) for i in range(peers)])  3.1 us
    ppermute x1, waiting for transfers between devices, by_gather(): lax.ppermute(jnp.where(odd == 1, last, first), 'space', pairs + [(j, i) f...  1.35 us
    pallas_call x1, Pallas kernels, by_gather(): pl.pallas_call(functools.partial(first_part, chans), out_shape=(jax.Shape...  0.97 us
    ppermute x4, waiting for transfers between devices, crossed(): return lax.ppermute(array, ('space', 'chan'), pairs)  0.89 us
    ppermute x1, starting transfers between devices, by_gather(): lax.ppermute(jnp.where(odd == 1, last, first), 'space', pairs + [(j, i) f...  0.69 us
  transfers between devices with their start and end apart: 17, of which 8 were waited for; matrix products, arithmetic and copies ran while one was open for 2% of the time, Pallas kernels for 3%

profile of v4, /device:TPU:0, one launch (start us, length us, event | category | flops | bytes accessed | tf_op | source)
XLA Modules:
  0.0 28.1 jit_solution(12472125908596425122)
XLA Ops:
  0.6 3.5 %collective-permute-start.1 = (bf16[32,2,2,128]{3,2,1,0:T(2,128)(2,1)}, bf16[32,2,2,128]{3,2,1,0:T(2,128)(2,1)S(1)}, u32[]{:S(2)}, u32[]{:S(2)}) collective-permute-start(bf16[32,2,2,128]{3,2,1,0:T(2,128)(2,1)} %param.4), channel_id=1, source_target_pairs={{0,6},{1,7},{2,4},{3,5},{4,2},{5,3},{6,0},{7,1},{8,14},{9,15},{10,... | collective-permute-start | bytes 98312 | tf_op jit(solution)/shard_map/ppermute | solution.py:253
  4.2 1.6 %collective-permute-start = (bf16[32,2,2,128]{3,2,1,0:T(2,128)(2,1)}, bf16[32,2,2,128]{3,2,1,0:T(2,128)(2,1)S(1)}, u32[]{:S(2)}, u32[]{:S(2)}) collective-permute-start(bf16[32,2,2,128]{3,2,1,0:T(2,128)(2,1)} %param.4), channel_id=1, source_target_pairs={{0,7},{1,6},{2,5},{3,4},{4,3},{5,2},{6,1},{7,0},{8,15},{9,14},{10,... | collective-permute-start | bytes 98312 | tf_op jit(solution)/shard_map/ppermute | solution.py:253
  5.8 0.2 collective-permute-start.3
  6.0 0.1 collective-permute-start.2
  6.0 2.6 %collective-permute-start.8 = (bf16[128,256]{1,0:T(8,128)(2,1)}, bf16[128,256]{1,0:T(8,128)(2,1)S(1)}, u32[]{:S(2)}, u32[]{:S(2)}) collective-permute-start(bf16[128,256]{1,0:T(8,128)(2,1)} %bitcast.59), channel_id=1, source_target_pairs={{0,28},{4,24},{8,20},{12,16},{16,12},{20,8},{24,4},{28,0},{1,29},{... | collective-permute-start | bytes 196616 | tf_op jit(solution)/shard_map/ppermute | solution.py:247
  8.6 0.1 collective-permute-start.7
  8.8 0.9 %collective-permute-done.refs_3_ = bf16[32,2,2,128]{3,2,1,0:T(2,128)(2,1)S(1)} collective-permute-done((bf16[32,2,2,128]{3,2,1,0:T(2,128)(2,1)}, bf16[32,2,2,128]{3,2,1,0:T(2,128)(2,1)S(1)}, u32[]{:S(2)}, u32[]{:S(2)}) %collective-permute-start) | collective-permute-done | bytes 32800 | tf_op jit(solution)/shard_map/ppermute | solution.py:253
  9.6 1.9 %collective-permute-start.6 = (bf16[128,256]{1,0:T(8,128)(2,1)S(1)}, bf16[128,256]{1,0:T(8,128)(2,1)S(1)}, u32[]{:S(2)}, u32[]{:S(2)}) collective-permute-start(bf16[128,256]{1,0:T(8,128)(2,1)S(1)} %bitcast.61), channel_id=1, source_target_pairs={{0,12},{4,8},{8,4},{12,0},{16,28},{20,24},{24,20},{28,16},{1,13},{... | collective-permute-start | bytes 196616 | tf_op jit(solution)/shard_map/ppermute | solution.py:247
  11.7 0.0 copy-start
  11.7 0.3 %broadcast_select_fusion = (bf16[4,32,2,128]{3,2,1,0:T(2,128)(2,1)S(1)}, bf16[4,32,2,128]{3,2,1,0:T(2,128)(2,1)S(1)}, bf16[4,32,2,128]{3,2,1,0:T(2,128)(2,1)S(1)}) fusion(pred[]{:T(512)S(6)} %eq.4, bf16[1,32,2,128]{3,2,1,0:T(2,128)(2,1)S(1)} %get-tuple-element.30, bf16[1,32,2,128]{3,2,1,0:T(2,128)(2,1)S(1)} %get-tuple-element.28, ...), kind=kLoop, calls=%fused_computation.1 | loop fusion | flops 229376 | bytes 327681 | tf_op jit(solution)/shard_map/jit(_where)/select_n | solution.py:276
  12.0 0.1 collective-permute-start.5
  12.1 0.7 %collective-permute-start.4 = (bf16[4,32,2,128]{3,2,1,0:T(2,128)(2,1)S(1)}, bf16[4,32,2,128]{3,2,1,0:T(2,128)(2,1)S(1)}, u32[]{:S(2)}, u32[]{:S(2)}) collective-permute-start(bf16[4,32,2,128]{3,2,1,0:T(2,128)(2,1)S(1)} %bitcast.58), channel_id=1, source_target_pairs={{0,12},{8,20},{16,28},{24,4},{12,0},{20,8},{28,16},{4,24},{1,13},{... | collective-permute-start | bytes 196616 | tf_op jit(solution)/shard_map/ppermute | solution.py:278
  12.8 0.3 collective-permute-done.7.refs_5_
  13.0 0.5 %collective-permute-done.6.refs_4_ = bf16[128,256]{1,0:T(8,128)(2,1)S(1)} collective-permute-done((bf16[128,256]{1,0:T(8,128)(2,1)S(1)}, bf16[128,256]{1,0:T(8,128)(2,1)S(1)}, u32[]{:S(2)}, u32[]{:S(2)}) %collective-permute-start.6) | collective-permute-done | bytes 65568 | tf_op jit(solution)/shard_map/ppermute | solution.py:247
  13.5 1.0 %first_part.1 = (f32[64,1024]{1,0:T(8,128)S(1)}, f32[64,512]{1,0:T(8,128)S(1)}) custom-call(bf16[3,288,64]{2,1,0:T(8,128)(2,1)S(1)} %bitcast.50, bf16[4,32,2,128]{3,2,1,0:T(2,128)(2,1)S(1)} %collective-permute-done.5.near_ref, bf16[32,2,2,128]{3,2,1,0:T(2,128)(2,1)S(1)} %collective-permute-done.3.refs_0_, ...), custom_call_target="tpu_custom_call" | custom-call | bytes 5000000 | tf_op jit(solution)/shard_map/first_part/pallas_call | solution.py:295
  14.5 1.3 %collective-permute-done.4.far_ref = bf16[4,32,2,128]{3,2,1,0:T(2,128)(2,1)S(1)} collective-permute-done((bf16[4,32,2,128]{3,2,1,0:T(2,128)(2,1)S(1)}, bf16[4,32,2,128]{3,2,1,0:T(2,128)(2,1)S(1)}, u32[]{:S(2)}, u32[]{:S(2)}) %collective-permute-start.4) | collective-permute-done | bytes 65568 | tf_op jit(solution)/shard_map/ppermute | solution.py:278
  15.8 0.7 %first_rest.1.refs_0_ = bf16[64,256]{1,0:T(8,128)(2,1)S(1)} custom-call(bf16[3,288,64]{2,1,0:T(8,128)(2,1)S(1)} %bitcast.51, bf16[4,32,2,128]{3,2,1,0:T(2,128)(2,1)S(1)} %collective-permute-done.4.far_ref, f32[64,1024]{1,0:T(8,128)S(1)} %get-tuple-element.11.part_ref, f32[64,512]{1,0:T(8,128)S(1)} %get-tuple-element.12.sums_ref), custom_call_target="tpu_custom_call" | custom-call | bytes 4000000 | tf_op jit(solution)/shard_map/first_rest/pallas_call | solution.py:309
  16.5 0.0 copy-start.1
  16.6 1.5 %collective-permute-start.9 = (bf16[4,128,256]{2,1,0:T(8,128)(2,1)S(1)}, bf16[4,128,256]{2,1,0:T(8,128)(2,1)S(1)}, u32[]{:S(2)}, u32[]{:S(2)}) collective-permute-start(bf16[4,128,256]{2,1,0:T(8,128)(2,1)S(1)} %pad_maximum_fusion.cot_ref), channel_id=1, source_target_pairs={{0,4},{4,0},{8,12},{12,8},{16,20},{20,16},{24,28},{28,24},{1,5},{5... | collective-permute-start | bytes 786440 | tf_op jit(solution)/shard_map/ppermute | solution.py:247
  18.1 1.5 %collective-permute-start.15 = (bf16[64,256]{1,0:T(8,128)(2,1)S(1)}, bf16[64,256]{1,0:T(8,128)(2,1)S(1)}, u32[]{:S(2)}, u32[]{:S(2)}) collective-permute-start(bf16[64,256]{1,0:T(8,128)(2,1)S(1)} %first_rest.1.refs_0_), channel_id=1, source_target_pairs={{0,28},{4,24},{8,20},{12,16},{16,12},{20,8},{24,4},{28,0},{1,29},{... | collective-permute-start | bytes 98312 | tf_op jit(solution)/shard_map/ppermute | solution.py:247
  19.6 0.2 collective-permute-start.13
  19.8 1.2 %collective-permute-start.11 = (bf16[64,256]{1,0:T(8,128)(2,1)S(1)}, bf16[64,256]{1,0:T(8,128)(2,1)S(1)}, u32[]{:S(2)}, u32[]{:S(2)}) collective-permute-start(bf16[64,256]{1,0:T(8,128)(2,1)S(1)} %first_rest.1.refs_0_), channel_id=1, source_target_pairs={{0,12},{4,8},{8,4},{12,0},{16,28},{20,24},{24,20},{28,16},{1,13},{... | collective-permute-start | bytes 98312 | tf_op jit(solution)/shard_map/ppermute | solution.py:247
  21.0 0.4 %collective-permute-start.10 = (bf16[64,256]{1,0:T(8,128)(2,1)S(1)}, bf16[64,256]{1,0:T(8,128)(2,1)S(1)}, u32[]{:S(2)}, u32[]{:S(2)}) collective-permute-start(bf16[64,256]{1,0:T(8,128)(2,1)S(1)} %first_rest.1.refs_0_), channel_id=1, source_target_pairs={{0,4},{4,0},{8,12},{12,8},{16,20},{20,16},{24,28},{28,24},{1,5},{5... | collective-permute-start | bytes 98312 | tf_op jit(solution)/shard_map/ppermute | solution.py:247
  21.4 1.0 %collective-permute-done.15.refs_7_ = bf16[64,256]{1,0:T(8,128)(2,1)S(1)} collective-permute-done((bf16[64,256]{1,0:T(8,128)(2,1)S(1)}, bf16[64,256]{1,0:T(8,128)(2,1)S(1)}, u32[]{:S(2)}, u32[]{:S(2)}) %collective-permute-start.15) | collective-permute-done | bytes 32800 | tf_op jit(solution)/shard_map/ppermute | solution.py:247
  22.4 0.1 collective-permute-start.16
  22.6 0.8 %collective-permute-done.13.refs_5_ = bf16[64,256]{1,0:T(8,128)(2,1)S(1)} collective-permute-done((bf16[64,256]{1,0:T(8,128)(2,1)S(1)}, bf16[64,256]{1,0:T(8,128)(2,1)S(1)}, u32[]{:S(2)}, u32[]{:S(2)}) %collective-permute-start.13) | collective-permute-done | bytes 32800 | tf_op jit(solution)/shard_map/ppermute | solution.py:247
  23.3 0.1 collective-permute-start.14
  23.4 0.4 %collective-permute-start.12 = (bf16[64,256]{1,0:T(8,128)(2,1)S(1)}, bf16[64,256]{1,0:T(8,128)(2,1)S(1)}, u32[]{:S(2)}, u32[]{:S(2)}) collective-permute-start(bf16[64,256]{1,0:T(8,128)(2,1)S(1)} %collective-permute-done.11.refs_3_), channel_id=1, source_target_pairs={{0,4},{4,0},{8,12},{12,8},{16,20},{20,16},{24,28},{28,24},{1,5},{5... | collective-permute-start | bytes 98312 | tf_op jit(solution)/shard_map/ppermute | solution.py:247
  23.8 0.2 copy.23.w_ref
  24.1 0.5 %collective-permute-done.14.refs_4_ = bf16[64,256]{1,0:T(8,128)(2,1)S(1)} collective-permute-done((bf16[64,256]{1,0:T(8,128)(2,1)S(1)}, bf16[64,256]{1,0:T(8,128)(2,1)S(1)}, u32[]{:S(2)}, u32[]{:S(2)}) %collective-permute-start.14) | collective-permute-done | bytes 32800 | tf_op jit(solution)/shard_map/ppermute | solution.py:247
  24.5 0.2 collective-permute-done.12.refs_2_
  24.7 3.4 %deep.1 = (bf16[128,256]{1,0:T(8,128)(2,1)}, f32[1728,128]{1,0:T(8,128)}) custom-call(bf16[128,1728]{1,0:T(8,128)(2,1)S(1)} %copy.23.w_ref, bf16[4,128,256]{2,1,0:T(8,128)(2,1)S(1)} %pad_maximum_fusion.cot_ref, bf16[4,128,256]{2,1,0:T(8,128)(2,1)S(1)} %collective-permute-done.9.cot_swapped_ref, bf16[64,256]{1,0:T(8,128)(2,1)S(1)} %first_rest.1.refs_0_, ...), custom_call_target="tpu_custom_call" | custom-call | bytes 12000000 | tf_op jit(solution)/shard_map/deep/pallas_call | solution.py:328
  (19 shorter events, 0.2 us)
Async XLA Ops:
  0.6 9.0 %copy-start.2 = (bf16[128,1,256]{2,0,1:T(8,128)(2,1)S(1)}, bf16[128,1,256]{2,0,1:T(8,128)(2,1)}, u32[]{:S(2)}) copy-start(bf16[128,1,256]{2,0,1:T(8,128)(2,1)} %param.7) | copy-start | bytes 196612
  0.6 8.0 %collective-permute-start.1 = (bf16[32,2,2,128]{3,2,1,0:T(2,128)(2,1)}, bf16[32,2,2,128]{3,2,1,0:T(2,128)(2,1)S(1)}, u32[]{:S(2)}, u32[]{:S(2)}) collective-permute-start(bf16[32,2,2,128]{3,2,1,0:T(2,128)(2,1)} %param.4), channel_id=1, source_target_pairs={{0,6},{1,7},{2,4},{3,5},{4,2},{5,3},{6,0},{7,1},{8,14},{9,15},{10,... | collective-permute-start | bytes 98312 | tf_op jit(solution)/shard_map/ppermute | solution.py:253
  4.2 5.5 %collective-permute-start = (bf16[32,2,2,128]{3,2,1,0:T(2,128)(2,1)}, bf16[32,2,2,128]{3,2,1,0:T(2,128)(2,1)S(1)}, u32[]{:S(2)}, u32[]{:S(2)}) collective-permute-start(bf16[32,2,2,128]{3,2,1,0:T(2,128)(2,1)} %param.4), channel_id=1, source_target_pairs={{0,7},{1,6},{2,5},{3,4},{4,3},{5,2},{6,1},{7,0},{8,15},{9,14},{10,... | collective-permute-start | bytes 98312 | tf_op jit(solution)/shard_map/ppermute | solution.py:253
  5.8 5.8 %collective-permute-start.3 = (bf16[32,2,2,128]{3,2,1,0:T(2,128)(2,1)}, bf16[32,2,2,128]{3,2,1,0:T(2,128)(2,1)S(1)}, u32[]{:S(2)}, u32[]{:S(2)}) collective-permute-start(bf16[32,2,2,128]{3,2,1,0:T(2,128)(2,1)} %param.4), channel_id=1, source_target_pairs={{0,4},{1,5},{2,6},{3,7},{4,0},{5,1},{6,2},{7,3},{8,12},{9,13},{10,... | collective-permute-start | bytes 98312 | tf_op jit(solution)/shard_map/ppermute | solution.py:253
  6.0 5.7 %collective-permute-start.2 = (bf16[32,2,2,128]{3,2,1,0:T(2,128)(2,1)}, bf16[32,2,2,128]{3,2,1,0:T(2,128)(2,1)S(1)}, u32[]{:S(2)}, u32[]{:S(2)}) collective-permute-start(bf16[32,2,2,128]{3,2,1,0:T(2,128)(2,1)} %param.4), channel_id=1, source_target_pairs={{0,5},{1,4},{2,7},{3,6},{4,1},{5,0},{6,3},{7,2},{8,13},{9,12},{10,... | collective-permute-start | bytes 98312 | tf_op jit(solution)/shard_map/ppermute | solution.py:253
  6.0 6.7 %collective-permute-start.8 = (bf16[128,256]{1,0:T(8,128)(2,1)}, bf16[128,256]{1,0:T(8,128)(2,1)S(1)}, u32[]{:S(2)}, u32[]{:S(2)}) collective-permute-start(bf16[128,256]{1,0:T(8,128)(2,1)} %bitcast.59), channel_id=1, source_target_pairs={{0,28},{4,24},{8,20},{12,16},{16,12},{20,8},{24,4},{28,0},{1,29},{... | collective-permute-start | bytes 196616 | tf_op jit(solution)/shard_map/ppermute | solution.py:247
  8.6 4.4 %collective-permute-start.7 = (bf16[128,256]{1,0:T(8,128)(2,1)}, bf16[128,256]{1,0:T(8,128)(2,1)S(1)}, u32[]{:S(2)}, u32[]{:S(2)}) collective-permute-start(bf16[128,256]{1,0:T(8,128)(2,1)} %bitcast.60), channel_id=1, source_target_pairs={{0,20},{4,16},{8,28},{12,24},{16,4},{20,0},{24,12},{28,8},{1,21},{... | collective-permute-start | bytes 196616 | tf_op jit(solution)/shard_map/ppermute | solution.py:247
  9.6 3.9 %collective-permute-start.6 = (bf16[128,256]{1,0:T(8,128)(2,1)S(1)}, bf16[128,256]{1,0:T(8,128)(2,1)S(1)}, u32[]{:S(2)}, u32[]{:S(2)}) collective-permute-start(bf16[128,256]{1,0:T(8,128)(2,1)S(1)} %bitcast.61), channel_id=1, source_target_pairs={{0,12},{4,8},{8,4},{12,0},{16,28},{20,24},{24,20},{28,16},{1,13},{... | collective-permute-start | bytes 196616 | tf_op jit(solution)/shard_map/ppermute | solution.py:247
  11.7 1.8 %copy-start = (bf16[3,3,3,64,32]{3,4,2,1,0:T(8,128)(2,1)S(1)}, bf16[3,3,3,64,32]{3,4,2,1,0:T(8,128)(2,1)}, u32[]{:S(2)}) copy-start(bf16[3,3,3,64,32]{3,4,2,1,0:T(8,128)(2,1)} %param.5) | copy-start | bytes 331780
  12.0 1.5 %collective-permute-start.5 = (bf16[4,32,2,128]{3,2,1,0:T(2,128)(2,1)S(1)}, bf16[4,32,2,128]{3,2,1,0:T(2,128)(2,1)S(1)}, u32[]{:S(2)}, u32[]{:S(2)}) collective-permute-start(bf16[4,32,2,128]{3,2,1,0:T(2,128)(2,1)S(1)} %get-tuple-element.20), channel_id=1, source_target_pairs={{0,4},{4,0},{8,12},{12,8},{16,20},{20,16},{24,28},{28,24},{1,5},{5... | collective-permute-start | bytes 196616 | tf_op jit(solution)/shard_map/ppermute | solution.py:247
  12.1 3.8 %collective-permute-start.4 = (bf16[4,32,2,128]{3,2,1,0:T(2,128)(2,1)S(1)}, bf16[4,32,2,128]{3,2,1,0:T(2,128)(2,1)S(1)}, u32[]{:S(2)}, u32[]{:S(2)}) collective-permute-start(bf16[4,32,2,128]{3,2,1,0:T(2,128)(2,1)S(1)} %bitcast.58), channel_id=1, source_target_pairs={{0,12},{8,20},{16,28},{24,4},{12,0},{20,8},{28,16},{4,24},{1,13},{... | collective-permute-start | bytes 196616 | tf_op jit(solution)/shard_map/ppermute | solution.py:278
  16.5 7.3 %copy-start.1 = (bf16[3,3,3,128,64]{3,4,2,1,0:T(8,128)(2,1)S(1)}, bf16[3,3,3,128,64]{3,4,2,1,0:T(8,128)(2,1)}, u32[]{:S(2)}) copy-start(bf16[3,3,3,128,64]{3,4,2,1,0:T(8,128)(2,1)} %param.6) | copy-start | bytes 1327108
  16.6 8.1 %collective-permute-start.9 = (bf16[4,128,256]{2,1,0:T(8,128)(2,1)S(1)}, bf16[4,128,256]{2,1,0:T(8,128)(2,1)S(1)}, u32[]{:S(2)}, u32[]{:S(2)}) collective-permute-start(bf16[4,128,256]{2,1,0:T(8,128)(2,1)S(1)} %pad_maximum_fusion.cot_ref), channel_id=1, source_target_pairs={{0,4},{4,0},{8,12},{12,8},{16,20},{20,16},{24,28},{28,24},{1,5},{5... | collective-permute-start | bytes 786440 | tf_op jit(solution)/shard_map/ppermute | solution.py:247
  18.1 4.3 %collective-permute-start.15 = (bf16[64,256]{1,0:T(8,128)(2,1)S(1)}, bf16[64,256]{1,0:T(8,128)(2,1)S(1)}, u32[]{:S(2)}, u32[]{:S(2)}) collective-permute-start(bf16[64,256]{1,0:T(8,128)(2,1)S(1)} %first_rest.1.refs_0_), channel_id=1, source_target_pairs={{0,28},{4,24},{8,20},{12,16},{16,12},{20,8},{24,4},{28,0},{1,29},{... | collective-permute-start | bytes 98312 | tf_op jit(solution)/shard_map/ppermute | solution.py:247
  19.6 3.7 %collective-permute-start.13 = (bf16[64,256]{1,0:T(8,128)(2,1)S(1)}, bf16[64,256]{1,0:T(8,128)(2,1)S(1)}, u32[]{:S(2)}, u32[]{:S(2)}) collective-permute-start(bf16[64,256]{1,0:T(8,128)(2,1)S(1)} %first_rest.1.refs_0_), channel_id=1, source_target_pairs={{0,20},{4,16},{8,28},{12,24},{16,4},{20,0},{24,12},{28,8},{1,21},{... | collective-permute-start | bytes 98312 | tf_op jit(solution)/shard_map/ppermute | solution.py:247
  19.8 3.7 %collective-permute-start.11 = (bf16[64,256]{1,0:T(8,128)(2,1)S(1)}, bf16[64,256]{1,0:T(8,128)(2,1)S(1)}, u32[]{:S(2)}, u32[]{:S(2)}) collective-permute-start(bf16[64,256]{1,0:T(8,128)(2,1)S(1)} %first_rest.1.refs_0_), channel_id=1, source_target_pairs={{0,12},{4,8},{8,4},{12,0},{16,28},{20,24},{24,20},{28,16},{1,13},{... | collective-permute-start | bytes 98312 | tf_op jit(solution)/shard_map/ppermute | solution.py:247
  21.0 3.0 %collective-permute-start.10 = (bf16[64,256]{1,0:T(8,128)(2,1)S(1)}, bf16[64,256]{1,0:T(8,128)(2,1)S(1)}, u32[]{:S(2)}, u32[]{:S(2)}) collective-permute-start(bf16[64,256]{1,0:T(8,128)(2,1)S(1)} %first_rest.1.refs_0_), channel_id=1, source_target_pairs={{0,4},{4,0},{8,12},{12,8},{16,20},{20,16},{24,28},{28,24},{1,5},{5... | collective-permute-start | bytes 98312 | tf_op jit(solution)/shard_map/ppermute | solution.py:247
  22.4 1.6 %collective-permute-start.16 = (bf16[64,256]{1,0:T(8,128)(2,1)S(1)}, bf16[64,256]{1,0:T(8,128)(2,1)S(1)}, u32[]{:S(2)}, u32[]{:S(2)}) collective-permute-start(bf16[64,256]{1,0:T(8,128)(2,1)S(1)} %collective-permute-done.15.refs_7_), channel_id=1, source_target_pairs={{0,4},{4,0},{8,12},{12,8},{16,20},{20,16},{24,28},{28,24},{1,5},{5... | collective-permute-start | bytes 98312 | tf_op jit(solution)/shard_map/ppermute | solution.py:247
  23.3 1.2 %collective-permute-start.14 = (bf16[64,256]{1,0:T(8,128)(2,1)S(1)}, bf16[64,256]{1,0:T(8,128)(2,1)S(1)}, u32[]{:S(2)}, u32[]{:S(2)}) collective-permute-start(bf16[64,256]{1,0:T(8,128)(2,1)S(1)} %collective-permute-done.13.refs_5_), channel_id=1, source_target_pairs={{0,4},{4,0},{8,12},{12,8},{16,20},{20,16},{24,28},{28,24},{1,5},{5... | collective-permute-start | bytes 98312 | tf_op jit(solution)/shard_map/ppermute | solution.py:247
  23.4 1.3 %collective-permute-start.12 = (bf16[64,256]{1,0:T(8,128)(2,1)S(1)}, bf16[64,256]{1,0:T(8,128)(2,1)S(1)}, u32[]{:S(2)}, u32[]{:S(2)}) collective-permute-start(bf16[64,256]{1,0:T(8,128)(2,1)S(1)} %collective-permute-done.11.refs_3_), channel_id=1, source_target_pairs={{0,4},{4,0},{8,12},{12,8},{16,20},{20,16},{24,28},{28,24},{1,5},{5... | collective-permute-start | bytes 98312 | tf_op jit(solution)/shard_map/ppermute | solution.py:247

commit v5 on v4

--- a/solution.py
+++ b/solution.py
@@ -151,12 +151,11 @@
         rows_k = far_ref[far_ref.shape[0] - 1 - k]
         place_rows(grid, 0, mine ^ k, jnp.where(has_far, rows_k, jnp.zeros_like(rows_k)))
     fill_patches(grid, moved, patches)
-    to_far = w_ref[2 * odd]
+    terms = lax.dot_general(w_ref[2 * odd], patches[...], TN, preferred_element_type=jnp.float32)
     sums = []
     for pair in range((rows - 2) // 2):
         cols = slice(pair * 2 * depth, (pair + 1) * 2 * depth)
-        term = lax.dot_general(to_far, patches[:, cols], TN, preferred_element_type=jnp.float32)
-        act = silu(part_ref[:, cols] + term)
+        act = silu(part_ref[:, cols] + terms[:, cols])
         total = sums_ref[:, pair * depth : (pair + 1) * depth] + act[:, :depth] + act[:, depth:]
         sums.append(total * 0.125)
     fold_in = lax.broadcasted_iota(jnp.int32, (2 * depth, depth), 0)

time: 28.3 us -> 28.3 us (level)
  no operation moved by 1% of the time
where the time goes in v5:
time: 28.3 us; the launch traced here: 28.1 us
  starting transfers between devices  16.3 us (58%)
  waiting for transfers between devices  5.34 us (19%)
  Pallas kernels  5.08 us (18%)
  between operations  0.77 us (3%)
  local copies, waits for them, and re-layouts  0.33 us (1%)
  other arithmetic  0.33 us (1%)
    ppermute x12, starting transfers between devices, swap(): return lax.ppermute(array, axis, [(i, i ^ bits) for i in range(peers)])  10.2 us
    ppermute x4, starting transfers between devices, crossed(): return lax.ppermute(array, ('space', 'chan'), pairs)  5.4 us
    pallas_call x1, Pallas kernels, by_gather(): pl.pallas_call(functools.partial(deep_kernel, depth // 2, order), out_sha...  3.43 us
    ppermute x12, waiting for transfers between devices, swap(): return lax.ppermute(array, axis, [(i, i ^ bits) for i in range(peers)])  3.1 us
    ppermute x1, waiting for transfers between devices, by_gather(): lax.ppermute(jnp.where(odd == 1, last, first), 'space', pairs + [(j, i) f...  1.35 us
    pallas_call x1, Pallas kernels, by_gather(): pl.pallas_call(functools.partial(first_part, chans), out_shape=(jax.Shape...  0.97 us
    ppermute x4, waiting for transfers between devices, crossed(): return lax.ppermute(array, ('space', 'chan'), pairs)  0.89 us
    ppermute x1, starting transfers between devices, by_gather(): lax.ppermute(jnp.where(odd == 1, last, first), 'space', pairs + [(j, i) f...  0.69 us
  transfers between devices with their start and end apart: 17, of which 8 were waited for; matrix products, arithmetic and copies ran while one was open for 2% of the time, Pallas kernels for 3%

profile of v5, /device:TPU:0, one launch (start us, length us, event | category | flops | bytes accessed | tf_op | source)
XLA Modules:
  0.0 28.1 jit_solution(12472125908596425122)
XLA Ops:
  0.6 3.5 %collective-permute-start.1 = (bf16[32,2,2,128]{3,2,1,0:T(2,128)(2,1)}, bf16[32,2,2,128]{3,2,1,0:T(2,128)(2,1)S(1)}, u32[]{:S(2)}, u32[]{:S(2)}) collective-permute-start(bf16[32,2,2,128]{3,2,1,0:T(2,128)(2,1)} %param.4), channel_id=1, source_target_pairs={{0,6},{1,7},{2,4},{3,5},{4,2},{5,3},{6,0},{7,1},{8,14},{9,15},{10,... | collective-permute-start | bytes 98312 | tf_op jit(solution)/shard_map/ppermute | solution.py:252
  4.2 1.6 %collective-permute-start = (bf16[32,2,2,128]{3,2,1,0:T(2,128)(2,1)}, bf16[32,2,2,128]{3,2,1,0:T(2,128)(2,1)S(1)}, u32[]{:S(2)}, u32[]{:S(2)}) collective-permute-start(bf16[32,2,2,128]{3,2,1,0:T(2,128)(2,1)} %param.4), channel_id=1, source_target_pairs={{0,7},{1,6},{2,5},{3,4},{4,3},{5,2},{6,1},{7,0},{8,15},{9,14},{10,... | collective-permute-start | bytes 98312 | tf_op jit(solution)/shard_map/ppermute | solution.py:252
  5.8 0.2 collective-permute-start.3
  6.0 0.1 collective-permute-start.2
  6.0 2.6 %collective-permute-start.8 = (bf16[128,256]{1,0:T(8,128)(2,1)}, bf16[128,256]{1,0:T(8,128)(2,1)S(1)}, u32[]{:S(2)}, u32[]{:S(2)}) collective-permute-start(bf16[128,256]{1,0:T(8,128)(2,1)} %bitcast.59), channel_id=1, source_target_pairs={{0,28},{4,24},{8,20},{12,16},{16,12},{20,8},{24,4},{28,0},{1,29},{... | collective-permute-start | bytes 196616 | tf_op jit(solution)/shard_map/ppermute | solution.py:246
  8.6 0.1 collective-permute-start.7
  8.8 0.9 %collective-permute-done.refs_3_ = bf16[32,2,2,128]{3,2,1,0:T(2,128)(2,1)S(1)} collective-permute-done((bf16[32,2,2,128]{3,2,1,0:T(2,128)(2,1)}, bf16[32,2,2,128]{3,2,1,0:T(2,128)(2,1)S(1)}, u32[]{:S(2)}, u32[]{:S(2)}) %collective-permute-start) | collective-permute-done | bytes 32800 | tf_op jit(solution)/shard_map/ppermute | solution.py:252
  9.6 1.9 %collective-permute-start.6 = (bf16[128,256]{1,0:T(8,128)(2,1)S(1)}, bf16[128,256]{1,0:T(8,128)(2,1)S(1)}, u32[]{:S(2)}, u32[]{:S(2)}) collective-permute-start(bf16[128,256]{1,0:T(8,128)(2,1)S(1)} %bitcast.61), channel_id=1, source_target_pairs={{0,12},{4,8},{8,4},{12,0},{16,28},{20,24},{24,20},{28,16},{1,13},{... | collective-permute-start | bytes 196616 | tf_op jit(solution)/shard_map/ppermute | solution.py:246
  11.7 0.0 copy-start
  11.7 0.3 %broadcast_select_fusion = (bf16[4,32,2,128]{3,2,1,0:T(2,128)(2,1)S(1)}, bf16[4,32,2,128]{3,2,1,0:T(2,128)(2,1)S(1)}, bf16[4,32,2,128]{3,2,1,0:T(2,128)(2,1)S(1)}) fusion(pred[]{:T(512)S(6)} %eq.4, bf16[1,32,2,128]{3,2,1,0:T(2,128)(2,1)S(1)} %get-tuple-element.30, bf16[1,32,2,128]{3,2,1,0:T(2,128)(2,1)S(1)} %get-tuple-element.28, ...), kind=kLoop, calls=%fused_computation.1 | loop fusion | flops 229376 | bytes 327681 | tf_op jit(solution)/shard_map/jit(_where)/select_n | solution.py:275
  12.0 0.1 collective-permute-start.5
  12.1 0.7 %collective-permute-start.4 = (bf16[4,32,2,128]{3,2,1,0:T(2,128)(2,1)S(1)}, bf16[4,32,2,128]{3,2,1,0:T(2,128)(2,1)S(1)}, u32[]{:S(2)}, u32[]{:S(2)}) collective-permute-start(bf16[4,32,2,128]{3,2,1,0:T(2,128)(2,1)S(1)} %bitcast.58), channel_id=1, source_target_pairs={{0,12},{8,20},{16,28},{24,4},{12,0},{20,8},{28,16},{4,24},{1,13},{... | collective-permute-start | bytes 196616 | tf_op jit(solution)/shard_map/ppermute | solution.py:277
  12.8 0.3 collective-permute-done.7.refs_5_
  13.0 0.5 %collective-permute-done.6.refs_4_ = bf16[128,256]{1,0:T(8,128)(2,1)S(1)} collective-permute-done((bf16[128,256]{1,0:T(8,128)(2,1)S(1)}, bf16[128,256]{1,0:T(8,128)(2,1)S(1)}, u32[]{:S(2)}, u32[]{:S(2)}) %collective-permute-start.6) | collective-permute-done | bytes 65568 | tf_op jit(solution)/shard_map/ppermute | solution.py:246
  13.5 1.0 %first_part.1 = (f32[64,1024]{1,0:T(8,128)S(1)}, f32[64,512]{1,0:T(8,128)S(1)}) custom-call(bf16[3,288,64]{2,1,0:T(8,128)(2,1)S(1)} %bitcast.50, bf16[4,32,2,128]{3,2,1,0:T(2,128)(2,1)S(1)} %collective-permute-done.5.near_ref, bf16[32,2,2,128]{3,2,1,0:T(2,128)(2,1)S(1)} %collective-permute-done.3.refs_0_, ...), custom_call_target="tpu_custom_call" | custom-call | bytes 5000000 | tf_op jit(solution)/shard_map/first_part/pallas_call | solution.py:294
  14.5 1.3 %collective-permute-done.4.far_ref = bf16[4,32,2,128]{3,2,1,0:T(2,128)(2,1)S(1)} collective-permute-done((bf16[4,32,2,128]{3,2,1,0:T(2,128)(2,1)S(1)}, bf16[4,32,2,128]{3,2,1,0:T(2,128)(2,1)S(1)}, u32[]{:S(2)}, u32[]{:S(2)}) %collective-permute-start.4) | collective-permute-done | bytes 65568 | tf_op jit(solution)/shard_map/ppermute | solution.py:277
  15.8 0.7 %first_rest.1.refs_0_ = bf16[64,256]{1,0:T(8,128)(2,1)S(1)} custom-call(bf16[3,288,64]{2,1,0:T(8,128)(2,1)S(1)} %bitcast.51, bf16[4,32,2,128]{3,2,1,0:T(2,128)(2,1)S(1)} %collective-permute-done.4.far_ref, f32[64,1024]{1,0:T(8,128)S(1)} %get-tuple-element.11.part_ref, f32[64,512]{1,0:T(8,128)S(1)} %get-tuple-element.12.sums_ref), custom_call_target="tpu_custom_call" | custom-call | bytes 4000000 | tf_op jit(solution)/shard_map/first_rest/pallas_call | solution.py:308
  16.5 0.0 copy-start.1
  16.6 1.5 %collective-permute-start.9 = (bf16[4,128,256]{2,1,0:T(8,128)(2,1)S(1)}, bf16[4,128,256]{2,1,0:T(8,128)(2,1)S(1)}, u32[]{:S(2)}, u32[]{:S(2)}) collective-permute-start(bf16[4,128,256]{2,1,0:T(8,128)(2,1)S(1)} %pad_maximum_fusion.cot_ref), channel_id=1, source_target_pairs={{0,4},{4,0},{8,12},{12,8},{16,20},{20,16},{24,28},{28,24},{1,5},{5... | collective-permute-start | bytes 786440 | tf_op jit(solution)/shard_map/ppermute | solution.py:246
  18.1 1.5 %collective-permute-start.15 = (bf16[64,256]{1,0:T(8,128)(2,1)S(1)}, bf16[64,256]{1,0:T(8,128)(2,1)S(1)}, u32[]{:S(2)}, u32[]{:S(2)}) collective-permute-start(bf16[64,256]{1,0:T(8,128)(2,1)S(1)} %first_rest.1.refs_0_), channel_id=1, source_target_pairs={{0,28},{4,24},{8,20},{12,16},{16,12},{20,8},{24,4},{28,0},{1,29},{... | collective-permute-start | bytes 98312 | tf_op jit(solution)/shard_map/ppermute | solution.py:246
  19.6 0.2 collective-permute-start.13
  19.8 1.2 %collective-permute-start.11 = (bf16[64,256]{1,0:T(8,128)(2,1)S(1)}, bf16[64,256]{1,0:T(8,128)(2,1)S(1)}, u32[]{:S(2)}, u32[]{:S(2)}) collective-permute-start(bf16[64,256]{1,0:T(8,128)(2,1)S(1)} %first_rest.1.refs_0_), channel_id=1, source_target_pairs={{0,12},{4,8},{8,4},{12,0},{16,28},{20,24},{24,20},{28,16},{1,13},{... | collective-permute-start | bytes 98312 | tf_op jit(solution)/shard_map/ppermute | solution.py:246
  21.0 0.4 %collective-permute-start.10 = (bf16[64,256]{1,0:T(8,128)(2,1)S(1)}, bf16[64,256]{1,0:T(8,128)(2,1)S(1)}, u32[]{:S(2)}, u32[]{:S(2)}) collective-permute-start(bf16[64,256]{1,0:T(8,128)(2,1)S(1)} %first_rest.1.refs_0_), channel_id=1, source_target_pairs={{0,4},{4,0},{8,12},{12,8},{16,20},{20,16},{24,28},{28,24},{1,5},{5... | collective-permute-start | bytes 98312 | tf_op jit(solution)/shard_map/ppermute | solution.py:246
  21.4 1.0 %collective-permute-done.15.refs_7_ = bf16[64,256]{1,0:T(8,128)(2,1)S(1)} collective-permute-done((bf16[64,256]{1,0:T(8,128)(2,1)S(1)}, bf16[64,256]{1,0:T(8,128)(2,1)S(1)}, u32[]{:S(2)}, u32[]{:S(2)}) %collective-permute-start.15) | collective-permute-done | bytes 32800 | tf_op jit(solution)/shard_map/ppermute | solution.py:246
  22.4 0.1 collective-permute-start.16
  22.6 0.8 %collective-permute-done.13.refs_5_ = bf16[64,256]{1,0:T(8,128)(2,1)S(1)} collective-permute-done((bf16[64,256]{1,0:T(8,128)(2,1)S(1)}, bf16[64,256]{1,0:T(8,128)(2,1)S(1)}, u32[]{:S(2)}, u32[]{:S(2)}) %collective-permute-start.13) | collective-permute-done | bytes 32800 | tf_op jit(solution)/shard_map/ppermute | solution.py:246
  23.3 0.1 collective-permute-start.14
  23.4 0.4 %collective-permute-start.12 = (bf16[64,256]{1,0:T(8,128)(2,1)S(1)}, bf16[64,256]{1,0:T(8,128)(2,1)S(1)}, u32[]{:S(2)}, u32[]{:S(2)}) collective-permute-start(bf16[64,256]{1,0:T(8,128)(2,1)S(1)} %collective-permute-done.11.refs_3_), channel_id=1, source_target_pairs={{0,4},{4,0},{8,12},{12,8},{16,20},{20,16},{24,28},{28,24},{1,5},{5... | collective-permute-start | bytes 98312 | tf_op jit(solution)/shard_map/ppermute | solution.py:246
  23.8 0.2 copy.23.w_ref
  24.1 0.5 %collective-permute-done.14.refs_4_ = bf16[64,256]{1,0:T(8,128)(2,1)S(1)} collective-permute-done((bf16[64,256]{1,0:T(8,128)(2,1)S(1)}, bf16[64,256]{1,0:T(8,128)(2,1)S(1)}, u32[]{:S(2)}, u32[]{:S(2)}) %collective-permute-start.14) | collective-permute-done | bytes 32800 | tf_op jit(solution)/shard_map/ppermute | solution.py:246
  24.5 0.2 collective-permute-done.12.refs_2_
  24.7 3.4 %deep.1 = (bf16[128,256]{1,0:T(8,128)(2,1)}, f32[1728,128]{1,0:T(8,128)}) custom-call(bf16[128,1728]{1,0:T(8,128)(2,1)S(1)} %copy.23.w_ref, bf16[4,128,256]{2,1,0:T(8,128)(2,1)S(1)} %pad_maximum_fusion.cot_ref, bf16[4,128,256]{2,1,0:T(8,128)(2,1)S(1)} %collective-permute-done.9.cot_swapped_ref, bf16[64,256]{1,0:T(8,128)(2,1)S(1)} %first_rest.1.refs_0_, ...), custom_call_target="tpu_custom_call" | custom-call | bytes 12000000 | tf_op jit(solution)/shard_map/deep/pallas_call | solution.py:327
  (19 shorter events, 0.2 us)
Async XLA Ops:
  0.6 9.0 %copy-start.2 = (bf16[128,1,256]{2,0,1:T(8,128)(2,1)S(1)}, bf16[128,1,256]{2,0,1:T(8,128)(2,1)}, u32[]{:S(2)}) copy-start(bf16[128,1,256]{2,0,1:T(8,128)(2,1)} %param.7) | copy-start | bytes 196612
  0.6 8.0 %collective-permute-start.1 = (bf16[32,2,2,128]{3,2,1,0:T(2,128)(2,1)}, bf16[32,2,2,128]{3,2,1,0:T(2,128)(2,1)S(1)}, u32[]{:S(2)}, u32[]{:S(2)}) collective-permute-start(bf16[32,2,2,128]{3,2,1,0:T(2,128)(2,1)} %param.4), channel_id=1, source_target_pairs={{0,6},{1,7},{2,4},{3,5},{4,2},{5,3},{6,0},{7,1},{8,14},{9,15},{10,... | collective-permute-start | bytes 98312 | tf_op jit(solution)/shard_map/ppermute | solution.py:252
  4.2 5.5 %collective-permute-start = (bf16[32,2,2,128]{3,2,1,0:T(2,128)(2,1)}, bf16[32,2,2,128]{3,2,1,0:T(2,128)(2,1)S(1)}, u32[]{:S(2)}, u32[]{:S(2)}) collective-permute-start(bf16[32,2,2,128]{3,2,1,0:T(2,128)(2,1)} %param.4), channel_id=1, source_target_pairs={{0,7},{1,6},{2,5},{3,4},{4,3},{5,2},{6,1},{7,0},{8,15},{9,14},{10,... | collective-permute-start | bytes 98312 | tf_op jit(solution)/shard_map/ppermute | solution.py:252
  5.8 5.8 %collective-permute-start.3 = (bf16[32,2,2,128]{3,2,1,0:T(2,128)(2,1)}, bf16[32,2,2,128]{3,2,1,0:T(2,128)(2,1)S(1)}, u32[]{:S(2)}, u32[]{:S(2)}) collective-permute-start(bf16[32,2,2,128]{3,2,1,0:T(2,128)(2,1)} %param.4), channel_id=1, source_target_pairs={{0,4},{1,5},{2,6},{3,7},{4,0},{5,1},{6,2},{7,3},{8,12},{9,13},{10,... | collective-permute-start | bytes 98312 | tf_op jit(solution)/shard_map/ppermute | solution.py:252
  6.0 5.7 %collective-permute-start.2 = (bf16[32,2,2,128]{3,2,1,0:T(2,128)(2,1)}, bf16[32,2,2,128]{3,2,1,0:T(2,128)(2,1)S(1)}, u32[]{:S(2)}, u32[]{:S(2)}) collective-permute-start(bf16[32,2,2,128]{3,2,1,0:T(2,128)(2,1)} %param.4), channel_id=1, source_target_pairs={{0,5},{1,4},{2,7},{3,6},{4,1},{5,0},{6,3},{7,2},{8,13},{9,12},{10,... | collective-permute-start | bytes 98312 | tf_op jit(solution)/shard_map/ppermute | solution.py:252
  6.0 6.7 %collective-permute-start.8 = (bf16[128,256]{1,0:T(8,128)(2,1)}, bf16[128,256]{1,0:T(8,128)(2,1)S(1)}, u32[]{:S(2)}, u32[]{:S(2)}) collective-permute-start(bf16[128,256]{1,0:T(8,128)(2,1)} %bitcast.59), channel_id=1, source_target_pairs={{0,28},{4,24},{8,20},{12,16},{16,12},{20,8},{24,4},{28,0},{1,29},{... | collective-permute-start | bytes 196616 | tf_op jit(solution)/shard_map/ppermute | solution.py:246
  8.6 4.4 %collective-permute-start.7 = (bf16[128,256]{1,0:T(8,128)(2,1)}, bf16[128,256]{1,0:T(8,128)(2,1)S(1)}, u32[]{:S(2)}, u32[]{:S(2)}) collective-permute-start(bf16[128,256]{1,0:T(8,128)(2,1)} %bitcast.60), channel_id=1, source_target_pairs={{0,20},{4,16},{8,28},{12,24},{16,4},{20,0},{24,12},{28,8},{1,21},{... | collective-permute-start | bytes 196616 | tf_op jit(solution)/shard_map/ppermute | solution.py:246
  9.6 3.9 %collective-permute-start.6 = (bf16[128,256]{1,0:T(8,128)(2,1)S(1)}, bf16[128,256]{1,0:T(8,128)(2,1)S(1)}, u32[]{:S(2)}, u32[]{:S(2)}) collective-permute-start(bf16[128,256]{1,0:T(8,128)(2,1)S(1)} %bitcast.61), channel_id=1, source_target_pairs={{0,12},{4,8},{8,4},{12,0},{16,28},{20,24},{24,20},{28,16},{1,13},{... | collective-permute-start | bytes 196616 | tf_op jit(solution)/shard_map/ppermute | solution.py:246
  11.7 1.8 %copy-start = (bf16[3,3,3,64,32]{3,4,2,1,0:T(8,128)(2,1)S(1)}, bf16[3,3,3,64,32]{3,4,2,1,0:T(8,128)(2,1)}, u32[]{:S(2)}) copy-start(bf16[3,3,3,64,32]{3,4,2,1,0:T(8,128)(2,1)} %param.5) | copy-start | bytes 331780
  12.0 1.5 %collective-permute-start.5 = (bf16[4,32,2,128]{3,2,1,0:T(2,128)(2,1)S(1)}, bf16[4,32,2,128]{3,2,1,0:T(2,128)(2,1)S(1)}, u32[]{:S(2)}, u32[]{:S(2)}) collective-permute-start(bf16[4,32,2,128]{3,2,1,0:T(2,128)(2,1)S(1)} %get-tuple-element.20), channel_id=1, source_target_pairs={{0,4},{4,0},{8,12},{12,8},{16,20},{20,16},{24,28},{28,24},{1,5},{5... | collective-permute-start | bytes 196616 | tf_op jit(solution)/shard_map/ppermute | solution.py:246
  12.1 3.8 %collective-permute-start.4 = (bf16[4,32,2,128]{3,2,1,0:T(2,128)(2,1)S(1)}, bf16[4,32,2,128]{3,2,1,0:T(2,128)(2,1)S(1)}, u32[]{:S(2)}, u32[]{:S(2)}) collective-permute-start(bf16[4,32,2,128]{3,2,1,0:T(2,128)(2,1)S(1)} %bitcast.58), channel_id=1, source_target_pairs={{0,12},{8,20},{16,28},{24,4},{12,0},{20,8},{28,16},{4,24},{1,13},{... | collective-permute-start | bytes 196616 | tf_op jit(solution)/shard_map/ppermute | solution.py:277
  16.5 7.3 %copy-start.1 = (bf16[3,3,3,128,64]{3,4,2,1,0:T(8,128)(2,1)S(1)}, bf16[3,3,3,128,64]{3,4,2,1,0:T(8,128)(2,1)}, u32[]{:S(2)}) copy-start(bf16[3,3,3,128,64]{3,4,2,1,0:T(8,128)(2,1)} %param.6) | copy-start | bytes 1327108
  16.6 8.1 %collective-permute-start.9 = (bf16[4,128,256]{2,1,0:T(8,128)(2,1)S(1)}, bf16[4,128,256]{2,1,0:T(8,128)(2,1)S(1)}, u32[]{:S(2)}, u32[]{:S(2)}) collective-permute-start(bf16[4,128,256]{2,1,0:T(8,128)(2,1)S(1)} %pad_maximum_fusion.cot_ref), channel_id=1, source_target_pairs={{0,4},{4,0},{8,12},{12,8},{16,20},{20,16},{24,28},{28,24},{1,5},{5... | collective-permute-start | bytes 786440 | tf_op jit(solution)/shard_map/ppermute | solution.py:246
  18.1 4.3 %collective-permute-start.15 = (bf16[64,256]{1,0:T(8,128)(2,1)S(1)}, bf16[64,256]{1,0:T(8,128)(2,1)S(1)}, u32[]{:S(2)}, u32[]{:S(2)}) collective-permute-start(bf16[64,256]{1,0:T(8,128)(2,1)S(1)} %first_rest.1.refs_0_), channel_id=1, source_target_pairs={{0,28},{4,24},{8,20},{12,16},{16,12},{20,8},{24,4},{28,0},{1,29},{... | collective-permute-start | bytes 98312 | tf_op jit(solution)/shard_map/ppermute | solution.py:246
  19.6 3.7 %collective-permute-start.13 = (bf16[64,256]{1,0:T(8,128)(2,1)S(1)}, bf16[64,256]{1,0:T(8,128)(2,1)S(1)}, u32[]{:S(2)}, u32[]{:S(2)}) collective-permute-start(bf16[64,256]{1,0:T(8,128)(2,1)S(1)} %first_rest.1.refs_0_), channel_id=1, source_target_pairs={{0,20},{4,16},{8,28},{12,24},{16,4},{20,0},{24,12},{28,8},{1,21},{... | collective-permute-start | bytes 98312 | tf_op jit(solution)/shard_map/ppermute | solution.py:246
  19.8 3.7 %collective-permute-start.11 = (bf16[64,256]{1,0:T(8,128)(2,1)S(1)}, bf16[64,256]{1,0:T(8,128)(2,1)S(1)}, u32[]{:S(2)}, u32[]{:S(2)}) collective-permute-start(bf16[64,256]{1,0:T(8,128)(2,1)S(1)} %first_rest.1.refs_0_), channel_id=1, source_target_pairs={{0,12},{4,8},{8,4},{12,0},{16,28},{20,24},{24,20},{28,16},{1,13},{... | collective-permute-start | bytes 98312 | tf_op jit(solution)/shard_map/ppermute | solution.py:246
  21.0 3.0 %collective-permute-start.10 = (bf16[64,256]{1,0:T(8,128)(2,1)S(1)}, bf16[64,256]{1,0:T(8,128)(2,1)S(1)}, u32[]{:S(2)}, u32[]{:S(2)}) collective-permute-start(bf16[64,256]{1,0:T(8,128)(2,1)S(1)} %first_rest.1.refs_0_), channel_id=1, source_target_pairs={{0,4},{4,0},{8,12},{12,8},{16,20},{20,16},{24,28},{28,24},{1,5},{5... | collective-permute-start | bytes 98312 | tf_op jit(solution)/shard_map/ppermute | solution.py:246
  22.4 1.6 %collective-permute-start.16 = (bf16[64,256]{1,0:T(8,128)(2,1)S(1)}, bf16[64,256]{1,0:T(8,128)(2,1)S(1)}, u32[]{:S(2)}, u32[]{:S(2)}) collective-permute-start(bf16[64,256]{1,0:T(8,128)(2,1)S(1)} %collective-permute-done.15.refs_7_), channel_id=1, source_target_pairs={{0,4},{4,0},{8,12},{12,8},{16,20},{20,16},{24,28},{28,24},{1,5},{5... | collective-permute-start | bytes 98312 | tf_op jit(solution)/shard_map/ppermute | solution.py:246
  23.3 1.2 %collective-permute-start.14 = (bf16[64,256]{1,0:T(8,128)(2,1)S(1)}, bf16[64,256]{1,0:T(8,128)(2,1)S(1)}, u32[]{:S(2)}, u32[]{:S(2)}) collective-permute-start(bf16[64,256]{1,0:T(8,128)(2,1)S(1)} %collective-permute-done.13.refs_5_), channel_id=1, source_target_pairs={{0,4},{4,0},{8,12},{12,8},{16,20},{20,16},{24,28},{28,24},{1,5},{5... | collective-permute-start | bytes 98312 | tf_op jit(solution)/shard_map/ppermute | solution.py:246
  23.4 1.3 %collective-permute-start.12 = (bf16[64,256]{1,0:T(8,128)(2,1)S(1)}, bf16[64,256]{1,0:T(8,128)(2,1)S(1)}, u32[]{:S(2)}, u32[]{:S(2)}) collective-permute-start(bf16[64,256]{1,0:T(8,128)(2,1)S(1)} %collective-permute-done.11.refs_3_), channel_id=1, source_target_pairs={{0,4},{4,0},{8,12},{12,8},{16,20},{20,16},{24,28},{28,24},{1,5},{5... | collective-permute-start | bytes 98312 | tf_op jit(solution)/shard_map/ppermute | solution.py:246

commit v6 on v4

--- a/solution.py
+++ b/solution.py
@@ -214,8 +214,9 @@
         )
         value = lax.dot_general(w_ref[...], rhs, DN, preferred_element_type=jnp.float32)
         sigma = 1.0 / (1.0 + jnp.exp(-value))
-        act[p] = (value * sigma).astype(jnp.bfloat16)
-        grad_pre = cot[p].astype(jnp.float32) * sigma * (1.0 + value * (1.0 - sigma))
+        out = value * sigma
+        act[p] = out.astype(jnp.bfloat16)
+        grad_pre = cot[p].astype(jnp.float32) * (sigma + out * (1.0 - sigma))
         for a in range(3):
             q = p + a - 1
             if 0 <= q < count:

time: 28.3 us -> 28.3 us (level)
  no operation moved by 1% of the time
where the time goes in v6:
time: 28.3 us; the launch traced here: 28.1 us
  starting transfers between devices  16.3 us (58%)
  waiting for transfers between devices  5.34 us (19%)
  Pallas kernels  5.07 us (18%)
  between operations  0.77 us (3%)
  local copies, waits for them, and re-layouts  0.33 us (1%)
  other arithmetic  0.33 us (1%)
    ppermute x12, starting transfers between devices, swap(): return lax.ppermute(array, axis, [(i, i ^ bits) for i in range(peers)])  10.2 us
    ppermute x4, starting transfers between devices, crossed(): return lax.ppermute(array, ('space', 'chan'), pairs)  5.4 us
    pallas_call x1, Pallas kernels, by_gather(): pl.pallas_call(functools.partial(deep_kernel, depth // 2, order), out_sha...  3.42 us
    ppermute x12, waiting for transfers between devices, swap(): return lax.ppermute(array, axis, [(i, i ^ bits) for i in range(peers)])  3.1 us
    ppermute x1, waiting for transfers between devices, by_gather(): lax.ppermute(jnp.where(odd == 1, last, first), 'space', pairs + [(j, i) f...  1.35 us
    pallas_call x1, Pallas kernels, by_gather(): pl.pallas_call(functools.partial(first_part, chans), out_shape=(jax.Shape...  0.97 us
    ppermute x4, waiting for transfers between devices, crossed(): return lax.ppermute(array, ('space', 'chan'), pairs)  0.89 us
    ppermute x1, starting transfers between devices, by_gather(): lax.ppermute(jnp.where(odd == 1, last, first), 'space', pairs + [(j, i) f...  0.69 us
  transfers between devices with their start and end apart: 17, of which 8 were waited for; matrix products, arithmetic and copies ran while one was open for 2% of the time, Pallas kernels for 3%

profile of v6, /device:TPU:0, one launch (start us, length us, event | category | flops | bytes accessed | tf_op | source)
XLA Modules:
  0.0 28.1 jit_solution(9277126778517220302)
XLA Ops:
  0.6 3.5 %collective-permute-start.1 = (bf16[32,2,2,128]{3,2,1,0:T(2,128)(2,1)}, bf16[32,2,2,128]{3,2,1,0:T(2,128)(2,1)S(1)}, u32[]{:S(2)}, u32[]{:S(2)}) collective-permute-start(bf16[32,2,2,128]{3,2,1,0:T(2,128)(2,1)} %param.4), channel_id=1, source_target_pairs={{0,6},{1,7},{2,4},{3,5},{4,2},{5,3},{6,0},{7,1},{8,14},{9,15},{10,... | collective-permute-start | bytes 98312 | tf_op jit(solution)/shard_map/ppermute | solution.py:254
  4.2 1.6 %collective-permute-start = (bf16[32,2,2,128]{3,2,1,0:T(2,128)(2,1)}, bf16[32,2,2,128]{3,2,1,0:T(2,128)(2,1)S(1)}, u32[]{:S(2)}, u32[]{:S(2)}) collective-permute-start(bf16[32,2,2,128]{3,2,1,0:T(2,128)(2,1)} %param.4), channel_id=1, source_target_pairs={{0,7},{1,6},{2,5},{3,4},{4,3},{5,2},{6,1},{7,0},{8,15},{9,14},{10,... | collective-permute-start | bytes 98312 | tf_op jit(solution)/shard_map/ppermute | solution.py:254
  5.8 0.2 collective-permute-start.3
  6.0 0.1 collective-permute-start.2
  6.0 2.6 %collective-permute-start.8 = (bf16[128,256]{1,0:T(8,128)(2,1)}, bf16[128,256]{1,0:T(8,128)(2,1)S(1)}, u32[]{:S(2)}, u32[]{:S(2)}) collective-permute-start(bf16[128,256]{1,0:T(8,128)(2,1)} %bitcast.59), channel_id=1, source_target_pairs={{0,28},{4,24},{8,20},{12,16},{16,12},{20,8},{24,4},{28,0},{1,29},{... | collective-permute-start | bytes 196616 | tf_op jit(solution)/shard_map/ppermute | solution.py:248
  8.6 0.1 collective-permute-start.7
  8.8 0.9 %collective-permute-done.refs_3_ = bf16[32,2,2,128]{3,2,1,0:T(2,128)(2,1)S(1)} collective-permute-done((bf16[32,2,2,128]{3,2,1,0:T(2,128)(2,1)}, bf16[32,2,2,128]{3,2,1,0:T(2,128)(2,1)S(1)}, u32[]{:S(2)}, u32[]{:S(2)}) %collective-permute-start) | collective-permute-done | bytes 32800 | tf_op jit(solution)/shard_map/ppermute | solution.py:254
  9.6 1.9 %collective-permute-start.6 = (bf16[128,256]{1,0:T(8,128)(2,1)S(1)}, bf16[128,256]{1,0:T(8,128)(2,1)S(1)}, u32[]{:S(2)}, u32[]{:S(2)}) collective-permute-start(bf16[128,256]{1,0:T(8,128)(2,1)S(1)} %bitcast.61), channel_id=1, source_target_pairs={{0,12},{4,8},{8,4},{12,0},{16,28},{20,24},{24,20},{28,16},{1,13},{... | collective-permute-start | bytes 196616 | tf_op jit(solution)/shard_map/ppermute | solution.py:248
  11.7 0.0 copy-start
  11.7 0.3 %broadcast_select_fusion = (bf16[4,32,2,128]{3,2,1,0:T(2,128)(2,1)S(1)}, bf16[4,32,2,128]{3,2,1,0:T(2,128)(2,1)S(1)}, bf16[4,32,2,128]{3,2,1,0:T(2,128)(2,1)S(1)}) fusion(pred[]{:T(512)S(6)} %eq.4, bf16[1,32,2,128]{3,2,1,0:T(2,128)(2,1)S(1)} %get-tuple-element.30, bf16[1,32,2,128]{3,2,1,0:T(2,128)(2,1)S(1)} %get-tuple-element.28, ...), kind=kLoop, calls=%fused_computation.1 | loop fusion | flops 229376 | bytes 327681 | tf_op jit(solution)/shard_map/jit(_where)/select_n | solution.py:277
  12.0 0.1 collective-permute-start.5
  12.1 0.7 %collective-permute-start.4 = (bf16[4,32,2,128]{3,2,1,0:T(2,128)(2,1)S(1)}, bf16[4,32,2,128]{3,2,1,0:T(2,128)(2,1)S(1)}, u32[]{:S(2)}, u32[]{:S(2)}) collective-permute-start(bf16[4,32,2,128]{3,2,1,0:T(2,128)(2,1)S(1)} %bitcast.58), channel_id=1, source_target_pairs={{0,12},{8,20},{16,28},{24,4},{12,0},{20,8},{28,16},{4,24},{1,13},{... | collective-permute-start | bytes 196616 | tf_op jit(solution)/shard_map/ppermute | solution.py:279
  12.8 0.3 collective-permute-done.7.refs_5_
  13.0 0.5 %collective-permute-done.6.refs_4_ = bf16[128,256]{1,0:T(8,128)(2,1)S(1)} collective-permute-done((bf16[128,256]{1,0:T(8,128)(2,1)S(1)}, bf16[128,256]{1,0:T(8,128)(2,1)S(1)}, u32[]{:S(2)}, u32[]{:S(2)}) %collective-permute-start.6) | collective-permute-done | bytes 65568 | tf_op jit(solution)/shard_map/ppermute | solution.py:248
  13.5 1.0 %first_part.1 = (f32[64,1024]{1,0:T(8,128)S(1)}, f32[64,512]{1,0:T(8,128)S(1)}) custom-call(bf16[3,288,64]{2,1,0:T(8,128)(2,1)S(1)} %bitcast.50, bf16[4,32,2,128]{3,2,1,0:T(2,128)(2,1)S(1)} %collective-permute-done.5.near_ref, bf16[32,2,2,128]{3,2,1,0:T(2,128)(2,1)S(1)} %collective-permute-done.3.refs_0_, ...), custom_call_target="tpu_custom_call" | custom-call | bytes 5000000 | tf_op jit(solution)/shard_map/first_part/pallas_call | solution.py:296
  14.5 1.3 %collective-permute-done.4.far_ref = bf16[4,32,2,128]{3,2,1,0:T(2,128)(2,1)S(1)} collective-permute-done((bf16[4,32,2,128]{3,2,1,0:T(2,128)(2,1)S(1)}, bf16[4,32,2,128]{3,2,1,0:T(2,128)(2,1)S(1)}, u32[]{:S(2)}, u32[]{:S(2)}) %collective-permute-start.4) | collective-permute-done | bytes 65568 | tf_op jit(solution)/shard_map/ppermute | solution.py:279
  15.8 0.7 %first_rest.1.refs_0_ = bf16[64,256]{1,0:T(8,128)(2,1)S(1)} custom-call(bf16[3,288,64]{2,1,0:T(8,128)(2,1)S(1)} %bitcast.51, bf16[4,32,2,128]{3,2,1,0:T(2,128)(2,1)S(1)} %collective-permute-done.4.far_ref, f32[64,1024]{1,0:T(8,128)S(1)} %get-tuple-element.11.part_ref, f32[64,512]{1,0:T(8,128)S(1)} %get-tuple-element.12.sums_ref), custom_call_target="tpu_custom_call" | custom-call | bytes 4000000 | tf_op jit(solution)/shard_map/first_rest/pallas_call | solution.py:310
  16.5 0.0 copy-start.1
  16.6 1.5 %collective-permute-start.9 = (bf16[4,128,256]{2,1,0:T(8,128)(2,1)S(1)}, bf16[4,128,256]{2,1,0:T(8,128)(2,1)S(1)}, u32[]{:S(2)}, u32[]{:S(2)}) collective-permute-start(bf16[4,128,256]{2,1,0:T(8,128)(2,1)S(1)} %pad_maximum_fusion.cot_ref), channel_id=1, source_target_pairs={{0,4},{4,0},{8,12},{12,8},{16,20},{20,16},{24,28},{28,24},{1,5},{5... | collective-permute-start | bytes 786440 | tf_op jit(solution)/shard_map/ppermute | solution.py:248
  18.1 1.5 %collective-permute-start.15 = (bf16[64,256]{1,0:T(8,128)(2,1)S(1)}, bf16[64,256]{1,0:T(8,128)(2,1)S(1)}, u32[]{:S(2)}, u32[]{:S(2)}) collective-permute-start(bf16[64,256]{1,0:T(8,128)(2,1)S(1)} %first_rest.1.refs_0_), channel_id=1, source_target_pairs={{0,28},{4,24},{8,20},{12,16},{16,12},{20,8},{24,4},{28,0},{1,29},{... | collective-permute-start | bytes 98312 | tf_op jit(solution)/shard_map/ppermute | solution.py:248
  19.6 0.2 collective-permute-start.13
  19.8 1.2 %collective-permute-start.11 = (bf16[64,256]{1,0:T(8,128)(2,1)S(1)}, bf16[64,256]{1,0:T(8,128)(2,1)S(1)}, u32[]{:S(2)}, u32[]{:S(2)}) collective-permute-start(bf16[64,256]{1,0:T(8,128)(2,1)S(1)} %first_rest.1.refs_0_), channel_id=1, source_target_pairs={{0,12},{4,8},{8,4},{12,0},{16,28},{20,24},{24,20},{28,16},{1,13},{... | collective-permute-start | bytes 98312 | tf_op jit(solution)/shard_map/ppermute | solution.py:248
  21.0 0.4 %collective-permute-start.10 = (bf16[64,256]{1,0:T(8,128)(2,1)S(1)}, bf16[64,256]{1,0:T(8,128)(2,1)S(1)}, u32[]{:S(2)}, u32[]{:S(2)}) collective-permute-start(bf16[64,256]{1,0:T(8,128)(2,1)S(1)} %first_rest.1.refs_0_), channel_id=1, source_target_pairs={{0,4},{4,0},{8,12},{12,8},{16,20},{20,16},{24,28},{28,24},{1,5},{5... | collective-permute-start | bytes 98312 | tf_op jit(solution)/shard_map/ppermute | solution.py:248
  21.4 1.0 %collective-permute-done.15.refs_7_ = bf16[64,256]{1,0:T(8,128)(2,1)S(1)} collective-permute-done((bf16[64,256]{1,0:T(8,128)(2,1)S(1)}, bf16[64,256]{1,0:T(8,128)(2,1)S(1)}, u32[]{:S(2)}, u32[]{:S(2)}) %collective-permute-start.15) | collective-permute-done | bytes 32800 | tf_op jit(solution)/shard_map/ppermute | solution.py:248
  22.4 0.1 collective-permute-start.16
  22.6 0.8 %collective-permute-done.13.refs_5_ = bf16[64,256]{1,0:T(8,128)(2,1)S(1)} collective-permute-done((bf16[64,256]{1,0:T(8,128)(2,1)S(1)}, bf16[64,256]{1,0:T(8,128)(2,1)S(1)}, u32[]{:S(2)}, u32[]{:S(2)}) %collective-permute-start.13) | collective-permute-done | bytes 32800 | tf_op jit(solution)/shard_map/ppermute | solution.py:248
  23.3 0.1 collective-permute-start.14
  23.4 0.4 %collective-permute-start.12 = (bf16[64,256]{1,0:T(8,128)(2,1)S(1)}, bf16[64,256]{1,0:T(8,128)(2,1)S(1)}, u32[]{:S(2)}, u32[]{:S(2)}) collective-permute-start(bf16[64,256]{1,0:T(8,128)(2,1)S(1)} %collective-permute-done.11.refs_3_), channel_id=1, source_target_pairs={{0,4},{4,0},{8,12},{12,8},{16,20},{20,16},{24,28},{28,24},{1,5},{5... | collective-permute-start | bytes 98312 | tf_op jit(solution)/shard_map/ppermute | solution.py:248
  23.8 0.2 copy.23.w_ref
  24.1 0.5 %collective-permute-done.14.refs_4_ = bf16[64,256]{1,0:T(8,128)(2,1)S(1)} collective-permute-done((bf16[64,256]{1,0:T(8,128)(2,1)S(1)}, bf16[64,256]{1,0:T(8,128)(2,1)S(1)}, u32[]{:S(2)}, u32[]{:S(2)}) %collective-permute-start.14) | collective-permute-done | bytes 32800 | tf_op jit(solution)/shard_map/ppermute | solution.py:248
  24.5 0.2 collective-permute-done.12.refs_2_
  24.7 3.4 %deep.1 = (bf16[128,256]{1,0:T(8,128)(2,1)}, f32[1728,128]{1,0:T(8,128)}) custom-call(bf16[128,1728]{1,0:T(8,128)(2,1)S(1)} %copy.23.w_ref, bf16[4,128,256]{2,1,0:T(8,128)(2,1)S(1)} %pad_maximum_fusion.cot_ref, bf16[4,128,256]{2,1,0:T(8,128)(2,1)S(1)} %collective-permute-done.9.cot_swapped_ref, bf16[64,256]{1,0:T(8,128)(2,1)S(1)} %first_rest.1.refs_0_, ...), custom_call_target="tpu_custom_call" | custom-call | bytes 12000000 | tf_op jit(solution)/shard_map/deep/pallas_call | solution.py:329
  (19 shorter events, 0.2 us)
Async XLA Ops:
  0.6 9.0 %copy-start.2 = (bf16[128,1,256]{2,0,1:T(8,128)(2,1)S(1)}, bf16[128,1,256]{2,0,1:T(8,128)(2,1)}, u32[]{:S(2)}) copy-start(bf16[128,1,256]{2,0,1:T(8,128)(2,1)} %param.7) | copy-start | bytes 196612
  0.6 8.0 %collective-permute-start.1 = (bf16[32,2,2,128]{3,2,1,0:T(2,128)(2,1)}, bf16[32,2,2,128]{3,2,1,0:T(2,128)(2,1)S(1)}, u32[]{:S(2)}, u32[]{:S(2)}) collective-permute-start(bf16[32,2,2,128]{3,2,1,0:T(2,128)(2,1)} %param.4), channel_id=1, source_target_pairs={{0,6},{1,7},{2,4},{3,5},{4,2},{5,3},{6,0},{7,1},{8,14},{9,15},{10,... | collective-permute-start | bytes 98312 | tf_op jit(solution)/shard_map/ppermute | solution.py:254
  4.2 5.5 %collective-permute-start = (bf16[32,2,2,128]{3,2,1,0:T(2,128)(2,1)}, bf16[32,2,2,128]{3,2,1,0:T(2,128)(2,1)S(1)}, u32[]{:S(2)}, u32[]{:S(2)}) collective-permute-start(bf16[32,2,2,128]{3,2,1,0:T(2,128)(2,1)} %param.4), channel_id=1, source_target_pairs={{0,7},{1,6},{2,5},{3,4},{4,3},{5,2},{6,1},{7,0},{8,15},{9,14},{10,... | collective-permute-start | bytes 98312 | tf_op jit(solution)/shard_map/ppermute | solution.py:254
  5.8 5.8 %collective-permute-start.3 = (bf16[32,2,2,128]{3,2,1,0:T(2,128)(2,1)}, bf16[32,2,2,128]{3,2,1,0:T(2,128)(2,1)S(1)}, u32[]{:S(2)}, u32[]{:S(2)}) collective-permute-start(bf16[32,2,2,128]{3,2,1,0:T(2,128)(2,1)} %param.4), channel_id=1, source_target_pairs={{0,4},{1,5},{2,6},{3,7},{4,0},{5,1},{6,2},{7,3},{8,12},{9,13},{10,... | collective-permute-start | bytes 98312 | tf_op jit(solution)/shard_map/ppermute | solution.py:254
  6.0 5.7 %collective-permute-start.2 = (bf16[32,2,2,128]{3,2,1,0:T(2,128)(2,1)}, bf16[32,2,2,128]{3,2,1,0:T(2,128)(2,1)S(1)}, u32[]{:S(2)}, u32[]{:S(2)}) collective-permute-start(bf16[32,2,2,128]{3,2,1,0:T(2,128)(2,1)} %param.4), channel_id=1, source_target_pairs={{0,5},{1,4},{2,7},{3,6},{4,1},{5,0},{6,3},{7,2},{8,13},{9,12},{10,... | collective-permute-start | bytes 98312 | tf_op jit(solution)/shard_map/ppermute | solution.py:254
  6.0 6.7 %collective-permute-start.8 = (bf16[128,256]{1,0:T(8,128)(2,1)}, bf16[128,256]{1,0:T(8,128)(2,1)S(1)}, u32[]{:S(2)}, u32[]{:S(2)}) collective-permute-start(bf16[128,256]{1,0:T(8,128)(2,1)} %bitcast.59), channel_id=1, source_target_pairs={{0,28},{4,24},{8,20},{12,16},{16,12},{20,8},{24,4},{28,0},{1,29},{... | collective-permute-start | bytes 196616 | tf_op jit(solution)/shard_map/ppermute | solution.py:248
  8.6 4.4 %collective-permute-start.7 = (bf16[128,256]{1,0:T(8,128)(2,1)}, bf16[128,256]{1,0:T(8,128)(2,1)S(1)}, u32[]{:S(2)}, u32[]{:S(2)}) collective-permute-start(bf16[128,256]{1,0:T(8,128)(2,1)} %bitcast.60), channel_id=1, source_target_pairs={{0,20},{4,16},{8,28},{12,24},{16,4},{20,0},{24,12},{28,8},{1,21},{... | collective-permute-start | bytes 196616 | tf_op jit(solution)/shard_map/ppermute | solution.py:248
  9.6 3.9 %collective-permute-start.6 = (bf16[128,256]{1,0:T(8,128)(2,1)S(1)}, bf16[128,256]{1,0:T(8,128)(2,1)S(1)}, u32[]{:S(2)}, u32[]{:S(2)}) collective-permute-start(bf16[128,256]{1,0:T(8,128)(2,1)S(1)} %bitcast.61), channel_id=1, source_target_pairs={{0,12},{4,8},{8,4},{12,0},{16,28},{20,24},{24,20},{28,16},{1,13},{... | collective-permute-start | bytes 196616 | tf_op jit(solution)/shard_map/ppermute | solution.py:248
  11.7 1.8 %copy-start = (bf16[3,3,3,64,32]{3,4,2,1,0:T(8,128)(2,1)S(1)}, bf16[3,3,3,64,32]{3,4,2,1,0:T(8,128)(2,1)}, u32[]{:S(2)}) copy-start(bf16[3,3,3,64,32]{3,4,2,1,0:T(8,128)(2,1)} %param.5) | copy-start | bytes 331780
  12.0 1.5 %collective-permute-start.5 = (bf16[4,32,2,128]{3,2,1,0:T(2,128)(2,1)S(1)}, bf16[4,32,2,128]{3,2,1,0:T(2,128)(2,1)S(1)}, u32[]{:S(2)}, u32[]{:S(2)}) collective-permute-start(bf16[4,32,2,128]{3,2,1,0:T(2,128)(2,1)S(1)} %get-tuple-element.20), channel_id=1, source_target_pairs={{0,4},{4,0},{8,12},{12,8},{16,20},{20,16},{24,28},{28,24},{1,5},{5... | collective-permute-start | bytes 196616 | tf_op jit(solution)/shard_map/ppermute | solution.py:248
  12.1 3.8 %collective-permute-start.4 = (bf16[4,32,2,128]{3,2,1,0:T(2,128)(2,1)S(1)}, bf16[4,32,2,128]{3,2,1,0:T(2,128)(2,1)S(1)}, u32[]{:S(2)}, u32[]{:S(2)}) collective-permute-start(bf16[4,32,2,128]{3,2,1,0:T(2,128)(2,1)S(1)} %bitcast.58), channel_id=1, source_target_pairs={{0,12},{8,20},{16,28},{24,4},{12,0},{20,8},{28,16},{4,24},{1,13},{... | collective-permute-start | bytes 196616 | tf_op jit(solution)/shard_map/ppermute | solution.py:279
  16.5 7.3 %copy-start.1 = (bf16[3,3,3,128,64]{3,4,2,1,0:T(8,128)(2,1)S(1)}, bf16[3,3,3,128,64]{3,4,2,1,0:T(8,128)(2,1)}, u32[]{:S(2)}) copy-start(bf16[3,3,3,128,64]{3,4,2,1,0:T(8,128)(2,1)} %param.6) | copy-start | bytes 1327108
  16.6 8.1 %collective-permute-start.9 = (bf16[4,128,256]{2,1,0:T(8,128)(2,1)S(1)}, bf16[4,128,256]{2,1,0:T(8,128)(2,1)S(1)}, u32[]{:S(2)}, u32[]{:S(2)}) collective-permute-start(bf16[4,128,256]{2,1,0:T(8,128)(2,1)S(1)} %pad_maximum_fusion.cot_ref), channel_id=1, source_target_pairs={{0,4},{4,0},{8,12},{12,8},{16,20},{20,16},{24,28},{28,24},{1,5},{5... | collective-permute-start | bytes 786440 | tf_op jit(solution)/shard_map/ppermute | solution.py:248
  18.1 4.3 %collective-permute-start.15 = (bf16[64,256]{1,0:T(8,128)(2,1)S(1)}, bf16[64,256]{1,0:T(8,128)(2,1)S(1)}, u32[]{:S(2)}, u32[]{:S(2)}) collective-permute-start(bf16[64,256]{1,0:T(8,128)(2,1)S(1)} %first_rest.1.refs_0_), channel_id=1, source_target_pairs={{0,28},{4,24},{8,20},{12,16},{16,12},{20,8},{24,4},{28,0},{1,29},{... | collective-permute-start | bytes 98312 | tf_op jit(solution)/shard_map/ppermute | solution.py:248
  19.6 3.7 %collective-permute-start.13 = (bf16[64,256]{1,0:T(8,128)(2,1)S(1)}, bf16[64,256]{1,0:T(8,128)(2,1)S(1)}, u32[]{:S(2)}, u32[]{:S(2)}) collective-permute-start(bf16[64,256]{1,0:T(8,128)(2,1)S(1)} %first_rest.1.refs_0_), channel_id=1, source_target_pairs={{0,20},{4,16},{8,28},{12,24},{16,4},{20,0},{24,12},{28,8},{1,21},{... | collective-permute-start | bytes 98312 | tf_op jit(solution)/shard_map/ppermute | solution.py:248
  19.8 3.7 %collective-permute-start.11 = (bf16[64,256]{1,0:T(8,128)(2,1)S(1)}, bf16[64,256]{1,0:T(8,128)(2,1)S(1)}, u32[]{:S(2)}, u32[]{:S(2)}) collective-permute-start(bf16[64,256]{1,0:T(8,128)(2,1)S(1)} %first_rest.1.refs_0_), channel_id=1, source_target_pairs={{0,12},{4,8},{8,4},{12,0},{16,28},{20,24},{24,20},{28,16},{1,13},{... | collective-permute-start | bytes 98312 | tf_op jit(solution)/shard_map/ppermute | solution.py:248
  21.0 3.0 %collective-permute-start.10 = (bf16[64,256]{1,0:T(8,128)(2,1)S(1)}, bf16[64,256]{1,0:T(8,128)(2,1)S(1)}, u32[]{:S(2)}, u32[]{:S(2)}) collective-permute-start(bf16[64,256]{1,0:T(8,128)(2,1)S(1)} %first_rest.1.refs_0_), channel_id=1, source_target_pairs={{0,4},{4,0},{8,12},{12,8},{16,20},{20,16},{24,28},{28,24},{1,5},{5... | collective-permute-start | bytes 98312 | tf_op jit(solution)/shard_map/ppermute | solution.py:248
  22.4 1.6 %collective-permute-start.16 = (bf16[64,256]{1,0:T(8,128)(2,1)S(1)}, bf16[64,256]{1,0:T(8,128)(2,1)S(1)}, u32[]{:S(2)}, u32[]{:S(2)}) collective-permute-start(bf16[64,256]{1,0:T(8,128)(2,1)S(1)} %collective-permute-done.15.refs_7_), channel_id=1, source_target_pairs={{0,4},{4,0},{8,12},{12,8},{16,20},{20,16},{24,28},{28,24},{1,5},{5... | collective-permute-start | bytes 98312 | tf_op jit(solution)/shard_map/ppermute | solution.py:248
  23.3 1.2 %collective-permute-start.14 = (bf16[64,256]{1,0:T(8,128)(2,1)S(1)}, bf16[64,256]{1,0:T(8,128)(2,1)S(1)}, u32[]{:S(2)}, u32[]{:S(2)}) collective-permute-start(bf16[64,256]{1,0:T(8,128)(2,1)S(1)} %collective-permute-done.13.refs_5_), channel_id=1, source_target_pairs={{0,4},{4,0},{8,12},{12,8},{16,20},{20,16},{24,28},{28,24},{1,5},{5... | collective-permute-start | bytes 98312 | tf_op jit(solution)/shard_map/ppermute | solution.py:248
  23.4 1.3 %collective-permute-start.12 = (bf16[64,256]{1,0:T(8,128)(2,1)S(1)}, bf16[64,256]{1,0:T(8,128)(2,1)S(1)}, u32[]{:S(2)}, u32[]{:S(2)}) collective-permute-start(bf16[64,256]{1,0:T(8,128)(2,1)S(1)} %collective-permute-done.11.refs_3_), channel_id=1, source_target_pairs={{0,4},{4,0},{8,12},{12,8},{16,20},{20,16},{24,28},{28,24},{1,5},{5... | collective-permute-start | bytes 98312 | tf_op jit(solution)/shard_map/ppermute | solution.py:248
